TPU v7x, 32 devices: a whole 2x2x4 slice. The times are simulated.
32 devices in a mesh: members: 2 (over y), tiles: 4 (over z), rows: 2 (over x), lev: 2 (over core).
Axes of the slice: x: 2, y: 2, z: 4, core: 2. Of those that a mesh axis runs over, the one named last changes fastest.
Arguments:
- air_state: float32 [64, 48, 1536], P(('members', 'lev'), 'rows', 'tiles'), parts along dimension 0, may hold values from -6 to 6
- wind_east: float32 [64, 48, 1536], P(('members', 'lev'), 'rows', 'tiles'), parts along dimension 0, may hold values from -0.4 to 0.4
- wind_north: float32 [64, 48, 1536], P(('members', 'lev'), 'rows', 'tiles'), parts along dimension 0, may hold values from -0.4 to 0.4
- feedback_weight: float32 [32], P('lev'), may hold values from 0.2 to 1
- nest_west: int32 [4], P('members'), parts along dimension 0, may hold values from 1 to 1023
- nest_south: int32 [4], P('members'), parts along dimension 0, may hold values from 1 to 31
Outputs:
- new_state: float32 [64, 48, 1536], P(('members', 'lev'), 'rows', 'tiles'), parts along dimension 0
There are 2 independent parts, one for each index of `members`. A program takes and returns all parts, laid end to end along the dimension named above; an argument that names none is the same for every part. Nothing has to cross between parts.
Inputs may be any that keep to these rules, and one draw needn't show every extreme that they name: `nest_west`: the nest's footprint with one cell of margin lies inside the parent grid in both substeps.
All inputs are finite; a program needn't handle non-finite values.
Results may differ from a plain program's by a relative error of at most 0.000086.
Values sent between devices are 32-bit elements; how exact they have to be, the bound alone decides.
No kernel may reach another device: no remote copies, remote signals or barrier semaphores. Data moves between devices by JAX's collectives and lax.ppermute only.
A program may use at most 64 MiB of HBM per device.

v0:
```python
import jax
import jax.numpy as jnp
from jax import lax
from jax.sharding import PartitionSpec as P

VERTICAL_MIX = 0.1
PARENT_MIXING = 0.04
NEST_MIXING = 0.18
NEST_ADVECT = 1.5
NUDGING = 0.2


def padded_2(array, sides, width):
    for axis, dim in sides:
        size, length = (lax.axis_size(axis), array.shape[dim])
        up = [(i, (i + 1) % size) for i in range(size - 1)]
        down = [(j, i) for i, j in up]
        last = lax.slice_in_dim(array, length - width, length, axis=dim)
        first = lax.slice_in_dim(array, 0, width, axis=dim)
        before = lax.ppermute(last, axis, up)
        after = lax.ppermute(first, axis, down)
        array = jnp.concatenate([before, array, after], axis=dim)
    return array


def interp_table(cells):
    extended = jnp.arange(cells + 2, dtype=jnp.int32) - 1
    coarse = jnp.floor_divide(extended, 3)
    offset = extended - 3 * coarse
    fraction = jnp.abs(offset - 1).astype(jnp.float32) / 3.0
    nearest = coarse + 1
    beside = nearest + (offset - 1)
    slots = jnp.arange(cells // 3 + 2, dtype=jnp.int32)[:, None]
    first_part = jnp.where(
        slots == nearest[None, :], 1.0 - fraction[None, :], jnp.zeros((), jnp.float32)
    )
    second_part = jnp.where(slots == beside[None, :], fraction[None, :], jnp.zeros((), jnp.float32))
    return first_part + second_part


def tendency(padded, speed_east, speed_north, advect_scale, mixing_scale):
    centre = padded[1:-1, 1:-1, 1:-1]
    eastern = padded[1:-1, 1:-1, 2:]
    western = padded[1:-1, 1:-1, :-2]
    southern = padded[1:-1, 2:, 1:-1]
    northern = padded[1:-1, :-2, 1:-1]
    upper = padded[2:, 1:-1, 1:-1]
    lower = padded[:-2, 1:-1, 1:-1]
    advect = speed_east * (eastern - western) + speed_north * (southern - northern)
    horizontal = eastern + western + southern + northern - 4.0 * centre
    vertical = upper + lower - 2.0 * centre
    return -0.5 * advect_scale * advect + mixing_scale * horizontal + VERTICAL_MIX * vertical


def padded_block(block_field):
    return padded_2(block_field, (("tiles", 2), ("rows", 1), ("lev", 0)), 1)


def per_device(air_state, wind_east, wind_north, feedback_weight, nest_west, nest_south):
    levels, height, breadth = air_state.shape
    tile_count = lax.axis_size("tiles")
    row_count = lax.axis_size("rows")
    tile_index = lax.axis_index("tiles")
    row_index = lax.axis_index("rows")
    parent_tiles = 3 * tile_count // 4
    nest_tiles = tile_count - parent_tiles
    in_nest = tile_index >= parent_tiles
    nest_tile = tile_index - parent_tiles
    cross_x = breadth // 3 + 2
    cross_y = height // 3 + 2
    third_x = breadth // 3
    third_y = height // 3
    first_x = tile_index * breadth
    first_y = row_index * height
    columns = jnp.arange(breadth, dtype=jnp.int32)
    lines = jnp.arange(height, dtype=jnp.int32)
    targets_x = jnp.arange(tile_count, dtype=jnp.int32)
    targets_y = jnp.arange(row_count, dtype=jnp.int32)
    highest = lax.Precision.HIGHEST
    table_x = interp_table(breadth)
    table_y = interp_table(height)
    zero_value = jnp.zeros((), jnp.float32)

    def boundary(source, substep):
        anchor_x = nest_west[substep] + (targets_x - parent_tiles) * third_x - 1
        slot_x = jnp.arange(cross_x, dtype=jnp.int32)
        pick_x = (
            (first_x + columns)[None, :, None] == anchor_x[:, None, None] + slot_x[None, None, :]
        ) & (targets_x >= parent_tiles)[:, None, None]
        pick_x = pick_x.astype(jnp.float32)
        anchor_y = nest_south[substep] + targets_y * third_y - 1
        slot_y = jnp.arange(cross_y, dtype=jnp.int32)
        pick_y = (
            (first_y + lines)[None, :, None] == anchor_y[:, None, None] + slot_y[None, None, :]
        ).astype(jnp.float32)
        pieces = jnp.einsum("lyi,tij->tlyj", source, pick_x, precision=highest)
        merged = lax.all_to_all(pieces, "tiles", split_axis=0, concat_axis=0, tiled=True).sum(
            axis=0
        )
        pieces = jnp.einsum("lyj,ryw->rlwj", merged, pick_y, precision=highest)
        window = lax.all_to_all(pieces, "rows", split_axis=0, concat_axis=0, tiled=True).sum(axis=0)
        along = jnp.einsum("lwj,je->lwe", window, table_x, precision=highest)
        return jnp.einsum("lwe,wf->lfe", along, table_y, precision=highest)

    def assemble(block_field, fine):
        padded = padded_block(block_field)
        fine_padded = jnp.pad(fine, ((1, 1), (0, 0), (0, 0)))
        column_place = lax.broadcasted_iota(jnp.int32, padded.shape, 2)
        line_place = lax.broadcasted_iota(jnp.int32, padded.shape, 1)
        outside = (column_place == 0) & (nest_tile == 0) | (column_place == breadth + 1) & (
            nest_tile == nest_tiles - 1
        )
        outside = (
            outside
            | (line_place == 0) & (row_index == 0)
            | (line_place == height + 1) & (row_index == row_count - 1)
        )
        padded = jnp.where(outside & in_nest, fine_padded, padded)
        seam_cells = (column_place == breadth + 1) & (tile_index == parent_tiles - 1)
        return jnp.where(seam_cells, zero_value, padded)

    advect_scale = jnp.where(in_nest, jnp.float32(NEST_ADVECT), jnp.float32(1.0))
    mixing_scale = jnp.where(in_nest, jnp.float32(NEST_MIXING), jnp.float32(PARENT_MIXING))
    fine_first = boundary(air_state, 0)
    change = tendency(
        assemble(air_state, fine_first), wind_east, wind_north, advect_scale, mixing_scale
    )
    nudging_term = jnp.where(in_nest, NUDGING * (fine_first[:, 1:-1, 1:-1] - air_state), zero_value)
    step_one = air_state + change + nudging_term
    fine_second = boundary(step_one, 1)
    change = tendency(
        assemble(step_one, fine_second), wind_east, wind_north, advect_scale, mixing_scale
    )
    nested_two = step_one + change + NUDGING * (fine_second[:, 1:-1, 1:-1] - step_one)
    step_two = jnp.where(in_nest, nested_two, step_one)
    coarse = step_two.reshape(levels, third_y, 3, third_x, 3).mean(axis=(2, 4))
    avg_columns = jnp.arange(third_x, dtype=jnp.int32)
    avg_lines = jnp.arange(third_y, dtype=jnp.int32)
    west_last = nest_west[1]
    south_last = nest_south[1]
    place_x = (
        (west_last + (targets_x - parent_tiles) * third_x)[:, None, None]
        + avg_columns[None, :, None]
        == (first_x + columns)[None, None, :]
    ) & (targets_x >= parent_tiles)[:, None, None]
    place_x = place_x.astype(jnp.float32)
    place_y = (
        (south_last + targets_y * third_y)[:, None, None] + avg_lines[None, :, None]
        == (first_y + lines)[None, None, :]
    ).astype(jnp.float32)
    parent_y = south_last + row_index * third_y + avg_lines
    send_y = (jnp.floor_divide(parent_y, height)[None, :] == targets_y[:, None]) & in_nest
    pieces = jnp.where(send_y[:, None, :, None], coarse[None], zero_value)
    received = lax.all_to_all(pieces, "rows", split_axis=0, concat_axis=0, tiled=True)
    spread = jnp.einsum("slba,sby->lya", received, place_y, precision=highest)
    parent_x = west_last + nest_tile * third_x + avg_columns
    send_x = jnp.floor_divide(parent_x, breadth)[None, :] == targets_x[:, None]
    pieces = jnp.where(send_x[:, None, None, :], spread[None], zero_value)
    received = lax.all_to_all(pieces, "tiles", split_axis=0, concat_axis=0, tiled=True)
    placed = jnp.einsum("slya,sai->lyi", received, place_x, precision=highest)
    global_x = (first_x + columns)[None, None, :]
    global_y = (first_y + lines)[None, :, None]
    covered = (global_x >= west_last) & (global_x < west_last + nest_tiles * third_x)
    covered = covered & (global_y >= south_last) & (global_y < south_last + row_count * third_y)
    covered = covered & jnp.logical_not(in_nest)
    blended = step_two + feedback_weight[:, None, None] * (placed - step_two)
    return jnp.where(covered, blended, step_two)


def solution(mesh):
    in_specs = (
        P(("members", "lev"), "rows", "tiles"),
        P(("members", "lev"), "rows", "tiles"),
        P(("members", "lev"), "rows", "tiles"),
        P("lev"),
        P("members"),
        P("members"),
    )
    out_specs = P(("members", "lev"), "rows", "tiles")
    return jax.shard_map(
        per_device, mesh=mesh, in_specs=in_specs, out_specs=out_specs, check_vma=False
    )
```

profile of v0, /device:TPU:0, one launch (start us, length us, event | category | flops | bytes accessed | tf_op | source)
XLA Modules:
  0.0 189.7 jit_solution(18388391640201218736)
XLA Ops:
  2.1 3.8 %convolution_bitcast_fusion.1 = f32[4,16,24,130]{3,2,1,0:T(8,128)} fusion(f32[16,24,384]{2,1,0:T(8,128)} %param.6, s32[4,130]{1,0:T(4,128)S(1)} %iota_add_fusion.1, s32[384]{0:T(512)S(1)} %iota_add_fusion.4, pred[4]{0:T(512)(128)(4,1)S(1)} %iota_compare_fusion.15), kind=kOutput, calls=%fused_computation.1 | convolution fusion | flops 920524800 | bytes 1392164 | tf_op jit(solution)/shard_map/lyi,tij->tlyj/dot_general | solution.py:96
  5.9 6.5 %all-to-all-start = ((f32[4,16,24,130]{3,2,1,0:T(8,128)}), f32[4,16,24,130]{3,2,1,0:T(8,128)S(1)}, u32[]{:S(2)}, u32[]{:S(2)}) async-start(f32[4,16,24,130]{3,2,1,0:T(8,128)} %convolution_bitcast_fusion.1), calls=%async_computation | async-start | bytes 3145728 | tf_op jit(solution)/shard_map/all_to_all | solution.py:97
  12.5 3.9 %collective-permute-start = (f32[16,24,1]{2,1,0:T(8,128)S(1)}, f32[16,24,1]{2,1,0:T(8,128)S(1)}, u32[]{:S(2)}, u32[]{:S(2)}) collective-permute-start(f32[16,24,1]{2,1,0:T(8,128)S(1)} %get-tuple-element.15), channel_id=1, source_target_pairs={{0,4},{4,8},{8,12},{1,5},{5,9},{9,13},{2,6},{6,10},{10,14},{3,7},{... | collective-permute-start | bytes 4616 | tf_op jit(solution)/shard_map/ppermute | solution.py:20
  22.6 19.5 %collective-permute-done = f32[16,24,1]{2,1,0:T(8,128)S(1)} collective-permute-done((f32[16,24,1]{2,1,0:T(8,128)S(1)}, f32[16,24,1]{2,1,0:T(8,128)S(1)}, u32[]{:S(2)}, u32[]{:S(2)}) %collective-permute-start) | collective-permute-done | bytes 1568 | tf_op jit(solution)/shard_map/ppermute | solution.py:20
  42.3 3.4 %collective-permute-start.2 = (f32[16,1,386]{2,1,0:T(1,128)S(1)}, f32[16,1,386]{2,1,0:T(1,128)S(1)}, u32[]{:S(2)}, u32[]{:S(2)}) collective-permute-start(f32[16,1,386]{2,1,0:T(1,128)S(1)} %get-tuple-element.11), channel_id=1, source_target_pairs={{0,2},{1,3},{4,6},{5,7},{8,10},{9,11},{12,14},{13,15},{16,18},{17,... | collective-permute-start | bytes 74120 | tf_op jit(solution)/shard_map/ppermute | solution.py:20
  47.0 3.4 %all-to-all-done = f32[4,16,24,130]{3,2,1,0:T(8,128)S(1)} async-done(((f32[4,16,24,130]{3,2,1,0:T(8,128)}), f32[4,16,24,130]{3,2,1,0:T(8,128)S(1)}, u32[]{:S(2)}, u32[]{:S(2)}) %all-to-all-start) | async-done | bytes 798752 | tf_op jit(solution)/shard_map/all_to_all | solution.py:97
  51.8 3.5 %all-to-all-start.1 = ((f32[2,16,10,130]{3,1,2,0:T(8,128)}), f32[2,16,10,130]{3,1,2,0:T(8,128)S(1)}, u32[]{:S(2)}, u32[]{:S(2)}) async-start(f32[2,16,10,130]{3,1,2,0:T(8,128)} %copy.23), calls=%async_computation.1 | async-start | bytes 655360 | tf_op jit(solution)/shard_map/all_to_all | solution.py:101
  58.0 2.8 %all-to-all-done.1 = f32[2,16,10,130]{3,1,2,0:T(8,128)S(1)} async-done(((f32[2,16,10,130]{3,1,2,0:T(8,128)}), f32[2,16,10,130]{3,1,2,0:T(8,128)S(1)}, u32[]{:S(2)}, u32[]{:S(2)}) %all-to-all-start.1) | async-done | bytes 166432 | tf_op jit(solution)/shard_map/all_to_all | solution.py:101
  65.0 2.7 %convolution_bitcast_fusion = f32[4,16,24,130]{3,2,1,0:T(8,128)} fusion(f32[16,24,384]{2,1,0:T(8,128)S(1)} %fusion.24, s32[4,130]{1,0:T(4,128)S(1)} %iota_add_fusion, s32[384]{0:T(512)S(1)} %iota_add_fusion.4, pred[4]{0:T(512)(128)(4,1)S(1)} %iota_compare_fusion.15), kind=kOutput, calls=%fused_computation | convolution fusion | flops 920524800 | bytes 1392164 | tf_op jit(solution)/shard_map/lyi,tij->tlyj/dot_general | solution.py:96
  67.7 10.6 %all-to-all-start.2 = ((f32[4,16,24,130]{3,2,1,0:T(8,128)}), f32[4,16,24,130]{3,2,1,0:T(8,128)S(1)}, u32[]{:S(2)}, u32[]{:S(2)}) async-start(f32[4,16,24,130]{3,2,1,0:T(8,128)} %convolution_bitcast_fusion), calls=%async_computation.2 | async-start | bytes 3145728 | tf_op jit(solution)/shard_map/all_to_all | solution.py:97
  78.6 4.2 %collective-permute-start.6 = (f32[16,24,1]{2,1,0:T(8,128)S(1)}, f32[16,24,1]{2,1,0:T(8,128)S(1)}, u32[]{:S(2)}, u32[]{:S(2)}) collective-permute-start(f32[16,24,1]{2,1,0:T(8,128)S(1)} %get-tuple-element.13), channel_id=1, source_target_pairs={{0,4},{4,8},{8,12},{1,5},{5,9},{9,13},{2,6},{6,10},{10,14},{3,7},{... | collective-permute-start | bytes 4616 | tf_op jit(solution)/shard_map/ppermute | solution.py:20
  84.1 22.2 %collective-permute-done.6 = f32[16,24,1]{2,1,0:T(8,128)S(1)} collective-permute-done((f32[16,24,1]{2,1,0:T(8,128)S(1)}, f32[16,24,1]{2,1,0:T(8,128)S(1)}, u32[]{:S(2)}, u32[]{:S(2)}) %collective-permute-start.6) | collective-permute-done | bytes 1568 | tf_op jit(solution)/shard_map/ppermute | solution.py:20
  106.6 4.1 %collective-permute-start.8 = (f32[16,1,386]{2,1,0:T(1,128)S(1)}, f32[16,1,386]{2,1,0:T(1,128)S(1)}, u32[]{:S(2)}, u32[]{:S(2)}) collective-permute-start(f32[16,1,386]{2,1,0:T(1,128)S(1)} %get-tuple-element.9), channel_id=1, source_target_pairs={{0,2},{1,3},{4,6},{5,7},{8,10},{9,11},{12,14},{13,15},{16,18},{17,... | collective-permute-start | bytes 74120 | tf_op jit(solution)/shard_map/ppermute | solution.py:20
  112.0 2.7 %all-to-all-done.2 = f32[4,16,24,130]{3,2,1,0:T(8,128)S(1)} async-done(((f32[4,16,24,130]{3,2,1,0:T(8,128)}), f32[4,16,24,130]{3,2,1,0:T(8,128)S(1)}, u32[]{:S(2)}, u32[]{:S(2)}) %all-to-all-start.2) | async-done | bytes 798752 | tf_op jit(solution)/shard_map/all_to_all | solution.py:97
  117.9 3.5 %all-to-all-start.3 = ((f32[2,16,10,130]{3,1,2,0:T(8,128)}), f32[2,16,10,130]{3,1,2,0:T(8,128)S(1)}, u32[]{:S(2)}, u32[]{:S(2)}) async-start(f32[2,16,10,130]{3,1,2,0:T(8,128)} %copy.25), calls=%async_computation.3 | async-start | bytes 655360 | tf_op jit(solution)/shard_map/all_to_all | solution.py:101
  124.2 2.6 %all-to-all-done.3 = f32[2,16,10,130]{3,1,2,0:T(8,128)S(1)} async-done(((f32[2,16,10,130]{3,1,2,0:T(8,128)}), f32[2,16,10,130]{3,1,2,0:T(8,128)S(1)}, u32[]{:S(2)}, u32[]{:S(2)}) %all-to-all-start.3) | async-done | bytes 166432 | tf_op jit(solution)/shard_map/all_to_all | solution.py:101
  130.9 3.3 %copy.27 = f32[16,24,384]{0,2,1:T(8,128)} copy(f32[16,24,384]{2,1,0:T(8,128)S(1)} %fusion.17) | data formatting | bytes 1179648 | tf_op jit(solution)/shard_map/jit(_where)/select_n | solution.py:135
  134.2 8.2 %reshape.371 = f32[16,8,3,128,3]{0,4,3,2,1:T(4,128)} reshape(f32[16,24,384]{0,2,1:T(8,128)} %copy.27) | data formatting | bytes 1179648 | tf_op jit(solution)/shard_map/reshape | solution.py:136
  142.3 5.1 %reduce_sum.49 = f32[16,8,128]{0,2,1:T(8,128)S(1)} reduce(f32[16,8,3,128,3]{0,4,3,2,1:T(4,128)} %reshape.371, f32[]{:T(128)} %constant.92.clone.1), dimensions={2,4}, to_apply=%region_4.5 | reduce | flops 131072 | bytes 655364 | tf_op jit(solution)/shard_map/reduce_sum | solution.py:136
  148.3 3.4 %all-to-all-start.4 = ((f32[2,16,8,128]{3,2,1,0:T(8,128)}), f32[2,16,8,128]{3,2,1,0:T(8,128)S(1)}, u32[]{:S(2)}, u32[]{:S(2)}) async-start(f32[2,16,8,128]{3,2,1,0:T(8,128)} %broadcast_select_fusion.1), calls=%async_computation.4 | async-start | bytes 262144 | tf_op jit(solution)/shard_map/all_to_all | solution.py:154
  151.7 4.4 %all-to-all-done.4 = f32[2,16,8,128]{3,2,1,0:T(8,128)S(1)} async-done(((f32[2,16,8,128]{3,2,1,0:T(8,128)}), f32[2,16,8,128]{3,2,1,0:T(8,128)S(1)}, u32[]{:S(2)}, u32[]{:S(2)}) %all-to-all-start.4) | async-done | bytes 131104 | tf_op jit(solution)/shard_map/all_to_all | solution.py:154
  157.5 12.6 %all-to-all-start.5 = ((f32[4,16,24,128]{3,2,1,0:T(8,128)}), f32[4,16,24,128]{3,2,1,0:T(8,128)S(1)}, u32[]{:S(2)}, u32[]{:S(2)}) async-start(f32[4,16,24,128]{3,2,1,0:T(8,128)} %broadcast_select_fusion), calls=%async_computation.5 | async-start | bytes 1572864 | tf_op jit(solution)/shard_map/all_to_all | solution.py:159
  173.6 14.4 %all-to-all-done.5 = f32[4,16,24,128]{3,2,1,0:T(8,128)S(1)} async-done(((f32[4,16,24,128]{3,2,1,0:T(8,128)}), f32[4,16,24,128]{3,2,1,0:T(8,128)S(1)}, u32[]{:S(2)}, u32[]{:S(2)}) %all-to-all-start.5) | async-done | bytes 786464 | tf_op jit(solution)/shard_map/all_to_all | solution.py:159
  188.0 1.7 fusion.3
  (89 shorter events, 34.4 us)
Async XLA Ops:
  5.9 6.5 %copy-start = (f32[16,24,384]{2,1,0:T(8,128)S(1)}, f32[16,24,384]{2,1,0:T(8,128)}, u32[]{:S(2)}) copy-start(f32[16,24,384]{2,1,0:T(8,128)} %param.6) | copy-start | bytes 1769476
  5.9 11.9 %copy-start.4 = (s32[2]{0:T(128)S(1)}, s32[2]{0:T(128)}, u32[]{:S(2)}) copy-start(s32[2]{0:T(128)} %param.11) | copy-start | bytes 28
  5.9 44.5 %all-to-all-start = ((f32[4,16,24,130]{3,2,1,0:T(8,128)}), f32[4,16,24,130]{3,2,1,0:T(8,128)S(1)}, u32[]{:S(2)}, u32[]{:S(2)}) async-start(f32[4,16,24,130]{3,2,1,0:T(8,128)} %convolution_bitcast_fusion.1), calls=%async_computation | async-start | bytes 3145728 | tf_op jit(solution)/shard_map/all_to_all | solution.py:97
  12.5 29.6 %collective-permute-start = (f32[16,24,1]{2,1,0:T(8,128)S(1)}, f32[16,24,1]{2,1,0:T(8,128)S(1)}, u32[]{:S(2)}, u32[]{:S(2)}) collective-permute-start(f32[16,24,1]{2,1,0:T(8,128)S(1)} %get-tuple-element.15), channel_id=1, source_target_pairs={{0,4},{4,8},{8,12},{1,5},{5,9},{9,13},{2,6},{6,10},{10,14},{3,7},{... | collective-permute-start | bytes 4616 | tf_op jit(solution)/shard_map/ppermute | solution.py:20
  16.4 25.6 %collective-permute-start.1 = (f32[16,24,1]{2,1,0:T(8,128)S(1)}, f32[16,24,1]{2,1,0:T(8,128)S(1)}, u32[]{:S(2)}, u32[]{:S(2)}) collective-permute-start(f32[16,24,1]{2,1,0:T(8,128)S(1)} %get-tuple-element.16), channel_id=1, source_target_pairs={{4,0},{8,4},{12,8},{5,1},{9,5},{13,9},{6,2},{10,6},{14,10},{7,3},{... | collective-permute-start | bytes 4616 | tf_op jit(solution)/shard_map/ppermute | solution.py:21
  42.3 13.0 %collective-permute-start.2 = (f32[16,1,386]{2,1,0:T(1,128)S(1)}, f32[16,1,386]{2,1,0:T(1,128)S(1)}, u32[]{:S(2)}, u32[]{:S(2)}) collective-permute-start(f32[16,1,386]{2,1,0:T(1,128)S(1)} %get-tuple-element.11), channel_id=1, source_target_pairs={{0,2},{1,3},{4,6},{5,7},{8,10},{9,11},{12,14},{13,15},{16,18},{17,... | collective-permute-start | bytes 74120 | tf_op jit(solution)/shard_map/ppermute | solution.py:20
  45.7 9.6 %collective-permute-start.3 = (f32[16,1,386]{2,1,0:T(1,128)S(1)}, f32[16,1,386]{2,1,0:T(1,128)S(1)}, u32[]{:S(2)}, u32[]{:S(2)}) collective-permute-start(f32[16,1,386]{2,1,0:T(1,128)S(1)} %get-tuple-element.12), channel_id=1, source_target_pairs={{2,0},{3,1},{6,4},{7,5},{10,8},{11,9},{14,12},{15,13},{18,16},{19,... | collective-permute-start | bytes 74120 | tf_op jit(solution)/shard_map/ppermute | solution.py:21
  51.8 9.0 %all-to-all-start.1 = ((f32[2,16,10,130]{3,1,2,0:T(8,128)}), f32[2,16,10,130]{3,1,2,0:T(8,128)S(1)}, u32[]{:S(2)}, u32[]{:S(2)}) async-start(f32[2,16,10,130]{3,1,2,0:T(8,128)} %copy.23), calls=%async_computation.1 | async-start | bytes 655360 | tf_op jit(solution)/shard_map/all_to_all | solution.py:101
  55.4 7.1 %collective-permute-start.4 = (f32[1,26,386]{2,1,0:T(8,128)S(1)}, f32[1,26,386]{2,1,0:T(8,128)S(1)}, u32[]{:S(2)}, u32[]{:S(2)}) collective-permute-start(f32[1,26,386]{2,1,0:T(8,128)S(1)} %get-tuple-element.7), channel_id=1, source_target_pairs={{0,1},{2,3},{4,5},{6,7},{8,9},{10,11},{12,13},{14,15},{16,17},{18,... | collective-permute-start | bytes 120440 | tf_op jit(solution)/shard_map/ppermute | solution.py:20
  56.7 5.8 %collective-permute-start.5 = (f32[1,26,386]{2,1,0:T(8,128)S(1)}, f32[1,26,386]{2,1,0:T(8,128)S(1)}, u32[]{:S(2)}, u32[]{:S(2)}) collective-permute-start(f32[1,26,386]{2,1,0:T(8,128)S(1)} %get-tuple-element.8), channel_id=1, source_target_pairs={{1,0},{3,2},{5,4},{7,6},{9,8},{11,10},{13,12},{15,14},{17,16},{19,... | collective-permute-start | bytes 120440 | tf_op jit(solution)/shard_map/ppermute | solution.py:21
  62.6 1.1 copy-start.1
  62.6 1.2 copy-start.2
  67.7 46.9 %all-to-all-start.2 = ((f32[4,16,24,130]{3,2,1,0:T(8,128)}), f32[4,16,24,130]{3,2,1,0:T(8,128)S(1)}, u32[]{:S(2)}, u32[]{:S(2)}) async-start(f32[4,16,24,130]{3,2,1,0:T(8,128)} %convolution_bitcast_fusion), calls=%async_computation.2 | async-start | bytes 3145728 | tf_op jit(solution)/shard_map/all_to_all | solution.py:97
  78.6 27.7 %collective-permute-start.6 = (f32[16,24,1]{2,1,0:T(8,128)S(1)}, f32[16,24,1]{2,1,0:T(8,128)S(1)}, u32[]{:S(2)}, u32[]{:S(2)}) collective-permute-start(f32[16,24,1]{2,1,0:T(8,128)S(1)} %get-tuple-element.13), channel_id=1, source_target_pairs={{0,4},{4,8},{8,12},{1,5},{5,9},{9,13},{2,6},{6,10},{10,14},{3,7},{... | collective-permute-start | bytes 4616 | tf_op jit(solution)/shard_map/ppermute | solution.py:20
  82.8 23.5 %collective-permute-start.7 = (f32[16,24,1]{2,1,0:T(8,128)S(1)}, f32[16,24,1]{2,1,0:T(8,128)S(1)}, u32[]{:S(2)}, u32[]{:S(2)}) collective-permute-start(f32[16,24,1]{2,1,0:T(8,128)S(1)} %get-tuple-element.14), channel_id=1, source_target_pairs={{4,0},{8,4},{12,8},{5,1},{9,5},{13,9},{6,2},{10,6},{14,10},{7,3},{... | collective-permute-start | bytes 4616 | tf_op jit(solution)/shard_map/ppermute | solution.py:21
  106.6 14.8 %collective-permute-start.8 = (f32[16,1,386]{2,1,0:T(1,128)S(1)}, f32[16,1,386]{2,1,0:T(1,128)S(1)}, u32[]{:S(2)}, u32[]{:S(2)}) collective-permute-start(f32[16,1,386]{2,1,0:T(1,128)S(1)} %get-tuple-element.9), channel_id=1, source_target_pairs={{0,2},{1,3},{4,6},{5,7},{8,10},{9,11},{12,14},{13,15},{16,18},{17,... | collective-permute-start | bytes 74120 | tf_op jit(solution)/shard_map/ppermute | solution.py:20
  110.7 10.7 %collective-permute-start.9 = (f32[16,1,386]{2,1,0:T(1,128)S(1)}, f32[16,1,386]{2,1,0:T(1,128)S(1)}, u32[]{:S(2)}, u32[]{:S(2)}) collective-permute-start(f32[16,1,386]{2,1,0:T(1,128)S(1)} %get-tuple-element.10), channel_id=1, source_target_pairs={{2,0},{3,1},{6,4},{7,5},{10,8},{11,9},{14,12},{15,13},{18,16},{19,... | collective-permute-start | bytes 74120 | tf_op jit(solution)/shard_map/ppermute | solution.py:21
  117.9 9.0 %all-to-all-start.3 = ((f32[2,16,10,130]{3,1,2,0:T(8,128)}), f32[2,16,10,130]{3,1,2,0:T(8,128)S(1)}, u32[]{:S(2)}, u32[]{:S(2)}) async-start(f32[2,16,10,130]{3,1,2,0:T(8,128)} %copy.25), calls=%async_computation.3 | async-start | bytes 655360 | tf_op jit(solution)/shard_map/all_to_all | solution.py:101
  121.5 7.2 %collective-permute-start.10 = (f32[1,26,386]{2,1,0:T(8,128)S(1)}, f32[1,26,386]{2,1,0:T(8,128)S(1)}, u32[]{:S(2)}, u32[]{:S(2)}) collective-permute-start(f32[1,26,386]{2,1,0:T(8,128)S(1)} %get-tuple-element.5), channel_id=1, source_target_pairs={{0,1},{2,3},{4,5},{6,7},{8,9},{10,11},{12,13},{14,15},{16,17},{18,... | collective-permute-start | bytes 120440 | tf_op jit(solution)/shard_map/ppermute | solution.py:20
  122.8 5.9 %collective-permute-start.11 = (f32[1,26,386]{2,1,0:T(8,128)S(1)}, f32[1,26,386]{2,1,0:T(8,128)S(1)}, u32[]{:S(2)}, u32[]{:S(2)}) collective-permute-start(f32[1,26,386]{2,1,0:T(8,128)S(1)} %get-tuple-element.6), channel_id=1, source_target_pairs={{1,0},{3,2},{5,4},{7,6},{9,8},{11,10},{13,12},{15,14},{17,16},{19,... | collective-permute-start | bytes 120440 | tf_op jit(solution)/shard_map/ppermute | solution.py:21
  128.6 1.1 copy-start.3
  148.3 7.8 %all-to-all-start.4 = ((f32[2,16,8,128]{3,2,1,0:T(8,128)}), f32[2,16,8,128]{3,2,1,0:T(8,128)S(1)}, u32[]{:S(2)}, u32[]{:S(2)}) async-start(f32[2,16,8,128]{3,2,1,0:T(8,128)} %broadcast_select_fusion.1), calls=%async_computation.4 | async-start | bytes 262144 | tf_op jit(solution)/shard_map/all_to_all | solution.py:154
  156.5 31.4 %copy-start.5 = (f32[16]{0:T(128)S(1)}, f32[16]{0:T(128)}, u32[]{:S(2)}) copy-start(f32[16]{0:T(128)} %param.9) | copy-start | bytes 196
  157.5 30.5 %all-to-all-start.5 = ((f32[4,16,24,128]{3,2,1,0:T(8,128)}), f32[4,16,24,128]{3,2,1,0:T(8,128)S(1)}, u32[]{:S(2)}, u32[]{:S(2)}) async-start(f32[4,16,24,128]{3,2,1,0:T(8,128)} %broadcast_select_fusion), calls=%async_computation.5 | async-start | bytes 1572864 | tf_op jit(solution)/shard_map/all_to_all | solution.py:159
where the time goes:
time: 191 us; the launch traced here: 190 us
  waiting for transfers between devices  71.9 us (38%)
  starting transfers between devices  66 us (35%)
  other arithmetic  17.9 us (9%)
  local copies, waits for them, and re-layouts  16.9 us (9%)
  matrix products  13.8 us (7%)
  between operations  3.15 us (2%)
    ppermute x6, waiting for transfers between devices, padded_2(): before = lax.ppermute(last, axis, up)  41.7 us
    ppermute x6, starting transfers between devices, padded_2(): before = lax.ppermute(last, axis, up)  18.2 us
    all_to_all x2, starting transfers between devices, boundary(): lax.all_to_all(pieces, 'tiles', split_axis=0, concat_axis=0, tiled=True)  17 us
    all_to_all x1, waiting for transfers between devices, per_device(): lax.all_to_all(pieces, 'tiles', split_axis=0, concat_axis=0, tiled=True)  14.4 us
    all_to_all x1, starting transfers between devices, per_device(): lax.all_to_all(pieces, 'tiles', split_axis=0, concat_axis=0, tiled=True)  12.6 us
    reshape x1, local copies, waits for them, and re-layouts, per_device(): coarse = step_two.reshape(levels, third_y, 3, third_x, 3).mean(axis=(2, 4))  8.15 us
    ppermute x6, starting transfers between devices, padded_2(): after = lax.ppermute(first, axis, down)  7.93 us
    all_to_all x2, starting transfers between devices, boundary(): lax.all_to_all(pieces, 'rows', split_axis=0, concat_axis=0, tiled=True)  6.91 us
  transfers between devices with their start and end apart: 18, of which 8 were waited for; matrix products, arithmetic and copies ran while one was open for 8% of the time, Pallas kernels for 0%

commit v1 on v0

--- a/solution.py
+++ b/solution.py
@@ -1,6 +1,10 @@
+import functools
+
 import jax
 import jax.numpy as jnp
 from jax import lax
+from jax.experimental import pallas as pl
+from jax.experimental.pallas import tpu as pltpu
 from jax.sharding import PartitionSpec as P
 
 VERTICAL_MIX = 0.1
@@ -167,6 +171,655 @@
     return jnp.where(covered, blended, step_two)
 
 
+LANES = 128
+FIRST_LANE = 48
+LAST_LANE = 80
+
+
+def iota(shape, dim):
+    return lax.broadcasted_iota(jnp.int32, shape, dim)
+
+
+def split_level(place, height):
+    level = ((place.astype(jnp.float32) + 0.5) * (1.0 / height)).astype(jnp.int32)
+    return level, place - level * height
+
+
+def table(values):
+    return values.astype(jnp.float32).astype(jnp.bfloat16)
+
+
+def parts_of(array):
+    high = array.astype(jnp.bfloat16)
+    rest = array - high.astype(jnp.float32)
+    middle = rest.astype(jnp.bfloat16)
+    low = (rest - middle.astype(jnp.float32)).astype(jnp.bfloat16)
+    return high, middle, low
+
+
+def dot(left, right):
+    return jnp.dot(left, right, preferred_element_type=jnp.float32)
+
+
+def from_left(weights, array):
+    high, middle, low = parts_of(array)
+    return dot(weights, high) + (dot(weights, middle) + dot(weights, low))
+
+
+def from_right(array, weights):
+    high, middle, low = parts_of(array)
+    return dot(high, weights) + (dot(middle, weights) + dot(low, weights))
+
+
+def hat(distance):
+    return jnp.maximum(0, 3 - jnp.abs(distance - 1))
+
+
+def place():
+    return lax.axis_index("tiles"), lax.axis_index("rows"), lax.axis_index("lev")
+
+
+def level_table(levels, height):
+    shape = (levels, levels * height)
+    level, _ = split_level(iota(shape, 1), height)
+    return table(iota(shape, 0) == level)
+
+
+def spread_table(levels, height):
+    shape = (levels * height, levels)
+    level, _ = split_level(iota(shape, 0), height)
+    return table(iota(shape, 1) == level)
+
+
+def row_table(levels, height, row):
+    shape = (levels, levels * height)
+    level, line = split_level(iota(shape, 1), height)
+    return table((iota(shape, 0) == level) & (line == row))
+
+
+def column_table(breadth, third, first_x, west):
+    shape = (breadth, third + LANES)
+    slot = iota(shape, 1)
+    target = jnp.where(
+        slot < third, west + slot, jnp.where(slot == third, west - 1, west + third)
+    )
+    return table((iota(shape, 0) + first_x == target) & (slot < third + 2))
+
+
+def window_rows_table(count, levels, height, first_y, top):
+    shape = (count * levels, levels * height)
+    taken = iota(shape, 0)
+    slot = taken // levels
+    level, line = split_level(iota(shape, 1), height)
+    return table((taken - slot * levels == level) & (line + first_y == top + slot))
+
+
+def store_window(ref, window, count, levels, third):
+    extra = jnp.zeros((levels, LANES), jnp.float32)
+    for slot in range(count):
+        rows = window[slot * levels : (slot + 1) * levels]
+        ref[slot] = rows[:, :third]
+        beside = rows[:, third:]
+        extra = extra + (pltpu.roll(beside, 2 * slot, 1) if slot else beside)
+    return extra
+
+
+def pack_edges(flat, levels, height):
+    breadth = flat.shape[1]
+    shape = (levels * height, LANES)
+    lane = iota(shape, 1)
+    _, line = split_level(iota(shape, 0), height)
+    columns = jnp.where(lane == line + FIRST_LANE, flat[:, 0:1], 0.0)
+    columns = jnp.where(lane == line + LAST_LANE, flat[:, breadth - 1 : breadth], columns)
+    return from_left(level_table(levels, height), columns)
+
+
+def neighbour_columns(by_one, by_three, parent_tiles, tile):
+    odd = tile % 2 == 1
+    west = jnp.where(odd, by_one, by_three)
+    east = jnp.where(odd, by_three, by_one)
+    west = jnp.where(tile == 0, jnp.zeros_like(west), west)
+    east = jnp.where(tile >= parent_tiles - 1, jnp.zeros_like(east), east)
+    return jnp.where(iota(west.shape, 1) < LAST_LANE, east, west)
+
+
+def unpack_edges(columns, levels, height):
+    wide = from_left(spread_table(levels, height), columns)
+    lane = iota(wide.shape, 1)
+    _, line = split_level(iota(wide.shape, 0), height)
+    west = jnp.sum(jnp.where(lane == line + LAST_LANE, wide, 0.0), axis=1, keepdims=True)
+    east = jnp.sum(jnp.where(lane == line + FIRST_LANE, wide, 0.0), axis=1, keepdims=True)
+    return jnp.where(lane == 0, west, jnp.where(lane == 1, east, 0.0))
+
+
+def join_row(ref, first, count):
+    return jnp.concatenate([ref[first + i] for i in range(count)], axis=1)
+
+
+def unpack_window(slabs, extra):
+    beside = [pltpu.roll(extra, (LANES - 2 * s) % LANES, 1) if s else extra for s in range(len(slabs))]
+    return jnp.concatenate(
+        [jnp.concatenate(slabs, axis=0), jnp.concatenate(beside, axis=0)], axis=1
+    )
+
+
+def refine(window, levels, height, breadth, row):
+    slots = window.shape[0] // levels
+    third = breadth // 3
+    shape = (third + LANES, breadth + LANES)
+    slot, cell = iota(shape, 0), iota(shape, 1)
+    at = jnp.where(slot < third, slot, jnp.where(slot == third, -1, third))
+    cell = jnp.where(cell == breadth, -1, jnp.where(cell == breadth + 1, breadth, cell))
+    across = jnp.where((slot < third + 2) & (cell <= breadth), hat(cell - 3 * at), 0)
+    wide = from_right(window, table(across))
+    shape = (levels * height, slots * levels)
+    taken = iota(shape, 1)
+    slot = taken // levels
+    level, line = split_level(iota(shape, 0), height)
+    along = jnp.where(taken - slot * levels == level, hat(line - 3 * (slot - 1)), 0)
+    shape = (levels, slots * levels)
+    taken = iota(shape, 1)
+    slot = taken // levels
+    line = jnp.where(row == 0, -1, height)
+    outer = jnp.where(taken - slot * levels == iota(shape, 0), hat(line - 3 * (slot - 1)), 0)
+    high, middle, low = parts_of(wide)
+    along, outer = table(along), table(outer)
+    cells = dot(along, high) + (dot(along, middle) + dot(along, low))
+    ring = dot(outer, high) + (dot(outer, middle) + dot(outer, low))
+    return cells * (1.0 / 9.0), ring[:, :breadth] * (1.0 / 9.0)
+
+
+def beside_rows(x, north, south):
+    height = x.shape[0]
+    line = iota(x.shape, 0)
+    northern = jnp.where(line == 0, north, pltpu.roll(x, 1, 0))
+    southern = jnp.where(line == height - 1, south, pltpu.roll(x, height - 1, 0))
+    return northern, southern
+
+
+def beside_columns(x, west, east):
+    breadth = x.shape[1]
+    column = iota(x.shape, 1)
+    western = jnp.where(column == 0, west, pltpu.roll(x, 1, 1))
+    eastern = jnp.where(column == breadth - 1, east, pltpu.roll(x, breadth - 1, 1))
+    return western, eastern
+
+
+def change_of(x, sides, u, v, upper, lower, advect_scale, mixing_scale):
+    northern, southern, western, eastern = sides
+    advect = u * (eastern - western) + v * (southern - northern)
+    horizontal = eastern + western + southern + northern - 4.0 * x
+    vertical = upper + lower - 2.0 * x
+    return -0.5 * advect_scale * advect + mixing_scale * horizontal + VERTICAL_MIX * vertical
+
+
+def vertical_sides(ref, l, level_ref, lev):
+    levels = ref.shape[0]
+    zero = jnp.zeros(ref.shape[1:], jnp.float32)
+    lower = ref[l - 1] if l > 0 else jnp.where(lev == 1, level_ref[...], zero)
+    upper = ref[l + 1] if l < levels - 1 else jnp.where(lev == 0, level_ref[...], zero)
+    return upper, lower
+
+
+def full_step(
+    out_ref, field_ref, u_ref, v_ref, level_ref, north_ref, south_ref, side_ref, fine_ref, lev, nest
+):
+    levels, height, breadth = field_ref.shape
+    for l in range(levels):
+        x = field_ref[l]
+        upper, lower = vertical_sides(field_ref, l, level_ref, lev)
+        side = side_ref[pl.ds(l * height, height)]
+        northern, southern = beside_rows(x, north_ref[pl.ds(l, 1)], south_ref[pl.ds(l, 1)])
+        western, eastern = beside_columns(x, side[:, 0:1], side[:, 1:2])
+        change = change_of(
+            x,
+            (northern, southern, western, eastern),
+            u_ref[l],
+            v_ref[l],
+            upper,
+            lower,
+            NEST_ADVECT if nest else 1.0,
+            NEST_MIXING if nest else PARENT_MIXING,
+        )
+        fresh = x + change
+        if nest:
+            fresh = fresh + NUDGING * (fine_ref[pl.ds(l * height, height)] - x)
+        out_ref[l] = fresh
+
+
+def inner_row(height, row):
+    return jnp.where(row == 0, height - 1, 0)
+
+
+def pack_kernel(slots, west_ref, south_ref, air_ref, north_ref, rows_ref, own_ref, level_ref):
+    levels, height, breadth = air_ref.shape
+    third_x, third_y = breadth // 3, height // 3
+    pieces = breadth // LANES
+    tile, row, lev = place()
+    nest = tile == lax.axis_size("tiles") - 1
+    level_ref[...] = jnp.where(lev == 0, air_ref[levels - 1], air_ref[0])
+    flat = air_ref[...].reshape(levels * height, breadth)
+    edge = row_table(levels, height, inner_row(height, row))
+    shared = from_left(edge, flat)
+    for i in range(pieces):
+        rows_ref[slots + 1 + i] = shared[:, i * LANES : (i + 1) * LANES]
+
+    @pl.when(nest)
+    def _():
+        speed = from_left(edge, north_ref[...].reshape(levels * height, breadth))
+        for i in range(pieces):
+            rows_ref[i] = speed[:, i * LANES : (i + 1) * LANES]
+        for i in range(pieces, slots + 1):
+            rows_ref[i] = jnp.zeros((levels, LANES), jnp.float32)
+        own_ref[...] = jnp.zeros_like(own_ref)
+
+    @pl.when(jnp.logical_not(nest))
+    def _():
+        columns = column_table(breadth, third_x, tile * breadth, west_ref[0])
+        high, middle, low = parts_of(from_right(flat, columns))
+        for ref, block in ((rows_ref, 1 - row), (own_ref, row)):
+            top = south_ref[0] + block * third_y - 1
+            picked = window_rows_table(slots, levels, height, row * height, top)
+            window = dot(picked, high) + (dot(picked, middle) + dot(picked, low))
+            extra = store_window(ref, window, slots, levels, third_x)
+            ref[slots] = extra
+        own_ref[slots] = own_ref[slots] + pack_edges(flat, levels, height)
+
+
+def first_kernel(
+    slots,
+    west_ref,
+    south_ref,
+    air_ref,
+    east_ref,
+    north_ref,
+    rows_ref,
+    level_ref,
+    one_ref,
+    two_ref,
+    three_ref,
+    out_ref,
+    edge_ref,
+    message_ref,
+    fine_ref,
+    side_ref,
+    northern_ref,
+    southern_ref,
+):
+    levels, height, breadth = air_ref.shape
+    third_x, third_y = breadth // 3, height // 3
+    pieces = breadth // LANES
+    tile_count = lax.axis_size("tiles")
+    tile, row, lev = place()
+    nest = tile == tile_count - 1
+    halo = join_row(rows_ref, slots + 1, pieces)
+
+    @pl.when(nest)
+    def _():
+        slabs = [one_ref[s] + two_ref[s] + three_ref[s] for s in range(slots + 1)]
+        window = unpack_window(slabs[:slots], slabs[slots])
+        cells, ring = refine(window, levels, height, breadth, row)
+        fine_ref[...] = cells[:, :breadth]
+        side_ref[...] = cells[:, breadth:]
+        northern_ref[...] = jnp.where(row == 0, ring, halo)
+        southern_ref[...] = jnp.where(row == 0, halo, ring)
+        full_step(
+            out_ref, air_ref, east_ref, north_ref, level_ref, northern_ref, southern_ref, side_ref, fine_ref, lev, True
+        )
+
+    @pl.when(jnp.logical_not(nest))
+    def _():
+        columns = neighbour_columns(one_ref[slots], three_ref[slots], tile_count - 1, tile)
+        side_ref[...] = unpack_edges(columns, levels, height)
+        zero = jnp.zeros_like(halo)
+        northern_ref[...] = jnp.where(row == 0, zero, halo)
+        southern_ref[...] = jnp.where(row == 0, halo, zero)
+        full_step(
+            out_ref, air_ref, east_ref, north_ref, level_ref, northern_ref, southern_ref, side_ref, fine_ref, lev, False
+        )
+        flat = out_ref[...].reshape(levels * height, breadth)
+        picked = column_table(breadth, third_x, tile * breadth, west_ref[1])
+        count = message_ref.shape[0] - 1
+        rows = window_rows_table(count, levels, height, row * height, south_ref[1] - 1)
+        window = from_left(rows, from_right(flat, picked))
+        extra = store_window(message_ref, window, count, levels, third_x)
+        message_ref[count] = extra + pack_edges(flat, levels, height)
+
+    edge_ref[...] = jnp.where(lev == 0, out_ref[levels - 1], out_ref[0])
+
+
+def average_kernel(slots, field_ref, east_ref, north_ref, rows_ref, level_ref, given_ref, message_ref, part_ref):
+    levels, height, breadth = field_ref.shape
+    third_x, third_y = breadth // 3, height // 3
+    pieces = breadth // LANES
+    size = levels * height
+    tile, row, lev = place()
+    nest = tile == lax.axis_size("tiles") - 1
+
+    @pl.when(jnp.logical_not(nest))
+    def _():
+        message_ref[...] = given_ref[...]
+
+    @pl.when(nest)
+    def _():
+        for l in range(levels):
+            x = field_ref[l]
+            upper, lower = vertical_sides(field_ref, l, level_ref, lev)
+            sides = beside_rows(x, 0.0, 0.0) + beside_columns(x, 0.0, 0.0)
+            change = change_of(x, sides, east_ref[l], north_ref[l], upper, lower, NEST_ADVECT, NEST_MIXING)
+            part_ref[pl.ds(l * height, height)] = x + change - NUDGING * x
+        cell, third = iota((breadth, third_x), 0), iota((breadth, third_x), 1)
+        offset = cell - 3 * third
+        sums = table((offset >= 0) & (offset <= 2))
+        shape = (third_y * levels, size)
+        taken = iota(shape, 0)
+        block = taken // levels
+        level, line = split_level(iota(shape, 1), height)
+        offset_y = line - 3 * block
+        rows = table((taken - block * levels == level) & (offset_y >= 0) & (offset_y <= 2))
+        means = from_left(rows, from_right(part_ref[...], sums)) * (1.0 / 9.0)
+        for m in range(third_y):
+            message_ref[m] = means[m * levels : (m + 1) * levels]
+        flat = field_ref[...].reshape(size, breadth)
+        speed = north_ref[...].reshape(size, breadth)
+        inner = inner_row(height, row)
+        outer = height - 1 - inner
+        sign = jnp.where(row == 0, 0.5 * NEST_ADVECT, -0.5 * NEST_ADVECT)
+        shared = from_left(row_table(levels, height, inner), flat)
+        shared = (sign * join_row(rows_ref, 0, pieces) + NEST_MIXING) * shared
+        ghost = sign * from_left(row_table(levels, height, outer), speed) + NEST_MIXING
+        message_ref[third_y + 4] = from_right(shared, sums) * (1.0 / 9.0)
+        weights = (
+            table(offset == 0),
+            table(jnp.where(offset == 1, 3, jnp.where((offset == 0) | (offset == 2), 2, 0))),
+            table(offset == 2),
+        )
+        for q in range(3):
+            message_ref[third_y + q] = from_right(ghost, weights[q]) * (1.0 / 27.0)
+        shape = (size, LANES)
+        lane = iota(shape, 1)
+        _, line = split_level(iota(shape, 0), height)
+        block = lane // 8
+        inside = lane - block * 8
+        eastern = inside >= 3
+        kind = jnp.where(eastern, inside - 3, inside)
+        offset = line - 3 * block
+        weight = jnp.where(
+            kind == 1,
+            jnp.where(offset == 1, 3, jnp.where((offset == 0) | (offset == 2), 2, 0)),
+            jnp.where(offset == kind, 1, 0),
+        )
+        weight = jnp.where((inside < 6) & (block < third_y), weight, 0).astype(jnp.float32)
+        speed = east_ref[...].reshape(size, breadth)
+        first = 0.5 * NEST_ADVECT * speed[:, 0:1] + NEST_MIXING
+        last = -0.5 * NEST_ADVECT * speed[:, breadth - 1 : breadth] + NEST_MIXING
+        columns = jnp.where(eastern, last, first) * weight
+        message_ref[third_y + 3] = from_left(level_table(levels, height), columns) * (1.0 / 27.0)
+        for i in range(third_y + 5, message_ref.shape[0]):
+            message_ref[i] = jnp.zeros((levels, LANES), jnp.float32)
+
+
+def nest_message(tile, one_ref, two_ref, three_ref, i):
+    return jnp.where(tile == 0, three_ref[i], jnp.where(tile == 1, two_ref[i], one_ref[i]))
+
+
+def swap_kernel(slots, field_ref, one_ref, two_ref, three_ref, rows_ref):
+    levels, height, breadth = field_ref.shape
+    third_y = height // 3
+    pieces = breadth // LANES
+    tile_count = lax.axis_size("tiles")
+    tile, row, _ = place()
+    nest = tile == tile_count - 1
+    last = one_ref.shape[0] - 1
+    flat = field_ref[...].reshape(levels * height, breadth)
+    edge = from_left(row_table(levels, height, inner_row(height, row)), flat)
+    base = third_y + 5
+    for i in range(pieces):
+        rows_ref[base + i] = edge[:, i * LANES : (i + 1) * LANES]
+
+    @pl.when(nest)
+    def _():
+        first = jnp.where(row == 0, third_y, 0)
+        for s in range(slots):
+            rows_ref[s] = one_ref[first + s] + two_ref[first + s] + three_ref[first + s]
+        extra = one_ref[last] + two_ref[last] + three_ref[last]
+        rows_ref[slots] = jnp.where(row == 0, pltpu.roll(extra, LANES - 2 * third_y, 1), extra)
+        for i in range(slots + 1, base):
+            rows_ref[i] = jnp.zeros((levels, LANES), jnp.float32)
+        rows_ref[base + pieces] = jnp.zeros((levels, LANES), jnp.float32)
+
+    @pl.when(jnp.logical_not(nest))
+    def _():
+        for i in range(base):
+            rows_ref[i] = nest_message(tile, one_ref, two_ref, three_ref, i)
+        columns = neighbour_columns(one_ref[last], three_ref[last], tile_count - 1, tile)
+
+        def moved(lane, to):
+            low = pltpu.roll(columns, (LANES + to - lane) % LANES, 1)
+            high = pltpu.roll(columns, (LANES + to - lane - height + 1) % LANES, 1)
+            return jnp.where(row == 0, high, low)
+
+        lane = iota(columns.shape, 1)
+        corners = jnp.where(lane == 1, moved(FIRST_LANE, 1), 0.0)
+        rows_ref[base + pieces] = jnp.where(lane == 0, moved(LAST_LANE, 0), corners)
+
+
+def last_kernel(
+    slots,
+    west_ref,
+    south_ref,
+    weight_ref,
+    field_ref,
+    east_ref,
+    north_ref,
+    level_ref,
+    rows_ref,
+    one_ref,
+    two_ref,
+    three_ref,
+    out_ref,
+    fine_ref,
+    side_ref,
+    northern_ref,
+    southern_ref,
+    placed_ref,
+    coef_ref,
+    edge_coef_ref,
+):
+    levels, height, breadth = field_ref.shape
+    third_x, third_y = breadth // 3, height // 3
+    pieces = breadth // LANES
+    size = levels * height
+    tile_count = lax.axis_size("tiles")
+    tile, row, lev = place()
+    nest = tile == tile_count - 1
+    last = one_ref.shape[0] - 1
+    base = third_y + 5
+    halo = join_row(rows_ref, base, pieces)
+
+    @pl.when(nest)
+    def _():
+        first = jnp.where(row == 0, 0, third_y)
+        slabs = [
+            one_ref[first + s] + two_ref[first + s] + three_ref[first + s] + rows_ref[s]
+            for s in range(slots)
+        ]
+        extra = one_ref[last] + two_ref[last] + three_ref[last]
+        extra = jnp.where(row == 0, extra, pltpu.roll(extra, LANES - 2 * third_y, 1))
+        window = unpack_window(slabs, extra + rows_ref[slots])
+        cells, ring = refine(window, levels, height, breadth, row)
+        fine_ref[...] = cells[:, :breadth]
+        side_ref[...] = cells[:, breadth:]
+        northern_ref[...] = jnp.where(row == 0, ring, halo)
+        southern_ref[...] = jnp.where(row == 0, halo, ring)
+        full_step(
+            out_ref, field_ref, east_ref, north_ref, level_ref, northern_ref, southern_ref, side_ref, fine_ref, lev, True
+        )
+
+    @pl.when(jnp.logical_not(nest))
+    def _():
+        west, south = west_ref[1], south_ref[1]
+        columns = neighbour_columns(one_ref[last], three_ref[last], tile_count - 1, tile)
+        side_ref[...] = unpack_edges(columns, levels, height)
+        zero = jnp.zeros_like(halo)
+        northern_ref[...] = jnp.where(row == 0, zero, halo)
+        southern_ref[...] = jnp.where(row == 0, halo, zero)
+
+        def block_slab(block, i):
+            mine = nest_message(tile, one_ref, two_ref, three_ref, i)
+            return jnp.where(row == block, mine, rows_ref[i])
+
+        means, beside = [], []
+        for block in range(2):
+            slabs = [block_slab(block, m) for m in range(third_y)]
+            correction = block_slab(1 - block, third_y + 4)
+            near = third_y - 1 if block == 0 else 0
+            slabs[near] = slabs[near] + correction
+            means += slabs
+            edges = block_slab(block, third_y + 3)
+            beside += [pltpu.roll(edges, LANES - 8 * m, 1) if m else edges for m in range(third_y)]
+        ghosts = [block_slab(block, third_y + q) for q in range(3) for block in range(2)]
+        shape = (third_x, breadth)
+        spread = table(iota(shape, 1) + tile * breadth == west + iota(shape, 0))
+        wide = from_right(jnp.concatenate(means + ghosts, axis=0), spread)
+        count = 2 * third_y * levels
+        both = jnp.concatenate([wide[:count], jnp.concatenate(beside, axis=0)], axis=1)
+        shape = (size, count)
+        taken = iota(shape, 1)
+        block = taken // levels
+        level, line = split_level(iota(shape, 0), height)
+        rows = (taken - block * levels == level) & (line + row * height == south + block)
+        both = from_left(table(rows), both)
+        placed_ref[...] = both[:, :breadth]
+        edge_coef_ref[...] = both[:, breadth:]
+        shape = (size, 2 * levels)
+        taken = iota(shape, 1)
+        block = taken // levels
+        level, line = split_level(iota(shape, 0), height)
+        target = south + block * (2 * third_y - 1)
+        rows = table((taken - block * levels == level) & (line + row * height == target))
+        for q in range(3):
+            piece = wide[count + 2 * q * levels : count + 2 * (q + 1) * levels]
+            coef_ref[q] = from_left(rows, piece)
+        line = iota((height, breadth), 0) + row * height
+        column = iota((height, breadth), 1) + tile * breadth
+        covered = (column >= west) & (column < west + third_x)
+        covered = covered & (line >= south) & (line < south + 2 * third_y)
+        top_row = line == south
+        first_column = column == west
+        last_column = column == west + third_x - 1
+        two, one = 2.0 / 3.0, 1.0 / 3.0
+        for l in range(levels):
+            part = pl.ds(l * height, height)
+            x = field_ref[l]
+            side = side_ref[part]
+            corner = rows_ref[base + pieces, pl.ds(l, 1)]
+            xn, xs = beside_rows(x, northern_ref[pl.ds(l, 1)], southern_ref[pl.ds(l, 1)])
+            sn, ss = beside_rows(side, corner, corner)
+            xw, xe = beside_columns(x, side[:, 0:1], side[:, 1:2])
+            xnw, xne = beside_columns(xn, sn[:, 0:1], sn[:, 1:2])
+            xsw, xse = beside_columns(xs, ss[:, 0:1], ss[:, 1:2])
+            q, qw, qe = xn + 7.0 * x + xs, xnw + 7.0 * xw + xsw, xne + 7.0 * xe + xse
+            value = placed_ref[part] + (NUDGING / 81.0) * (qw + 7.0 * q + qe)
+
+            def outward(n, c, s):
+                return two * jnp.where(top_row, n, s) + one * c
+
+            value = value + coef_ref[0, part] * outward(xnw, xw, xsw)
+            value = value + coef_ref[1, part] * outward(xn, x, xs)
+            value = value + coef_ref[2, part] * outward(xne, xe, xse)
+            ec = edge_coef_ref[part]
+
+            def sideward(w, c, e):
+                return two * jnp.where(first_column, w, e) + one * c
+
+            def coefficient(q):
+                return jnp.where(
+                    first_column, ec[:, q : q + 1], jnp.where(last_column, ec[:, q + 3 : q + 4], 0.0)
+                )
+
+            value = value + coefficient(0) * sideward(xnw, xn, xne)
+            value = value + coefficient(1) * sideward(xw, x, xe)
+            value = value + coefficient(2) * sideward(xsw, xs, xse)
+            out_ref[l] = jnp.where(covered, x + weight_ref[l] * (value - x), x)
+
+
+def call(kernel, outs, inputs, scalars, scratch=()):
+    smem = pl.BlockSpec(memory_space=pltpu.SMEM)
+    vmem = pl.BlockSpec(memory_space=pltpu.VMEM)
+    shapes = [jax.ShapeDtypeStruct(shape, jnp.float32) for shape in outs]
+    return pl.pallas_call(
+        kernel,
+        out_shape=shapes,
+        in_specs=[smem] * scalars + [vmem] * (len(inputs) - scalars),
+        out_specs=[vmem] * len(outs),
+        scratch_shapes=[pltpu.VMEM(shape, jnp.float32) for shape in scratch],
+        compiler_params=pltpu.CompilerParams(vmem_limit_bytes=48 * 1024 * 1024),
+    )(*inputs)
+
+
+def per_device_paired(air_state, wind_east, wind_north, feedback_weight, nest_west, nest_south):
+    levels, height, breadth = air_state.shape
+    third_y = height // 3
+    pieces = breadth // LANES
+    slots = third_y + 2
+    tile_count = lax.axis_size("tiles")
+    size = levels * height
+    block = (levels, height, breadth)
+    swap = [(0, 1), (1, 0)]
+
+    def slabs(count):
+        return (count, levels, LANES)
+
+    def over_tiles(message):
+        return [
+            lax.ppermute(message, "tiles", [(t, t ^ step) for t in range(tile_count)])
+            for step in (1, 2, 3)
+        ]
+
+    rows, own, level = call(
+        functools.partial(pack_kernel, slots),
+        [slabs(slots + 1 + pieces), slabs(slots + 1), block[1:]],
+        [nest_west, nest_south, air_state, wind_north],
+        2,
+    )
+    rows = lax.ppermute(rows, "rows", swap)
+    level = lax.ppermute(level, "lev", swap)
+    received = over_tiles(own + rows[: slots + 1])
+    steps = [(size, breadth), (size, LANES), (levels, breadth), (levels, breadth)]
+    field, edge, message = call(
+        functools.partial(first_kernel, slots),
+        [block, block[1:], slabs(2 * third_y + 3)],
+        [nest_west, nest_south, air_state, wind_east, wind_north, rows, level, *received],
+        2,
+        steps,
+    )
+    level = lax.ppermute(edge, "lev", swap)
+    (message,) = call(
+        functools.partial(average_kernel, slots),
+        [slabs(2 * third_y + 3)],
+        [field, wind_east, wind_north, rows, level, message],
+        0,
+        [(size, breadth)],
+    )
+    received = over_tiles(message)
+    (rows,) = call(
+        functools.partial(swap_kernel, slots),
+        [slabs(third_y + 6 + pieces)],
+        [field, *received],
+        0,
+    )
+    rows = lax.ppermute(rows, "rows", swap)
+    (out,) = call(
+        functools.partial(last_kernel, slots),
+        [block],
+        [nest_west, nest_south, feedback_weight, field, wind_east, wind_north, level, rows, *received],
+        3,
+        steps + [(size, breadth), (3, size, breadth), (size, LANES)],
+    )
+    return out
+
+
 def solution(mesh):
     in_specs = (
         P(("members", "lev"), "rows", "tiles"),
@@ -177,6 +830,7 @@
         P("members"),
     )
     out_specs = P(("members", "lev"), "rows", "tiles")
+    paired = mesh.shape["tiles"] == 4 and mesh.shape["rows"] == 2 and mesh.shape["lev"] == 2
     return jax.shard_map(
-        per_device, mesh=mesh, in_specs=in_specs, out_specs=out_specs, check_vma=False
-    )
+        per_device_paired if paired else per_device, mesh=mesh, in_specs=in_specs, out_specs=out_specs, check_vma=False
+    )

time: 191 us -> 52.7 us (0.28)
  starting transfers between devices: 66 us -> 13.5 us
  waiting for transfers between devices: 71.9 us -> 25.1 us
  other arithmetic: 17.9 us -> 0.01 us
  matrix products: 13.8 us -> 0 us
  local copies, waits for them, and re-layouts: 16.9 us -> 3.45 us
  Pallas kernels: 0 us -> 10.3 us
  between operations: 3.15 us -> 0.05 us
    all_to_all x6 -> x0, starting transfers between devices: 39.9 us -> none  [the longest x2 17 us: boundary(): lax.all_to_all(pieces, 'tiles', split_axis=0, concat_axis=0, tiled=True)]
    all_to_all x6 -> x0, waiting for transfers between devices: 30.2 us -> none  [the longest x1 14.4 us: per_device(): lax.all_to_all(pieces, 'tiles', split_axis=0, concat_axis=0, tiled=True)]
    ppermute x12 -> x10, waiting for transfers between devices: 41.7 us -> 25.1 us  [the longest x6 15.7 us: over_tiles(): lax.ppermute(message, 'tiles', [(t, t ^ step) for t in range(tile_count)])]
    dot_general x10 -> x0, matrix products: 13.8 us -> none  [the longest x2 6.47 us: boundary(): pieces = jnp.einsum('lyi,tij->tlyj', source, pick_x, precision=highest)]
    ppermute x12 -> x10, starting transfers between devices: 26.2 us -> 13.5 us  [the longest x6 8.91 us: over_tiles(): lax.ppermute(message, 'tiles', [(t, t ^ step) for t in range(tile_count)])]
    pallas_call x0 -> x5, Pallas kernels: none -> 10.3 us  [call(): pl.pallas_call(kernel, out_shape=shapes, in_specs=[smem] * scalars + [vme...]
    reshape x1 -> x0, local copies, waits for them, and re-layouts: 8.15 us -> none  [per_device(): coarse = step_two.reshape(levels, third_y, 3, third_x, 3).mean(axis=(2, 4))]
    reduce_sum x5 -> x0, other arithmetic: 6.14 us -> none  [the longest x1 5.08 us: per_device(): coarse = step_two.reshape(levels, third_y, 3, third_x, 3).mean(axis=(2, 4))]
  transfers between devices with their start and end apart: 18 -> 10, of which waited for: 8 -> 8; matrix products, arithmetic and copies ran while one was open for 8% -> 0% of each run, Pallas kernels for 0% -> 0%
where the time goes in v1:
time: 52.7 us; the launch traced here: 52.4 us
  waiting for transfers between devices  25.1 us (48%)
  starting transfers between devices  13.5 us (26%)
  Pallas kernels  10.3 us (20%)
  local copies, waits for them, and re-layouts  3.45 us (7%)
    ppermute x6, waiting for transfers between devices, over_tiles(): lax.ppermute(message, 'tiles', [(t, t ^ step) for t in range(tile_count)])  15.7 us
    pallas_call x5, Pallas kernels, call(): pl.pallas_call(kernel, out_shape=shapes, in_specs=[smem] * scalars + [vme...  10.3 us
    ppermute x6, starting transfers between devices, over_tiles(): lax.ppermute(message, 'tiles', [(t, t ^ step) for t in range(tile_count)])  8.91 us
    ppermute x2, waiting for transfers between devices, per_device_paired(): rows = lax.ppermute(rows, 'rows', swap)  6.95 us
    ppermute x2, starting transfers between devices, per_device_paired(): rows = lax.ppermute(rows, 'rows', swap)  4.51 us
    unnamed x14, local copies, waits for them, and re-layouts  3.45 us
    ppermute x1, waiting for transfers between devices, per_device_paired(): level = lax.ppermute(level, 'lev', swap)  1.21 us
    ppermute x1, waiting for transfers between devices, per_device_paired(): level = lax.ppermute(edge, 'lev', swap)  1.2 us
  transfers between devices with their start and end apart: 10, of which 8 were waited for; matrix products, arithmetic and copies ran while one was open for 0% of the time, Pallas kernels for 0%

profile of v1, /device:TPU:0, one launch (start us, length us, event | category | flops | bytes accessed | tf_op | source)
XLA Modules:
  0.0 52.4 jit_solution(6027561288172589263)
XLA Ops:
  0.0 1.1 %copy-done = f32[16,24,384]{2,1,0:T(8,128)S(1)} copy-done((f32[16,24,384]{2,1,0:T(8,128)S(1)}, f32[16,24,384]{2,1,0:T(8,128)}, u32[]{:S(2)}) %copy-start) | copy-done | bytes 589848
  1.1 1.1 %copy-done.3 = f32[16,24,384]{2,1,0:T(8,128)S(1)} copy-done((f32[16,24,384]{2,1,0:T(8,128)S(1)}, f32[16,24,384]{2,1,0:T(8,128)}, u32[]{:S(2)}) %copy-start.3) | copy-done | bytes 589848
  2.1 0.7 %copy-done.4 = s32[2]{0:T(128)S(1)} copy-done((s32[2]{0:T(128)S(1)}, s32[2]{0:T(128)}, u32[]{:S(2)}) %copy-start.4) | copy-done | bytes 32
  2.8 0.7 %copy-done.5 = s32[2]{0:T(128)S(1)} copy-done((s32[2]{0:T(128)S(1)}, s32[2]{0:T(128)}, u32[]{:S(2)}) %copy-start.5) | copy-done | bytes 32
  3.4 2.3 %shard_map.64 = (f32[14,16,128]{2,1,0:T(8,128)S(1)}, f32[11,16,128]{2,1,0:T(8,128)S(1)}, f32[24,384]{1,0:T(8,128)S(1)}) custom-call(s32[2]{0:T(128)S(1)} %copy-done.4, s32[2]{0:T(128)S(1)} %copy-done.5, f32[16,24,384]{2,1,0:T(8,128)S(1)} %copy-done.3, f32[16,24,384]{2,1,0:T(8,128)S(1)} %copy-done), custom_call_target="tpu_custom_call" | custom-call | tf_op jit(solution)/shard_map/pallas_call | solution.py:751
  5.8 3.0 %collective-permute-start = (f32[14,16,128]{2,1,0:T(8,128)S(1)}, f32[14,16,128]{2,1,0:T(8,128)S(1)}, u32[]{:S(2)}, u32[]{:S(2)}) collective-permute-start(f32[14,16,128]{2,1,0:T(8,128)S(1)} %get-tuple-element.11), channel_id=1, source_target_pairs={{0,2},{2,0},{1,3},{3,1},{4,6},{6,4},{5,7},{7,5},{8,10},{10,8},{9,1... | collective-permute-start | bytes 344072 | tf_op jit(solution)/shard_map/ppermute | solution.py:786
  8.8 3.1 %collective-permute-done.rows_ref = f32[14,16,128]{2,1,0:T(8,128)S(1)} collective-permute-done((f32[14,16,128]{2,1,0:T(8,128)S(1)}, f32[14,16,128]{2,1,0:T(8,128)S(1)}, u32[]{:S(2)}, u32[]{:S(2)}) %collective-permute-start) | collective-permute-done | bytes 114720 | tf_op jit(solution)/shard_map/ppermute | solution.py:786
  11.9 2.7 %collective-permute-start.4 = (f32[11,16,128]{2,1,0:T(8,128)S(1)}, f32[11,16,128]{2,1,0:T(8,128)S(1)}, u32[]{:S(2)}, u32[]{:S(2)}) collective-permute-start(f32[11,16,128]{2,1,0:T(8,128)S(1)} %slice_add_fusion), channel_id=1, source_target_pairs={{0,12},{4,8},{8,4},{12,0},{1,13},{5,9},{9,5},{13,1},{2,14},{6,10},... | collective-permute-start | bytes 270344 | tf_op jit(solution)/shard_map/ppermute | solution.py:776
  14.7 0.6 %collective-permute-start.3 = (f32[11,16,128]{2,1,0:T(8,128)S(1)}, f32[11,16,128]{2,1,0:T(8,128)S(1)}, u32[]{:S(2)}, u32[]{:S(2)}) collective-permute-start(f32[11,16,128]{2,1,0:T(8,128)S(1)} %slice_add_fusion), channel_id=1, source_target_pairs={{0,8},{4,12},{8,0},{12,4},{1,9},{5,13},{9,1},{13,5},{2,10},{6,14},... | collective-permute-start | bytes 270344 | tf_op jit(solution)/shard_map/ppermute | solution.py:776
  15.3 1.1 %collective-permute-start.2 = (f32[11,16,128]{2,1,0:T(8,128)S(1)}, f32[11,16,128]{2,1,0:T(8,128)S(1)}, u32[]{:S(2)}, u32[]{:S(2)}) collective-permute-start(f32[11,16,128]{2,1,0:T(8,128)S(1)} %slice_add_fusion), channel_id=1, source_target_pairs={{0,4},{4,0},{8,12},{12,8},{1,5},{5,1},{9,13},{13,9},{2,6},{6,2},{1... | collective-permute-start | bytes 270344 | tf_op jit(solution)/shard_map/ppermute | solution.py:776
  16.4 1.2 %collective-permute-done.1.level_ref = f32[24,384]{1,0:T(8,128)S(1)} collective-permute-done((f32[24,384]{1,0:T(8,128)S(1)}, f32[24,384]{1,0:T(8,128)S(1)}, u32[]{:S(2)}, u32[]{:S(2)}) %collective-permute-start.1) | collective-permute-done | bytes 36896 | tf_op jit(solution)/shard_map/ppermute | solution.py:787
  17.6 1.6 %collective-permute-done.4.three_ref = f32[11,16,128]{2,1,0:T(8,128)S(1)} collective-permute-done((f32[11,16,128]{2,1,0:T(8,128)S(1)}, f32[11,16,128]{2,1,0:T(8,128)S(1)}, u32[]{:S(2)}, u32[]{:S(2)}) %collective-permute-start.4) | collective-permute-done | bytes 90144 | tf_op jit(solution)/shard_map/ppermute | solution.py:776
  19.2 3.4 %collective-permute-done.3.two_ref = f32[11,16,128]{2,1,0:T(8,128)S(1)} collective-permute-done((f32[11,16,128]{2,1,0:T(8,128)S(1)}, f32[11,16,128]{2,1,0:T(8,128)S(1)}, u32[]{:S(2)}, u32[]{:S(2)}) %collective-permute-start.3) | collective-permute-done | bytes 90144 | tf_op jit(solution)/shard_map/ppermute | solution.py:776
  22.6 3.0 %shard_map.65 = (f32[16,24,384]{2,1,0:T(8,128)S(1)}, f32[24,384]{1,0:T(8,128)S(1)}, f32[19,16,128]{2,1,0:T(8,128)S(1)}) custom-call(s32[2]{0:T(128)S(1)} %copy-done.4, s32[2]{0:T(128)S(1)} %copy-done.5, f32[16,24,384]{2,1,0:T(8,128)S(1)} %copy-done.3, f32[16,24,384]{2,1,0:T(8,128)S(1)} %copy-done.2, f32[16,24,384]{2,1,0:T(8,128)S(1)} %copy-done, ...), custom_call_target="tpu_custom_call" | custom-call | tf_op jit(solution)/shard_map/pallas_call | solution.py:751
  25.7 0.1 collective-permute-start.5
  25.8 1.2 %collective-permute-done.5.level_ref = f32[24,384]{1,0:T(8,128)S(1)} collective-permute-done((f32[24,384]{1,0:T(8,128)S(1)}, f32[24,384]{1,0:T(8,128)S(1)}, u32[]{:S(2)}, u32[]{:S(2)}) %collective-permute-start.5) | collective-permute-done | bytes 36896 | tf_op jit(solution)/shard_map/ppermute | solution.py:797
  27.0 3.4 %collective-permute-start.8 = (f32[19,16,128]{2,1,0:T(8,128)S(1)}, f32[19,16,128]{2,1,0:T(8,128)S(1)}, u32[]{:S(2)}, u32[]{:S(2)}) collective-permute-start(f32[19,16,128]{2,1,0:T(8,128)S(1)} %shard_map.66), channel_id=1, source_target_pairs={{0,12},{4,8},{8,4},{12,0},{1,13},{5,9},{9,5},{13,1},{2,14},{6,10},... | collective-permute-start | bytes 466952 | tf_op jit(solution)/shard_map/ppermute | solution.py:776
  30.4 1.0 %collective-permute-start.6 = (f32[19,16,128]{2,1,0:T(8,128)S(1)}, f32[19,16,128]{2,1,0:T(8,128)S(1)}, u32[]{:S(2)}, u32[]{:S(2)}) collective-permute-start(f32[19,16,128]{2,1,0:T(8,128)S(1)} %shard_map.66), channel_id=1, source_target_pairs={{0,4},{4,0},{8,12},{12,8},{1,5},{5,1},{9,13},{13,9},{2,6},{6,2},{1... | collective-permute-start | bytes 466952 | tf_op jit(solution)/shard_map/ppermute | solution.py:776
  31.4 4.4 %collective-permute-done.8.three_ref = f32[19,16,128]{2,1,0:T(8,128)S(1)} collective-permute-done((f32[19,16,128]{2,1,0:T(8,128)S(1)}, f32[19,16,128]{2,1,0:T(8,128)S(1)}, u32[]{:S(2)}, u32[]{:S(2)}) %collective-permute-start.8) | collective-permute-done | bytes 155680 | tf_op jit(solution)/shard_map/ppermute | solution.py:776
  35.8 6.3 %collective-permute-done.7.two_ref = f32[19,16,128]{2,1,0:T(8,128)S(1)} collective-permute-done((f32[19,16,128]{2,1,0:T(8,128)S(1)}, f32[19,16,128]{2,1,0:T(8,128)S(1)}, u32[]{:S(2)}, u32[]{:S(2)}) %collective-permute-start.7) | collective-permute-done | bytes 155680 | tf_op jit(solution)/shard_map/ppermute | solution.py:776
  42.2 0.4 shard_map.67
  42.6 1.5 %collective-permute-start.9 = (f32[17,16,128]{2,1,0:T(8,128)S(1)}, f32[17,16,128]{2,1,0:T(8,128)S(1)}, u32[]{:S(2)}, u32[]{:S(2)}) collective-permute-start(f32[17,16,128]{2,1,0:T(8,128)S(1)} %shard_map.67), channel_id=1, source_target_pairs={{0,2},{2,0},{1,3},{3,1},{4,6},{6,4},{5,7},{7,5},{8,10},{10,8},{9,1... | collective-permute-start | bytes 417800 | tf_op jit(solution)/shard_map/ppermute | solution.py:812
  44.1 3.8 %collective-permute-done.9.rows_ref = f32[17,16,128]{2,1,0:T(8,128)S(1)} collective-permute-done((f32[17,16,128]{2,1,0:T(8,128)S(1)}, f32[17,16,128]{2,1,0:T(8,128)S(1)}, u32[]{:S(2)}, u32[]{:S(2)}) %collective-permute-start.9) | collective-permute-done | bytes 139296 | tf_op jit(solution)/shard_map/ppermute | solution.py:812
  47.9 4.5 %shard_map.68 = f32[16,24,384]{2,1,0:T(8,128)} custom-call(s32[2]{0:T(128)S(1)} %copy-done.4, s32[2]{0:T(128)S(1)} %copy-done.5, f32[16]{0:T(128)S(1)} %copy-done.6, f32[16,24,384]{2,1,0:T(8,128)S(1)} %get-tuple-element.14.field_ref, f32[16,24,384]{2,1,0:T(8,128)S(1)} %copy-done.2, f32[16,24,384]{2,1,0:T(8,128)S(1)} %copy-done.1, ...), custom_call_target="tpu_custom_call" | custom-call | tf_op jit(solution)/shard_map/pallas_call | solution.py:751
  (16 shorter events, 0.1 us)
Async XLA Ops:
  0.0 1.1 %copy-start = (f32[16,24,384]{2,1,0:T(8,128)S(1)}, f32[16,24,384]{2,1,0:T(8,128)}, u32[]{:S(2)}) copy-start(f32[16,24,384]{2,1,0:T(8,128)} %north_ref.7) | copy-start | bytes 1769476
  1.1 1.1 %copy-start.3 = (f32[16,24,384]{2,1,0:T(8,128)S(1)}, f32[16,24,384]{2,1,0:T(8,128)}, u32[]{:S(2)}) copy-start(f32[16,24,384]{2,1,0:T(8,128)} %air_ref.3) | copy-start | bytes 1769476
  2.1 0.7 %copy-start.4 = (s32[2]{0:T(128)S(1)}, s32[2]{0:T(128)}, u32[]{:S(2)}) copy-start(s32[2]{0:T(128)} %west_ref.5) | copy-start | bytes 28
  2.8 0.7 %copy-start.5 = (s32[2]{0:T(128)S(1)}, s32[2]{0:T(128)}, u32[]{:S(2)}) copy-start(s32[2]{0:T(128)} %south_ref.5) | copy-start | bytes 28
  3.4 19.2 %copy-start.2 = (f32[16,24,384]{2,1,0:T(8,128)S(1)}, f32[16,24,384]{2,1,0:T(8,128)}, u32[]{:S(2)}) copy-start(f32[16,24,384]{2,1,0:T(8,128)} %east_ref.5) | copy-start | bytes 1769476
  5.8 6.1 %collective-permute-start = (f32[14,16,128]{2,1,0:T(8,128)S(1)}, f32[14,16,128]{2,1,0:T(8,128)S(1)}, u32[]{:S(2)}, u32[]{:S(2)}) collective-permute-start(f32[14,16,128]{2,1,0:T(8,128)S(1)} %get-tuple-element.11), channel_id=1, source_target_pairs={{0,2},{2,0},{1,3},{3,1},{4,6},{6,4},{5,7},{7,5},{8,10},{10,8},{9,1... | collective-permute-start | bytes 344072 | tf_op jit(solution)/shard_map/ppermute | solution.py:786
  11.9 7.3 %collective-permute-start.4 = (f32[11,16,128]{2,1,0:T(8,128)S(1)}, f32[11,16,128]{2,1,0:T(8,128)S(1)}, u32[]{:S(2)}, u32[]{:S(2)}) collective-permute-start(f32[11,16,128]{2,1,0:T(8,128)S(1)} %slice_add_fusion), channel_id=1, source_target_pairs={{0,12},{4,8},{8,4},{12,0},{1,13},{5,9},{9,5},{13,1},{2,14},{6,10},... | collective-permute-start | bytes 270344 | tf_op jit(solution)/shard_map/ppermute | solution.py:776
  14.7 7.9 %collective-permute-start.3 = (f32[11,16,128]{2,1,0:T(8,128)S(1)}, f32[11,16,128]{2,1,0:T(8,128)S(1)}, u32[]{:S(2)}, u32[]{:S(2)}) collective-permute-start(f32[11,16,128]{2,1,0:T(8,128)S(1)} %slice_add_fusion), channel_id=1, source_target_pairs={{0,8},{4,12},{8,0},{12,4},{1,9},{5,13},{9,1},{13,5},{2,10},{6,14},... | collective-permute-start | bytes 270344 | tf_op jit(solution)/shard_map/ppermute | solution.py:776
  15.3 7.3 %collective-permute-start.2 = (f32[11,16,128]{2,1,0:T(8,128)S(1)}, f32[11,16,128]{2,1,0:T(8,128)S(1)}, u32[]{:S(2)}, u32[]{:S(2)}) collective-permute-start(f32[11,16,128]{2,1,0:T(8,128)S(1)} %slice_add_fusion), channel_id=1, source_target_pairs={{0,4},{4,0},{8,12},{12,8},{1,5},{5,1},{9,13},{13,9},{2,6},{6,2},{1... | collective-permute-start | bytes 270344 | tf_op jit(solution)/shard_map/ppermute | solution.py:776
  16.4 10.6 %copy-start.1 = (f32[16,24,384]{2,1,0:T(8,128)S(1)}, f32[16,24,384]{2,1,0:T(8,128)}, u32[]{:S(2)}) copy-start(f32[16,24,384]{2,1,0:T(8,128)} %north_ref.7) | copy-start | bytes 1769476
  16.4 1.2 %collective-permute-start.1 = (f32[24,384]{1,0:T(8,128)S(1)}, f32[24,384]{1,0:T(8,128)S(1)}, u32[]{:S(2)}, u32[]{:S(2)}) collective-permute-start(f32[24,384]{1,0:T(8,128)S(1)} %get-tuple-element.12), channel_id=1, source_target_pairs={{0,1},{1,0},{2,3},{3,2},{4,5},{5,4},{6,7},{7,6},{8,9},{9,8},{10,11... | collective-permute-start | bytes 110600 | tf_op jit(solution)/shard_map/ppermute | solution.py:787
  25.7 1.3 %collective-permute-start.5 = (f32[24,384]{1,0:T(8,128)S(1)}, f32[24,384]{1,0:T(8,128)S(1)}, u32[]{:S(2)}, u32[]{:S(2)}) collective-permute-start(f32[24,384]{1,0:T(8,128)S(1)} %get-tuple-element.15), channel_id=1, source_target_pairs={{0,1},{1,0},{2,3},{3,2},{4,5},{5,4},{6,7},{7,6},{8,9},{9,8},{10,11... | collective-permute-start | bytes 110600 | tf_op jit(solution)/shard_map/ppermute | solution.py:797
  27.0 20.9 %copy-start.6 = (f32[16]{0:T(128)S(1)}, f32[16]{0:T(128)}, u32[]{:S(2)}) copy-start(f32[16]{0:T(128)} %weight_ref.1) | copy-start | bytes 196
  27.0 8.8 %collective-permute-start.8 = (f32[19,16,128]{2,1,0:T(8,128)S(1)}, f32[19,16,128]{2,1,0:T(8,128)S(1)}, u32[]{:S(2)}, u32[]{:S(2)}) collective-permute-start(f32[19,16,128]{2,1,0:T(8,128)S(1)} %shard_map.66), channel_id=1, source_target_pairs={{0,12},{4,8},{8,4},{12,0},{1,13},{5,9},{9,5},{13,1},{2,14},{6,10},... | collective-permute-start | bytes 466952 | tf_op jit(solution)/shard_map/ppermute | solution.py:776
  30.4 11.8 %collective-permute-start.7 = (f32[19,16,128]{2,1,0:T(8,128)S(1)}, f32[19,16,128]{2,1,0:T(8,128)S(1)}, u32[]{:S(2)}, u32[]{:S(2)}) collective-permute-start(f32[19,16,128]{2,1,0:T(8,128)S(1)} %shard_map.66), channel_id=1, source_target_pairs={{0,8},{4,12},{8,0},{12,4},{1,9},{5,13},{9,1},{13,5},{2,10},{6,14},... | collective-permute-start | bytes 466952 | tf_op jit(solution)/shard_map/ppermute | solution.py:776
  30.4 11.8 %collective-permute-start.6 = (f32[19,16,128]{2,1,0:T(8,128)S(1)}, f32[19,16,128]{2,1,0:T(8,128)S(1)}, u32[]{:S(2)}, u32[]{:S(2)}) collective-permute-start(f32[19,16,128]{2,1,0:T(8,128)S(1)} %shard_map.66), channel_id=1, source_target_pairs={{0,4},{4,0},{8,12},{12,8},{1,5},{5,1},{9,13},{13,9},{2,6},{6,2},{1... | collective-permute-start | bytes 466952 | tf_op jit(solution)/shard_map/ppermute | solution.py:776
  42.6 5.3 %collective-permute-start.9 = (f32[17,16,128]{2,1,0:T(8,128)S(1)}, f32[17,16,128]{2,1,0:T(8,128)S(1)}, u32[]{:S(2)}, u32[]{:S(2)}) collective-permute-start(f32[17,16,128]{2,1,0:T(8,128)S(1)} %shard_map.67), channel_id=1, source_target_pairs={{0,2},{2,0},{1,3},{3,1},{4,6},{6,4},{5,7},{7,5},{8,10},{10,8},{9,1... | collective-permute-start | bytes 417800 | tf_op jit(solution)/shard_map/ppermute | solution.py:812

commit v2 on v0

--- a/solution.py
+++ b/solution.py
@@ -1,6 +1,11 @@
+import functools
+import math
+
 import jax
 import jax.numpy as jnp
 from jax import lax
+from jax.experimental import pallas as pl
+from jax.experimental.pallas import tpu as pltpu
 from jax.sharding import PartitionSpec as P
 
 VERTICAL_MIX = 0.1
@@ -167,6 +172,719 @@
     return jnp.where(covered, blended, step_two)
 
 
+LANES = 128
+FIRST_LANE = 32
+LAST_LANE = 96
+EAST_LANE = 64
+
+
+def iota(shape, dim):
+    return lax.broadcasted_iota(jnp.int32, shape, dim)
+
+
+def split_level(place, height):
+    level = ((place.astype(jnp.float32) + 0.5) * (1.0 / height)).astype(jnp.int32)
+    return level, place - level * height
+
+
+def table(values):
+    return values.astype(jnp.float32).astype(jnp.bfloat16)
+
+
+def parts_of(array):
+    high = array.astype(jnp.bfloat16)
+    low = (array - high.astype(jnp.float32)).astype(jnp.bfloat16)
+    return high, low
+
+
+def dot(left, right):
+    return jnp.dot(left, right, preferred_element_type=jnp.float32)
+
+
+def from_left(weights, array):
+    high, low = parts_of(array)
+    return dot(weights, high) + dot(weights, low)
+
+
+def from_right(array, weights):
+    high, low = parts_of(array)
+    return dot(high, weights) + dot(low, weights)
+
+
+def hat(distance):
+    return jnp.maximum(0, 3 - jnp.abs(distance - 1))
+
+
+def place():
+    return lax.axis_index("tiles"), lax.axis_index("rows"), lax.axis_index("lev")
+
+
+def level_table(levels, height):
+    shape = (levels, levels * height)
+    level, _ = split_level(iota(shape, 1), height)
+    return table(iota(shape, 0) == level)
+
+
+def spread_table(levels, height):
+    shape = (levels * height, levels)
+    level, _ = split_level(iota(shape, 0), height)
+    return table(iota(shape, 1) == level)
+
+
+def load_line(ref, levels, line):
+    rows = pl.ds(line, levels, stride=ref.shape[1] // levels)
+    return jnp.concatenate([ref[c, rows, :] for c in range(ref.shape[0])], axis=1)
+
+
+def store_line(ref, levels, line, value):
+    rows = pl.ds(line, levels, stride=ref.shape[1] // levels)
+    for c in range(ref.shape[0]):
+        ref[c, rows, :] = value[:, c * LANES : (c + 1) * LANES]
+
+
+def load_level(ref, height, l):
+    rows = pl.ds(l * height, height)
+    if len(ref.shape) == 2:
+        return ref[rows, :]
+    return jnp.concatenate([ref[c, rows, :] for c in range(ref.shape[0])], axis=1)
+
+
+def store_level(ref, height, l, value):
+    rows = pl.ds(l * height, height)
+    if len(ref.shape) == 2:
+        ref[rows, :] = value
+    else:
+        for c in range(ref.shape[0]):
+            ref[c, rows, :] = value[:, c * LANES : (c + 1) * LANES]
+
+
+def store_slabs(ref, first, wide):
+    for i in range(wide.shape[1] // LANES):
+        ref[first + i] = wide[:, i * LANES : (i + 1) * LANES]
+
+
+def join_slabs(ref, first, count):
+    return jnp.concatenate([ref[first + i] for i in range(count)], axis=1)
+
+
+def pack_window(ref, field_ref, levels, top, start):
+    height = field_ref.shape[1] // levels
+    breadth = field_ref.shape[0] * LANES
+    slots = ref.shape[0] - 1
+    lane = iota((levels, breadth), 1)
+    column = jnp.where(lane == breadth - 1, start - 1, start + lane)
+    inside = (column >= 0) & (column < breadth)
+    turn = lax.rem(4 * breadth - start, breadth)
+    lane = iota((levels, LANES), 1)
+    extra = jnp.zeros((levels, LANES), jnp.float32)
+    for slot in range(slots):
+        line = top + slot
+        there = (line >= 0) & (line < height)
+        rows = load_line(field_ref, levels, jnp.clip(line, 0, height - 1))
+        rows = jnp.where(inside & there, pltpu.roll(rows, turn, 1), 0.0)
+        ref[slot] = rows[:, :LANES]
+        east = rows[:, LANES : 2 * LANES]
+        west = rows[:, breadth - LANES :]
+        extra = jnp.where(lane == slot, pltpu.roll(west, slot + 1, 1), extra)
+        extra = jnp.where(lane == EAST_LANE + slot, pltpu.roll(east, EAST_LANE + slot, 1), extra)
+    ref[slots] = extra
+
+
+def pack_edges(field_ref, levels):
+    height = field_ref.shape[1] // levels
+    lane = iota((levels, LANES), 1)
+    packed = jnp.zeros((levels, LANES), jnp.float32)
+    for line in range(height):
+        rows = pl.ds(line, levels, stride=height)
+        first = field_ref[0, rows, :]
+        last = field_ref[field_ref.shape[0] - 1, rows, :]
+        packed = jnp.where(lane == FIRST_LANE + line, pltpu.roll(first, FIRST_LANE + line, 1), packed)
+        packed = jnp.where(lane == LAST_LANE + line, pltpu.roll(last, LAST_LANE + line + 1, 1), packed)
+    return packed
+
+
+def neighbour_columns(even, odd, parent_tiles, tile):
+    is_odd = tile % 2 == 1
+    west = jnp.where(is_odd, even, odd)
+    east = jnp.where(is_odd, odd, even)
+    west = jnp.where(tile == 0, jnp.zeros_like(west), west)
+    east = jnp.where(tile >= parent_tiles - 1, jnp.zeros_like(east), east)
+    return jnp.where(iota(west.shape, 1) < LAST_LANE, east, west)
+
+
+def unpack_edges(columns, levels, height):
+    wide = from_left(spread_table(levels, height), columns)
+    lane = iota(wide.shape, 1)
+    _, line = split_level(iota(wide.shape, 0), height)
+    west = jnp.sum(jnp.where(lane == line + LAST_LANE, wide, 0.0), axis=1, keepdims=True)
+    east = jnp.sum(jnp.where(lane == line + FIRST_LANE, wide, 0.0), axis=1, keepdims=True)
+    return jnp.where(lane == 0, west, jnp.where(lane == 1, east, 0.0))
+
+
+def refine(slabs, extra, height, breadth, row):
+    slots, levels = len(slabs), extra.shape[0]
+    beside = [pltpu.roll(extra, LANES - s, 1) if s else extra for s in range(slots)]
+    window = jnp.concatenate([jnp.concatenate(slabs, axis=0), jnp.concatenate(beside, axis=0)], axis=1)
+    shape = (2 * LANES, breadth + LANES)
+    slot, cell = iota(shape, 0), iota(shape, 1)
+    held = (slot <= LANES) | (slot == LANES + EAST_LANE)
+    at = jnp.where(slot < LANES, slot, jnp.where(slot == LANES, -1, LANES))
+    cell = jnp.where(cell == breadth, -1, jnp.where(cell == breadth + 1, breadth, cell))
+    across = jnp.where(held & (cell <= breadth), hat(cell - 3 * at), 0)
+    wide = from_right(window, table(across)) * (1.0 / 9.0)
+    shape = (levels * height, slots * levels)
+    taken = iota(shape, 1)
+    slot = taken // levels
+    level, line = split_level(iota(shape, 0), height)
+    along = jnp.where(taken - slot * levels == level, hat(line - 3 * (slot - 1)), 0)
+    cells = from_left(table(along), wide)
+    ring = jnp.where(
+        row == 0,
+        2.0 * wide[:levels] + wide[levels : 2 * levels],
+        2.0 * wide[(slots - 1) * levels :] + wide[(slots - 2) * levels : (slots - 1) * levels],
+    )
+    return cells, ring[:, :breadth]
+
+
+def beside_rows(x, north, south):
+    height = x.shape[0]
+    line = iota(x.shape, 0)
+    northern = jnp.where(line == 0, north, pltpu.roll(x, 1, 0))
+    southern = jnp.where(line == height - 1, south, pltpu.roll(x, height - 1, 0))
+    return northern, southern
+
+
+def beside_columns(x, west, east):
+    breadth = x.shape[1]
+    column = iota(x.shape, 1)
+    western = jnp.where(column == 0, west, pltpu.roll(x, 1, 1))
+    eastern = jnp.where(column == breadth - 1, east, pltpu.roll(x, breadth - 1, 1))
+    return western, eastern
+
+
+def change_of(x, sides, u, v, upper, lower, nest):
+    advect_scale = NEST_ADVECT if nest else 1.0
+    mixing_scale = NEST_MIXING if nest else PARENT_MIXING
+    northern, southern, western, eastern = sides
+    advect = u * (eastern - western) + v * (southern - northern)
+    horizontal = eastern + western + southern + northern - 4.0 * x
+    vertical = upper + lower - 2.0 * x
+    return -0.5 * advect_scale * advect + mixing_scale * horizontal + VERTICAL_MIX * vertical
+
+
+def ghost_weight(speed, before):
+    return jnp.where(before, 0.5 * NEST_ADVECT, -0.5 * NEST_ADVECT) * speed + NEST_MIXING
+
+
+def full_step(out_ref, field_ref, u_ref, v_ref, level_ref, levels, lev, nest, north, south, side, fine):
+    height, breadth = level_ref.shape
+    zero = jnp.zeros((height, breadth), jnp.float32)
+
+    def block(ref, l):
+        return load_level(ref, height, l)
+
+    for l in range(levels):
+        x = block(field_ref, l)
+        lower = block(field_ref, l - 1) if l else jnp.where(lev == 1, level_ref[...], zero)
+        upper = block(field_ref, l + 1) if l < levels - 1 else jnp.where(lev == 0, level_ref[...], zero)
+        rows = [0.0 if ref is None else ref[pl.ds(l, 1), :] for ref in (north, south)]
+        if side is None:
+            columns = (0.0, 0.0)
+        else:
+            beside = side[pl.ds(l * height, height), :]
+            columns = (beside[:, 0:1], beside[:, 1:2])
+        sides = beside_rows(x, *rows) + beside_columns(x, *columns)
+        fresh = x + change_of(x, sides, block(u_ref, l), block(v_ref, l), upper, lower, nest)
+        if nest:
+            fresh = fresh - NUDGING * x if fine is None else fresh + NUDGING * (block(fine, l) - x)
+        store_level(out_ref, height, l, fresh)
+
+
+def inner_line(height, row):
+    return jnp.where(row == 0, height - 1, 0)
+
+
+def edge_level(ref, height, lev):
+    last = ref.shape[1] // height - 1
+    return jnp.where(lev == 0, load_level(ref, height, last), load_level(ref, height, 0))
+
+
+def pack_kernel(
+    levels,
+    west_hbm,
+    south_hbm,
+    air_hbm,
+    north_hbm,
+    rows_ref,
+    own_ref,
+    edges_ref,
+    level_ref,
+    west_ref,
+    south_ref,
+    air_ref,
+    north_ref,
+    sems,
+):
+    pieces, size, _ = air_ref.shape
+    height, breadth = level_ref.shape
+    third_y = height // 3
+    slots = own_ref.shape[0] - 1
+    tile, row, lev = place()
+    nest = tile == lax.axis_size("tiles") - 1
+
+    def column_copies(source, target, first):
+        return [
+            pltpu.make_async_copy(source.at[:, pl.ds(c * LANES, LANES)], target.at[c], sems.at[first + c])
+            for c in range(pieces)
+        ]
+
+    copies = column_copies(air_hbm, air_ref, 0)
+    copies.append(pltpu.make_async_copy(west_hbm, west_ref, sems.at[2 * pieces]))
+    copies.append(pltpu.make_async_copy(south_hbm, south_ref, sems.at[2 * pieces + 1]))
+    speeds = column_copies(north_hbm, north_ref, pieces)
+    for copy in copies + speeds:
+        copy.start()
+    for copy in copies + speeds:
+        copy.wait()
+    inner = inner_line(height, row)
+    level_ref[...] = edge_level(air_ref, height, lev)
+    store_slabs(rows_ref, slots + 1, load_line(air_ref, levels, inner))
+
+    @pl.when(nest)
+    def _():
+        speed = load_line(north_ref, levels, inner)
+        store_slabs(rows_ref, 0, speed)
+        for i in range(pieces, slots + 1):
+            rows_ref[i] = jnp.zeros((levels, LANES), jnp.float32)
+        store_slabs(own_ref, 0, load_line(north_ref, levels, height - 1 - inner))
+        store_slabs(own_ref, pieces, speed)
+        edges_ref[...] = jnp.zeros_like(edges_ref)
+
+    @pl.when(jnp.logical_not(nest))
+    def _():
+        start = west_ref[0] - tile * breadth
+        top = south_ref[0] - 1 - row * height
+        part = rows_ref.at[pl.ds(0, slots + 1)]
+        pack_window(part, air_ref, levels, top + (1 - row) * third_y, start)
+        pack_window(own_ref, air_ref, levels, top + row * third_y, start)
+        edges_ref[...] = pack_edges(air_ref, levels)
+
+
+def early_kernel(
+    levels,
+    west_ref,
+    south_ref,
+    air_ref,
+    east_ref,
+    north_ref,
+    rows_ref,
+    level_ref,
+    even_ref,
+    odd_ref,
+    speeds_ref,
+    field_ref,
+    own_ref,
+    other_ref,
+    coef_ref,
+    side_ref,
+    northern_ref,
+    southern_ref,
+):
+    size, breadth = air_ref.shape
+    height = size // levels
+    third_y = height // 3
+    pieces = breadth // LANES
+    slots = own_ref.shape[0] - 1
+    tile_count = lax.axis_size("tiles")
+    tile, row, lev = place()
+    nest = tile == tile_count - 1
+    halo = join_slabs(rows_ref, slots + 1, pieces)
+    zero = jnp.zeros_like(halo)
+    northern_ref[...] = jnp.where(row == 0, zero, halo)
+    southern_ref[...] = jnp.where(row == 0, halo, zero)
+    shared = (field_ref, air_ref, east_ref, north_ref, level_ref, levels, lev)
+
+    @pl.when(nest)
+    def _():
+        full_step(*shared, True, northern_ref, southern_ref, None, None)
+        ghost = ghost_weight(join_slabs(speeds_ref, 0, pieces), row == 0)
+        cell, third = iota((breadth, 3 * LANES), 0), iota((breadth, 3 * LANES), 1)
+        kind = third // LANES
+        offset = cell - 3 * (third - kind * LANES)
+        middle = jnp.where(offset == 1, 3, jnp.where((offset == 0) | (offset == 2), 2, 0))
+        weight = jnp.where(kind == 1, middle, jnp.where(offset == kind, 1, 0))
+        store_slabs(coef_ref, 0, from_right(ghost, table(weight)) * (1.0 / 27.0))
+        shape = (size, LANES)
+        lane = iota(shape, 1)
+        _, line = split_level(iota(shape, 0), height)
+        block = lane // 8
+        inside = lane - block * 8
+        eastern = inside >= 3
+        kind = jnp.where(eastern, inside - 3, inside)
+        offset = line - 3 * block
+        middle = jnp.where(offset == 1, 3, jnp.where((offset == 0) | (offset == 2), 2, 0))
+        weight = jnp.where(kind == 1, middle, jnp.where(offset == kind, 1, 0))
+        weight = jnp.where((inside < 6) & (block < third_y), weight, 0).astype(jnp.float32)
+        first = ghost_weight(east_ref[:, 0:1], True)
+        last = ghost_weight(east_ref[:, breadth - 1 : breadth], False)
+        columns = jnp.where(eastern, last, first) * weight
+        coef_ref[3] = from_left(level_table(levels, height), columns) * (1.0 / 27.0)
+        own_ref[...] = jnp.zeros_like(own_ref)
+        other_ref[...] = jnp.zeros_like(other_ref)
+
+    @pl.when(jnp.logical_not(nest))
+    def _():
+        columns = neighbour_columns(even_ref[...], odd_ref[...], tile_count - 1, tile)
+        side_ref[...] = unpack_edges(columns, levels, height)
+        full_step(*shared, False, northern_ref, southern_ref, side_ref, None)
+        start = west_ref[1] - tile * breadth
+        top = south_ref[1] - 1 - row * height
+        pack_window(other_ref, field_ref, levels, top + (1 - row) * third_y, start)
+        pack_window(own_ref, field_ref, levels, top + row * third_y, start)
+        coef_ref[...] = jnp.zeros_like(coef_ref)
+
+
+def first_kernel(
+    levels, early_ref, east_ref, speeds_ref, one_ref, two_ref, three_ref, own_ref, other_ref, field_ref, edge_ref, window_ref
+):
+    pieces, size, _ = early_ref.shape
+    height, breadth = edge_ref.shape
+    slots = own_ref.shape[0] - 1
+    tile, row, lev = place()
+    nest = tile == lax.axis_size("tiles") - 1
+
+    @pl.when(jnp.logical_not(nest))
+    def _():
+        window_ref[...] = own_ref[...] + other_ref[...]
+        edge_ref[...] = jnp.zeros_like(edge_ref)
+
+    @pl.when(nest)
+    def _():
+        slabs = [one_ref[s] + two_ref[s] + three_ref[s] for s in range(slots + 1)]
+        cells, ring = refine(slabs[:slots], slabs[slots], height, breadth, row)
+        lane = iota((size, LANES), 1)
+        for c in range(pieces):
+            piece = slice(c * LANES, (c + 1) * LANES)
+            value = early_ref[c] + NUDGING * cells[:, piece]
+            if c == 0:
+                ghost = ghost_weight(east_ref[:, piece], True) * cells[:, breadth : breadth + 1]
+                value = value + jnp.where(lane == 0, ghost, 0.0)
+            if c == pieces - 1:
+                ghost = ghost_weight(east_ref[:, piece], False) * cells[:, breadth + 1 : breadth + 2]
+                value = value + jnp.where(lane == LANES - 1, ghost, 0.0)
+            field_ref[c] = value
+        outer = height - 1 - inner_line(height, row)
+        ghost = ghost_weight(join_slabs(speeds_ref, 0, pieces), row == 0) * ring
+        store_line(field_ref, levels, outer, load_line(field_ref, levels, outer) + ghost)
+        edge_ref[...] = edge_level(field_ref, height, lev)
+
+
+def average_kernel(
+    levels, field_ref, east_ref, north_ref, rows_ref, level_ref, coef_ref, window_ref, message_ref, part_ref
+):
+    pieces, size, _ = field_ref.shape
+    height, breadth = level_ref.shape
+    third_y = height // 3
+    tile, row, lev = place()
+    nest = tile == lax.axis_size("tiles") - 1
+
+    @pl.when(jnp.logical_not(nest))
+    def _():
+        slots = window_ref.shape[0]
+        message_ref[pl.ds(0, slots)] = window_ref[...]
+        for i in range(slots, message_ref.shape[0]):
+            message_ref[i] = jnp.zeros((levels, LANES), jnp.float32)
+
+    @pl.when(nest)
+    def _():
+        full_step(part_ref, field_ref, east_ref, north_ref, level_ref, levels, lev, True, None, None, None, None)
+        cell, third = iota((breadth, LANES), 0), iota((breadth, LANES), 1)
+        offset = cell - 3 * third
+        sums = table((offset >= 0) & (offset <= 2))
+        shape = (third_y * levels, size)
+        taken = iota(shape, 0)
+        block = taken // levels
+        level, line = split_level(iota(shape, 1), height)
+        offset = line - 3 * block
+        rows = table((taken - block * levels == level) & (offset >= 0) & (offset <= 2))
+        means = from_left(rows, from_right(part_ref[...], sums)) * (1.0 / 9.0)
+        for m in range(third_y):
+            message_ref[m] = means[m * levels : (m + 1) * levels]
+        message_ref[pl.ds(third_y, 4)] = coef_ref[...]
+        shared = load_line(field_ref, levels, inner_line(height, row))
+        shared = ghost_weight(join_slabs(rows_ref, 0, pieces), row == 0) * shared
+        message_ref[third_y + 4] = from_right(shared, sums) * (1.0 / 9.0)
+
+
+def blend_kernel(levels, weight_ref, field_ref, window_ref, one_ref, two_ref, three_ref, rows_ref):
+    pieces, size, _ = field_ref.shape
+    height = size // levels
+    third_y = height // 3
+    slots = third_y + 2
+    tile_count = lax.axis_size("tiles")
+    tile, row, _ = place()
+    nest = tile == tile_count - 1
+
+    @pl.when(nest)
+    def _():
+        store_slabs(rows_ref, 0, load_line(field_ref, levels, inner_line(height, row)))
+        for i in range(pieces, rows_ref.shape[0]):
+            rows_ref[i] = jnp.zeros((levels, LANES), jnp.float32)
+
+    @pl.when(jnp.logical_not(nest))
+    def _():
+        def mine(i):
+            return jnp.where(tile == 0, three_ref[i], jnp.where(tile == 1, two_ref[i], one_ref[i]))
+
+        def whole(i):
+            odd = tile % 2 == 1
+            west = jnp.where(odd, one_ref[i], three_ref[i])
+            east = jnp.where(odd, three_ref[i], one_ref[i])
+            part = jnp.where(tile == 0, window_ref[i], window_ref[i] + west)
+            return jnp.where(tile == tile_count - 2, part, part + east)
+
+        weight = weight_ref[:, 0:1]
+        extra = whole(slots)
+        lane = iota(extra.shape, 1)
+        at_first, at_last = lane == 0, lane == LANES - 1
+        lines = []
+        for s in range(slots):
+            x = whole(s)
+            west = jnp.where(at_first, extra[:, s : s + 1], pltpu.roll(x, 1, 1))
+            last = EAST_LANE + s
+            east = jnp.where(at_last, extra[:, last : last + 1], pltpu.roll(x, LANES - 1, 1))
+            lines.append((west, x, east))
+        edges = mine(third_y + 3)
+        ghosts = [mine(third_y + q) for q in range(3)]
+
+        def outward(side, q):
+            near = lines[1] if side == 0 else lines[slots - 2]
+            far = lines[0] if side == 0 else lines[slots - 1]
+            return (2.0 / 3.0) * far[q] + (1.0 / 3.0) * near[q]
+
+        def sideward(s):
+            west, x, east = lines[s]
+            return (2.0 / 3.0) * jnp.where(at_first, west, east) + (1.0 / 3.0) * x
+
+        sidewards = [sideward(s) for s in range(slots)]
+        columns = [w + 7.0 * x + e for w, x, e in lines]
+        for m in range(third_y):
+            x = lines[m + 1][1]
+            value = mine(m) + (NUDGING / 81.0) * (columns[m] + 7.0 * columns[m + 1] + columns[m + 2])
+            for q in range(3):
+                lane_of = 8 * m + q
+                first, last = edges[:, lane_of : lane_of + 1], edges[:, lane_of + 3 : lane_of + 4]
+                scale = jnp.where(at_first, first, jnp.where(at_last, last, 0.0))
+                value = value + scale * sidewards[m + q]
+            for side, at in ((0, 0), (1, third_y - 1)):
+                if m == at:
+                    for q in range(3):
+                        value = value + jnp.where(row == side, ghosts[q], 0.0) * outward(side, q)
+            rows_ref[m] = x + weight * (value - x)
+        rows_ref[third_y] = weight * mine(third_y + 4)
+
+
+def later_kernel(
+    levels,
+    field_ref,
+    east_ref,
+    north_ref,
+    level_ref,
+    one_ref,
+    two_ref,
+    three_ref,
+    out_ref,
+    fine_ref,
+    side_ref,
+    northern_ref,
+    southern_ref,
+):
+    height, breadth = level_ref.shape
+    slots = height // 3 + 2
+    tile, row, lev = place()
+
+    @pl.when(tile == lax.axis_size("tiles") - 1)
+    def _():
+        slabs = [one_ref[s] + two_ref[s] + three_ref[s] for s in range(slots + 1)]
+        cells, ring = refine(slabs[:slots], slabs[slots], height, breadth, row)
+        fine_ref[...] = cells[:, :breadth]
+        side_ref[...] = cells[:, breadth:]
+        zero = jnp.zeros_like(ring)
+        northern_ref[...] = jnp.where(row == 0, ring, zero)
+        southern_ref[...] = jnp.where(row == 0, zero, ring)
+        full_step(
+            out_ref,
+            field_ref,
+            east_ref,
+            north_ref,
+            level_ref,
+            levels,
+            lev,
+            True,
+            northern_ref,
+            southern_ref,
+            side_ref,
+            fine_ref,
+        )
+
+
+def last_kernel(
+    levels, west_ref, south_ref, parent_ref, nested_ref, speeds_ref, blend_ref, rows_ref, out_hbm, out_ref, sems
+):
+    pieces, size, _ = parent_ref.shape
+    breadth = pieces * LANES
+    height = size // levels
+    third_y = height // 3
+    tile, row, _ = place()
+    nest = tile == lax.axis_size("tiles") - 1
+
+    @pl.when(nest)
+    def _():
+        out_ref[...] = nested_ref[...]
+        inner = inner_line(height, row)
+        halo = ghost_weight(join_slabs(speeds_ref, pieces, pieces), row == 1) * join_slabs(rows_ref, 0, pieces)
+        store_line(out_ref, levels, inner, load_line(out_ref, levels, inner) + halo)
+
+    @pl.when(jnp.logical_not(nest))
+    def _():
+        out_ref[...] = parent_ref[...]
+        start = west_ref[1] - tile * breadth
+        top = south_ref[1] - row * height
+        lane = iota((levels, breadth), 1)
+        inside = (lane >= start) & (lane < start + LANES)
+        turn = lax.rem(start + 4 * breadth, breadth)
+        empty = jnp.zeros((levels, breadth - LANES), jnp.float32)
+        for block in range(2):
+            for m in range(third_y):
+                line = top + block * third_y + m
+
+                @pl.when((line >= 0) & (line < height))
+                def _():
+                    value = jnp.where(row == block, blend_ref[m], rows_ref[m])
+                    if m == (third_y - 1 if block == 0 else 0):
+                        value = value + jnp.where(row == block, rows_ref[third_y], blend_ref[third_y])
+                    wide = pltpu.roll(jnp.concatenate([value, empty], axis=1), turn, 1)
+                    kept = load_line(out_ref, levels, line)
+                    store_line(out_ref, levels, line, jnp.where(inside, wide, kept))
+
+    copies = [
+        pltpu.make_async_copy(out_ref.at[c], out_hbm.at[:, pl.ds(c * LANES, LANES)], sems.at[c])
+        for c in range(pieces)
+    ]
+    for copy in copies:
+        copy.start()
+    for copy in copies:
+        copy.wait()
+
+
+def call(kernel, outs, inputs, places, scratch=(), flops=0, out_place="v"):
+    spaces = {"s": pltpu.SMEM, "v": pltpu.VMEM, "h": pltpu.HBM}
+    moved = sum(4 * math.prod(shape) for shape in outs) + sum(array.nbytes for array in inputs)
+    return pl.pallas_call(
+        kernel,
+        out_shape=[jax.ShapeDtypeStruct(shape, jnp.float32) for shape in outs],
+        in_specs=[pl.BlockSpec(memory_space=spaces[p]) for p in places],
+        out_specs=[pl.BlockSpec(memory_space=spaces[out_place])] * len(outs),
+        scratch_shapes=[pltpu.VMEM(s, jnp.float32) if isinstance(s, tuple) else s for s in scratch],
+        compiler_params=pltpu.CompilerParams(vmem_limit_bytes=32 * 1024 * 1024),
+        cost_estimate=pl.CostEstimate(flops=flops, bytes_accessed=moved, transcendentals=0),
+    )(*inputs)
+
+
+def per_device_paired(air_state, wind_east, wind_north, feedback_weight, nest_west, nest_south):
+    levels, height, breadth = air_state.shape
+    third_y = height // 3
+    pieces = breadth // LANES
+    slots = third_y + 2
+    tile_count = lax.axis_size("tiles")
+    size = levels * height
+    flat = (size, breadth)
+    chunked = (pieces, size, LANES)
+    air, east, north = (array.reshape(flat) for array in (air_state, wind_east, wind_north))
+    weight = jnp.broadcast_to(feedback_weight[:, None], (levels, LANES))
+    swap = [(0, 1), (1, 0)]
+    last = tile_count - 1
+    near = [(0, 1), (1, 0)]
+    across = [(1, 2), (2, 1)]
+
+    def slabs(count):
+        return (count, levels, LANES)
+
+    def kernel(body):
+        return functools.partial(body, levels)
+
+    rows, own, edges, level = call(
+        kernel(pack_kernel),
+        [slabs(slots + 1 + pieces), slabs(slots + 1), (levels, LANES), (height, breadth)],
+        [nest_west, nest_south, air, north],
+        "hhhh",
+        [
+            pltpu.SMEM((2,), jnp.int32),
+            pltpu.SMEM((2,), jnp.int32),
+            chunked,
+            chunked,
+            pltpu.SemaphoreType.DMA((2 * pieces + 2,)),
+        ],
+    )
+    rows = lax.ppermute(rows, "rows", swap)
+    even = lax.ppermute(edges, "tiles", near)
+    odd = lax.ppermute(edges, "tiles", across)
+    level = lax.ppermute(level, "lev", swap)
+    window = own + rows[: slots + 1]
+    speeds = own
+    received = [lax.ppermute(window, "tiles", [(last - step, last)]) for step in (1, 2, 3)]
+    sides = [(size, LANES), (levels, breadth), (levels, breadth)]
+    early, own, other, coef = call(
+        kernel(early_kernel),
+        [chunked, slabs(slots + 1), slabs(slots + 1), slabs(4)],
+        [nest_west, nest_south, air, east, north, rows, level, even, odd, speeds],
+        "ssvvvvvvvv",
+        sides,
+        flops=30 * size * breadth,
+    )
+    other = lax.ppermute(other, "rows", swap)
+    first, edge, window = call(
+        kernel(first_kernel),
+        [chunked, (height, breadth), slabs(slots + 1)],
+        [early, east, speeds, *received, own, other],
+        "vvvvvvvv",
+    )
+    level = lax.ppermute(edge, "lev", swap)
+    (message,) = call(
+        kernel(average_kernel),
+        [slabs(third_y + 5)],
+        [first, east, north, rows, level, coef, window],
+        "vvvvvvv",
+        [flat],
+    )
+    pairs = [[(0, 1), (1, 0), (2, 3), (3, 2)], [(1, 3), (3, 1)], [(0, 3), (3, 0), (1, 2), (2, 1)]]
+    received = [lax.ppermute(message, "tiles", pair) for pair in pairs]
+    (blend,) = call(
+        kernel(blend_kernel),
+        [slabs(third_y + 1)],
+        [weight, first, window, *received],
+        "vvvvvv",
+    )
+    rows = lax.ppermute(blend, "rows", swap)
+    (later,) = call(
+        kernel(later_kernel),
+        [chunked],
+        [first, east, north, level, *received],
+        "vvvvvvv",
+        [flat, *sides],
+        flops=30 * size * breadth,
+    )
+    (out,) = call(
+        kernel(last_kernel),
+        [flat],
+        [nest_west, nest_south, early, later, speeds, blend, rows],
+        "ssvvvvv",
+        [chunked, pltpu.SemaphoreType.DMA((pieces,))],
+        out_place="h",
+    )
+    return out.reshape(air_state.shape)
+
+
 def solution(mesh):
     in_specs = (
         P(("members", "lev"), "rows", "tiles"),
@@ -177,6 +895,7 @@
         P("members"),
     )
     out_specs = P(("members", "lev"), "rows", "tiles")
+    paired = mesh.shape["tiles"] == 4 and mesh.shape["rows"] == 2 and mesh.shape["lev"] == 2
     return jax.shard_map(
-        per_device, mesh=mesh, in_specs=in_specs, out_specs=out_specs, check_vma=False
-    )
+        per_device_paired if paired else per_device, mesh=mesh, in_specs=in_specs, out_specs=out_specs, check_vma=False
+    )

time: 191 us -> 43 us (0.23)
  waiting for transfers between devices: 71.9 us -> 12.4 us
  starting transfers between devices: 66 us -> 20.5 us
  other arithmetic: 17.9 us -> 0.02 us
  local copies, waits for them, and re-layouts: 16.9 us -> 2.88 us
  matrix products: 13.8 us -> 0 us
  Pallas kernels: 0 us -> 6.48 us
  between operations: 3.15 us -> 0.16 us
    all_to_all x6 -> x0, starting transfers between devices: 39.9 us -> none  [the longest x2 17 us: boundary(): lax.all_to_all(pieces, 'tiles', split_axis=0, concat_axis=0, tiled=True)]
    all_to_all x6 -> x0, waiting for transfers between devices: 30.2 us -> none  [the longest x1 14.4 us: per_device(): lax.all_to_all(pieces, 'tiles', split_axis=0, concat_axis=0, tiled=True)]
    ppermute x12 -> x13, waiting for transfers between devices: 41.7 us -> 12.4 us  [the longest x1 4.19 us: per_device_paired(): other = lax.ppermute(other, 'rows', swap)]
    dot_general x10 -> x0, matrix products: 13.8 us -> none  [the longest x2 6.47 us: boundary(): pieces = jnp.einsum('lyi,tij->tlyj', source, pick_x, precision=highest)]
    reshape x1 -> x0, local copies, waits for them, and re-layouts: 8.15 us -> none  [per_device(): coarse = step_two.reshape(levels, third_y, 3, third_x, 3).mean(axis=(2, 4))]
    pallas_call x0 -> x7, Pallas kernels: none -> 6.48 us  [call(): pl.pallas_call(kernel, out_shape=[jax.ShapeDtypeStruct(shape, jnp.float32...]
    reduce_sum x5 -> x0, other arithmetic: 6.14 us -> none  [the longest x1 5.08 us: per_device(): coarse = step_two.reshape(levels, third_y, 3, third_x, 3).mean(axis=(2, 4))]
    ppermute x12 -> x13, starting transfers between devices: 26.2 us -> 20.5 us  [the longest x3 6.41 us: per_device_paired(): received = [lax.ppermute(message, 'tiles', pair) for pair in pairs]]
  transfers between devices with their start and end apart: 18 -> 13, of which waited for: 8 -> 5; matrix products, arithmetic and copies ran while one was open for 8% -> 0% of each run, Pallas kernels for 0% -> 6%
where the time goes in v2:
time: 43 us; the launch traced here: 42.4 us
  starting transfers between devices  20.5 us (48%)
  waiting for transfers between devices  12.4 us (29%)
  Pallas kernels  6.48 us (15%)
  local copies, waits for them, and re-layouts  2.88 us (7%)
    pallas_call x7, Pallas kernels, call(): pl.pallas_call(kernel, out_shape=[jax.ShapeDtypeStruct(shape, jnp.float32...  6.48 us
    ppermute x3, starting transfers between devices, per_device_paired(): received = [lax.ppermute(message, 'tiles', pair) for pair in pairs]  6.41 us
    ppermute x1, starting transfers between devices, per_device_paired(): even = lax.ppermute(edges, 'tiles', near)  6.31 us
    ppermute x1, waiting for transfers between devices, per_device_paired(): other = lax.ppermute(other, 'rows', swap)  4.19 us
    ppermute x1, waiting for transfers between devices, per_device_paired(): rows = lax.ppermute(blend, 'rows', swap)  3.97 us
    ppermute x3, waiting for transfers between devices, per_device_paired(): received = [lax.ppermute(message, 'tiles', pair) for pair in pairs]  3.01 us
    ppermute x1, starting transfers between devices, per_device_paired(): rows = lax.ppermute(rows, 'rows', swap)  3 us
    unnamed x14, local copies, waits for them, and re-layouts  2.81 us
  transfers between devices with their start and end apart: 13, of which 5 were waited for; matrix products, arithmetic and copies ran while one was open for 0% of the time, Pallas kernels for 6%

profile of v2, /device:TPU:0, one launch (start us, length us, event | category | flops | bytes accessed | tf_op | source)
XLA Modules:
  0.0 42.4 jit_solution(6080392786226931587)
XLA Ops:
  0.0 0.7 %copy-done.4 = s32[2]{0:T(128)S(1)} copy-done((s32[2]{0:T(128)S(1)}, s32[2]{0:T(128)}, u32[]{:S(2)}) %copy-start.4) | copy-done | bytes 32
  0.7 1.1 %copy-done.1 = f32[16,24,384]{2,1,0:T(8,128)S(1)} copy-done((f32[16,24,384]{2,1,0:T(8,128)S(1)}, f32[16,24,384]{2,1,0:T(8,128)}, u32[]{:S(2)}) %copy-start.1) | copy-done | bytes 589848
  1.7 1.1 %copy-done.3 = f32[16,24,384]{2,1,0:T(8,128)S(1)} copy-done((f32[16,24,384]{2,1,0:T(8,128)S(1)}, f32[16,24,384]{2,1,0:T(8,128)}, u32[]{:S(2)}) %copy-start.3) | copy-done | bytes 589848
  2.8 1.9 %shard_map.64 = (f32[14,16,128]{2,1,0:T(8,128)S(1)}, f32[11,16,128]{2,1,0:T(8,128)S(1)}, f32[16,128]{1,0:T(8,128)S(1)}, f32[24,384]{1,0:T(8,128)S(1)}) custom-call(s32[2]{0:T(128)S(1)} %copy-done.4, s32[2]{0:T(128)S(1)} %copy-done.5, f32[384,384]{1,0:T(8,128)S(1)} %bitcast.12, f32[384,384]{1,0:T(8,128)S(1)} %bitcast.8), custom_call_target="tpu_custom_call" | custom-call | bytes 1429520 | tf_op jit(solution)/shard_map/pallas_call | solution.py:783
  4.7 3.0 %collective-permute-start = (f32[14,16,128]{2,1,0:T(8,128)S(1)}, f32[14,16,128]{2,1,0:T(8,128)S(1)}, u32[]{:S(2)}, u32[]{:S(2)}) collective-permute-start(f32[14,16,128]{2,1,0:T(8,128)S(1)} %get-tuple-element.16), channel_id=1, source_target_pairs={{0,2},{2,0},{1,3},{3,1},{4,6},{6,4},{5,7},{7,5},{8,10},{10,8},{9,1... | collective-permute-start | bytes 344072 | tf_op jit(solution)/shard_map/ppermute | solution.py:829
  7.7 0.6 %collective-permute-start.3 = (f32[16,128]{1,0:T(8,128)S(1)}, f32[16,128]{1,0:T(8,128)S(1)}, u32[]{:S(2)}, u32[]{:S(2)}) collective-permute-start(f32[16,128]{1,0:T(8,128)S(1)} %get-tuple-element.18), channel_id=1, source_target_pairs={{4,8},{8,4},{5,9},{9,5},{6,10},{10,6},{7,11},{11,7},{20,24},{24,20... | collective-permute-start | bytes 24584 | tf_op jit(solution)/shard_map/ppermute | solution.py:831
  8.4 6.3 %collective-permute-start.2 = (f32[16,128]{1,0:T(8,128)S(1)}, f32[16,128]{1,0:T(8,128)S(1)}, u32[]{:S(2)}, u32[]{:S(2)}) collective-permute-start(f32[16,128]{1,0:T(8,128)S(1)} %get-tuple-element.18), channel_id=1, source_target_pairs={{0,4},{4,0},{1,5},{5,1},{2,6},{6,2},{3,7},{7,3},{16,20},{20,16},{1... | collective-permute-start | bytes 24584 | tf_op jit(solution)/shard_map/ppermute | solution.py:830
  14.7 0.1 collective-permute-start.1
  14.8 1.3 %collective-permute-start.6 = (f32[11,16,128]{2,1,0:T(8,128)S(1)}, f32[11,16,128]{2,1,0:T(8,128)S(1)}, u32[]{:S(2)}, u32[]{:S(2)}) collective-permute-start(f32[11,16,128]{2,1,0:T(8,128)S(1)} %slice_add_fusion), channel_id=1, source_target_pairs={{0,12},{1,13},{2,14},{3,15},{16,28},{17,29},{18,30},{19,31}} | collective-permute-start | bytes 270344 | tf_op jit(solution)/shard_map/ppermute | solution.py:835
  16.1 0.7 %collective-permute-start.5 = (f32[11,16,128]{2,1,0:T(8,128)S(1)}, f32[11,16,128]{2,1,0:T(8,128)S(1)}, u32[]{:S(2)}, u32[]{:S(2)}) collective-permute-start(f32[11,16,128]{2,1,0:T(8,128)S(1)} %slice_add_fusion), channel_id=1, source_target_pairs={{4,12},{5,13},{6,14},{7,15},{20,28},{21,29},{22,30},{23,31}} | collective-permute-start | bytes 270344 | tf_op jit(solution)/shard_map/ppermute | solution.py:835
  16.8 0.7 %collective-permute-start.4 = (f32[11,16,128]{2,1,0:T(8,128)S(1)}, f32[11,16,128]{2,1,0:T(8,128)S(1)}, u32[]{:S(2)}, u32[]{:S(2)}) collective-permute-start(f32[11,16,128]{2,1,0:T(8,128)S(1)} %slice_add_fusion), channel_id=1, source_target_pairs={{8,12},{9,13},{10,14},{11,15},{24,28},{25,29},{26,30},{27,31}} | collective-permute-start | bytes 270344 | tf_op jit(solution)/shard_map/ppermute | solution.py:835
  17.5 2.6 %shard_map.65 = (f32[3,384,128]{2,1,0:T(8,128)S(1)}, f32[11,16,128]{2,1,0:T(8,128)S(1)}, f32[11,16,128]{2,1,0:T(8,128)S(1)}, f32[4,16,128]{2,1,0:T(8,128)S(1)}) custom-call(s32[2]{0:T(128)S(1)} %copy-done.4, s32[2]{0:T(128)S(1)} %copy-done.5, f32[384,384]{1,0:T(8,128)S(1)} %bitcast.13, f32[384,384]{1,0:T(8,128)S(1)} %bitcast.4, f32[384,384]{1,0:T(8,128)S(1)} %bitcast.9, ...), custom_call_target="tpu_custom_call" | custom-call | flops 4423680 | bytes 2830352 | tf_op jit(solution)/shard_map/pallas_call | solution.py:783
  20.1 0.9 %collective-permute-start.7 = (f32[11,16,128]{2,1,0:T(8,128)S(1)}, f32[11,16,128]{2,1,0:T(8,128)S(1)}, u32[]{:S(2)}, u32[]{:S(2)}) collective-permute-start(f32[11,16,128]{2,1,0:T(8,128)S(1)} %get-tuple-element.22), channel_id=1, source_target_pairs={{0,2},{2,0},{1,3},{3,1},{4,6},{6,4},{5,7},{7,5},{8,10},{10,8},{9,1... | collective-permute-start | bytes 270344 | tf_op jit(solution)/shard_map/ppermute | solution.py:845
  21.0 4.2 %collective-permute-done.7.other_ref = f32[11,16,128]{2,1,0:T(8,128)S(1)} collective-permute-done((f32[11,16,128]{2,1,0:T(8,128)S(1)}, f32[11,16,128]{2,1,0:T(8,128)S(1)}, u32[]{:S(2)}, u32[]{:S(2)}) %collective-permute-start.7) | collective-permute-done | bytes 90144 | tf_op jit(solution)/shard_map/ppermute | solution.py:845
  25.3 1.2 %collective-permute-done.8.level_ref = f32[24,384]{1,0:T(8,128)S(1)} collective-permute-done((f32[24,384]{1,0:T(8,128)S(1)}, f32[24,384]{1,0:T(8,128)S(1)}, u32[]{:S(2)}, u32[]{:S(2)}) %collective-permute-start.8) | collective-permute-done | bytes 36896 | tf_op jit(solution)/shard_map/ppermute | solution.py:852
  26.5 2.2 %collective-permute-start.11 = (f32[13,16,128]{2,1,0:T(8,128)S(1)}, f32[13,16,128]{2,1,0:T(8,128)S(1)}, u32[]{:S(2)}, u32[]{:S(2)}) collective-permute-start(f32[13,16,128]{2,1,0:T(8,128)S(1)} %shard_map.67), channel_id=1, source_target_pairs={{0,12},{12,0},{4,8},{8,4},{1,13},{13,1},{5,9},{9,5},{2,14},{14,2},... | collective-permute-start | bytes 319496 | tf_op jit(solution)/shard_map/ppermute | solution.py:861
  28.7 0.7 %collective-permute-start.10 = (f32[13,16,128]{2,1,0:T(8,128)S(1)}, f32[13,16,128]{2,1,0:T(8,128)S(1)}, u32[]{:S(2)}, u32[]{:S(2)}) collective-permute-start(f32[13,16,128]{2,1,0:T(8,128)S(1)} %shard_map.67), channel_id=1, source_target_pairs={{4,12},{12,4},{5,13},{13,5},{6,14},{14,6},{7,15},{15,7},{20,28},{2... | collective-permute-start | bytes 319496 | tf_op jit(solution)/shard_map/ppermute | solution.py:861
  29.4 3.6 %collective-permute-start.9 = (f32[13,16,128]{2,1,0:T(8,128)S(1)}, f32[13,16,128]{2,1,0:T(8,128)S(1)}, u32[]{:S(2)}, u32[]{:S(2)}) collective-permute-start(f32[13,16,128]{2,1,0:T(8,128)S(1)} %shard_map.67), channel_id=1, source_target_pairs={{0,4},{4,0},{8,12},{12,8},{1,5},{5,1},{9,13},{13,9},{2,6},{6,2},{1... | collective-permute-start | bytes 319496 | tf_op jit(solution)/shard_map/ppermute | solution.py:861
  33.0 1.0 %collective-permute-done.11.three_ref = f32[13,16,128]{2,1,0:T(8,128)S(1)} collective-permute-done((f32[13,16,128]{2,1,0:T(8,128)S(1)}, f32[13,16,128]{2,1,0:T(8,128)S(1)}, u32[]{:S(2)}, u32[]{:S(2)}) %collective-permute-start.11) | collective-permute-done | bytes 106528 | tf_op jit(solution)/shard_map/ppermute | solution.py:861
  34.0 2.0 %collective-permute-done.9.one_ref = f32[13,16,128]{2,1,0:T(8,128)S(1)} collective-permute-done((f32[13,16,128]{2,1,0:T(8,128)S(1)}, f32[13,16,128]{2,1,0:T(8,128)S(1)}, u32[]{:S(2)}, u32[]{:S(2)}) %collective-permute-start.9) | collective-permute-done | bytes 106528 | tf_op jit(solution)/shard_map/ppermute | solution.py:861
  36.0 0.4 shard_map.69.blend_ref
  36.4 0.4 %collective-permute-start.12 = (f32[9,16,128]{2,1,0:T(8,128)S(1)}, f32[9,16,128]{2,1,0:T(8,128)S(1)}, u32[]{:S(2)}, u32[]{:S(2)}) collective-permute-start(f32[9,16,128]{2,1,0:T(8,128)S(1)} %shard_map.69.blend_ref), channel_id=1, source_target_pairs={{0,2},{2,0},{1,3},{3,1},{4,6},{6,4},{5,7},{7,5},{8,10},{10,8},{9,1... | collective-permute-start | bytes 221192 | tf_op jit(solution)/shard_map/ppermute | solution.py:868
  36.9 4.0 %collective-permute-done.12.rows_ref = f32[9,16,128]{2,1,0:T(8,128)S(1)} collective-permute-done((f32[9,16,128]{2,1,0:T(8,128)S(1)}, f32[9,16,128]{2,1,0:T(8,128)S(1)}, u32[]{:S(2)}, u32[]{:S(2)}) %collective-permute-start.12) | collective-permute-done | bytes 73760 | tf_op jit(solution)/shard_map/ppermute | solution.py:868
  40.8 1.5 %shard_map.70 = f32[384,384]{1,0:T(8,128)} custom-call(s32[2]{0:T(128)S(1)} %copy-done.4, s32[2]{0:T(128)S(1)} %copy-done.5, f32[3,384,128]{2,1,0:T(8,128)S(1)} %get-tuple-element.20.early_ref.parent_ref, f32[3,384,128]{2,1,0:T(8,128)S(1)} %shard_map.68.nested_ref, f32[11,16,128]{2,1,0:T(8,128)S(1)} %get-tuple-element.19.speeds_ref, ...), custom_call_target="tpu_custom_call" | custom-call | bytes 2007056 | tf_op jit(solution)/shard_map/pallas_call | solution.py:783
  (25 shorter events, 0.2 us)
Async XLA Ops:
  0.0 0.7 %copy-start.4 = (s32[2]{0:T(128)S(1)}, s32[2]{0:T(128)}, u32[]{:S(2)}) copy-start(s32[2]{0:T(128)} %west_ref.3) | copy-start | bytes 28
  0.0 0.7 %copy-start.5 = (s32[2]{0:T(128)S(1)}, s32[2]{0:T(128)}, u32[]{:S(2)}) copy-start(s32[2]{0:T(128)} %south_ref.3) | copy-start | bytes 28
  0.7 1.1 %copy-start.1 = (f32[16,24,384]{2,1,0:T(8,128)S(1)}, f32[16,24,384]{2,1,0:T(8,128)}, u32[]{:S(2)}) copy-start(f32[16,24,384]{2,1,0:T(8,128)} %param.8) | copy-start | bytes 1769476
  1.7 1.1 %copy-start.3 = (f32[16,24,384]{2,1,0:T(8,128)S(1)}, f32[16,24,384]{2,1,0:T(8,128)}, u32[]{:S(2)}) copy-start(f32[16,24,384]{2,1,0:T(8,128)} %param.6) | copy-start | bytes 1769476
  2.8 14.7 %copy-start = (f32[16,24,384]{2,1,0:T(8,128)S(1)}, f32[16,24,384]{2,1,0:T(8,128)}, u32[]{:S(2)}) copy-start(f32[16,24,384]{2,1,0:T(8,128)} %param.7) | copy-start | bytes 1769476
  4.7 10.1 %collective-permute-start = (f32[14,16,128]{2,1,0:T(8,128)S(1)}, f32[14,16,128]{2,1,0:T(8,128)S(1)}, u32[]{:S(2)}, u32[]{:S(2)}) collective-permute-start(f32[14,16,128]{2,1,0:T(8,128)S(1)} %get-tuple-element.16), channel_id=1, source_target_pairs={{0,2},{2,0},{1,3},{3,1},{4,6},{6,4},{5,7},{7,5},{8,10},{10,8},{9,1... | collective-permute-start | bytes 344072 | tf_op jit(solution)/shard_map/ppermute | solution.py:829
  7.7 9.1 %collective-permute-start.3 = (f32[16,128]{1,0:T(8,128)S(1)}, f32[16,128]{1,0:T(8,128)S(1)}, u32[]{:S(2)}, u32[]{:S(2)}) collective-permute-start(f32[16,128]{1,0:T(8,128)S(1)} %get-tuple-element.18), channel_id=1, source_target_pairs={{4,8},{8,4},{5,9},{9,5},{6,10},{10,6},{7,11},{11,7},{20,24},{24,20... | collective-permute-start | bytes 24584 | tf_op jit(solution)/shard_map/ppermute | solution.py:831
  8.4 9.1 %collective-permute-start.2 = (f32[16,128]{1,0:T(8,128)S(1)}, f32[16,128]{1,0:T(8,128)S(1)}, u32[]{:S(2)}, u32[]{:S(2)}) collective-permute-start(f32[16,128]{1,0:T(8,128)S(1)} %get-tuple-element.18), channel_id=1, source_target_pairs={{0,4},{4,0},{1,5},{5,1},{2,6},{6,2},{3,7},{7,3},{16,20},{20,16},{1... | collective-permute-start | bytes 24584 | tf_op jit(solution)/shard_map/ppermute | solution.py:830
  14.7 2.8 %collective-permute-start.1 = (f32[24,384]{1,0:T(8,128)S(1)}, f32[24,384]{1,0:T(8,128)S(1)}, u32[]{:S(2)}, u32[]{:S(2)}) collective-permute-start(f32[24,384]{1,0:T(8,128)S(1)} %get-tuple-element.17), channel_id=1, source_target_pairs={{0,1},{1,0},{2,3},{3,2},{4,5},{5,4},{6,7},{7,6},{8,9},{9,8},{10,11... | collective-permute-start | bytes 110600 | tf_op jit(solution)/shard_map/ppermute | solution.py:832
  14.8 6.2 %collective-permute-start.6 = (f32[11,16,128]{2,1,0:T(8,128)S(1)}, f32[11,16,128]{2,1,0:T(8,128)S(1)}, u32[]{:S(2)}, u32[]{:S(2)}) collective-permute-start(f32[11,16,128]{2,1,0:T(8,128)S(1)} %slice_add_fusion), channel_id=1, source_target_pairs={{0,12},{1,13},{2,14},{3,15},{16,28},{17,29},{18,30},{19,31}} | collective-permute-start | bytes 270344 | tf_op jit(solution)/shard_map/ppermute | solution.py:835
  16.1 4.9 %collective-permute-start.5 = (f32[11,16,128]{2,1,0:T(8,128)S(1)}, f32[11,16,128]{2,1,0:T(8,128)S(1)}, u32[]{:S(2)}, u32[]{:S(2)}) collective-permute-start(f32[11,16,128]{2,1,0:T(8,128)S(1)} %slice_add_fusion), channel_id=1, source_target_pairs={{4,12},{5,13},{6,14},{7,15},{20,28},{21,29},{22,30},{23,31}} | collective-permute-start | bytes 270344 | tf_op jit(solution)/shard_map/ppermute | solution.py:835
  16.8 4.2 %collective-permute-start.4 = (f32[11,16,128]{2,1,0:T(8,128)S(1)}, f32[11,16,128]{2,1,0:T(8,128)S(1)}, u32[]{:S(2)}, u32[]{:S(2)}) collective-permute-start(f32[11,16,128]{2,1,0:T(8,128)S(1)} %slice_add_fusion), channel_id=1, source_target_pairs={{8,12},{9,13},{10,14},{11,15},{24,28},{25,29},{26,30},{27,31}} | collective-permute-start | bytes 270344 | tf_op jit(solution)/shard_map/ppermute | solution.py:835
  20.1 5.1 %collective-permute-start.7 = (f32[11,16,128]{2,1,0:T(8,128)S(1)}, f32[11,16,128]{2,1,0:T(8,128)S(1)}, u32[]{:S(2)}, u32[]{:S(2)}) collective-permute-start(f32[11,16,128]{2,1,0:T(8,128)S(1)} %get-tuple-element.22), channel_id=1, source_target_pairs={{0,2},{2,0},{1,3},{3,1},{4,6},{6,4},{5,7},{7,5},{8,10},{10,8},{9,1... | collective-permute-start | bytes 270344 | tf_op jit(solution)/shard_map/ppermute | solution.py:845
  25.2 1.3 %copy-start.2 = (f32[16,24,384]{2,1,0:T(8,128)S(1)}, f32[16,24,384]{2,1,0:T(8,128)}, u32[]{:S(2)}) copy-start(f32[16,24,384]{2,1,0:T(8,128)} %param.8) | copy-start | bytes 1769476
  25.2 1.3 %collective-permute-start.8 = (f32[24,384]{1,0:T(8,128)S(1)}, f32[24,384]{1,0:T(8,128)S(1)}, u32[]{:S(2)}, u32[]{:S(2)}) collective-permute-start(f32[24,384]{1,0:T(8,128)S(1)} %get-tuple-element.24), channel_id=1, source_target_pairs={{0,1},{1,0},{2,3},{3,2},{4,5},{5,4},{6,7},{7,6},{8,9},{9,8},{10,11... | collective-permute-start | bytes 110600 | tf_op jit(solution)/shard_map/ppermute | solution.py:852
  26.5 9.5 %copy-start.6 = (f32[16]{0:T(128)S(1)}, f32[16]{0:T(128)}, u32[]{:S(2)}) copy-start(f32[16]{0:T(128)} %param.9) | copy-start | bytes 196
  26.5 7.4 %collective-permute-start.11 = (f32[13,16,128]{2,1,0:T(8,128)S(1)}, f32[13,16,128]{2,1,0:T(8,128)S(1)}, u32[]{:S(2)}, u32[]{:S(2)}) collective-permute-start(f32[13,16,128]{2,1,0:T(8,128)S(1)} %shard_map.67), channel_id=1, source_target_pairs={{0,12},{12,0},{4,8},{8,4},{1,13},{13,1},{5,9},{9,5},{2,14},{14,2},... | collective-permute-start | bytes 319496 | tf_op jit(solution)/shard_map/ppermute | solution.py:861
  28.7 5.2 %collective-permute-start.10 = (f32[13,16,128]{2,1,0:T(8,128)S(1)}, f32[13,16,128]{2,1,0:T(8,128)S(1)}, u32[]{:S(2)}, u32[]{:S(2)}) collective-permute-start(f32[13,16,128]{2,1,0:T(8,128)S(1)} %shard_map.67), channel_id=1, source_target_pairs={{4,12},{12,4},{5,13},{13,5},{6,14},{14,6},{7,15},{15,7},{20,28},{2... | collective-permute-start | bytes 319496 | tf_op jit(solution)/shard_map/ppermute | solution.py:861
  29.4 6.6 %collective-permute-start.9 = (f32[13,16,128]{2,1,0:T(8,128)S(1)}, f32[13,16,128]{2,1,0:T(8,128)S(1)}, u32[]{:S(2)}, u32[]{:S(2)}) collective-permute-start(f32[13,16,128]{2,1,0:T(8,128)S(1)} %shard_map.67), channel_id=1, source_target_pairs={{0,4},{4,0},{8,12},{12,8},{1,5},{5,1},{9,13},{13,9},{2,6},{6,2},{1... | collective-permute-start | bytes 319496 | tf_op jit(solution)/shard_map/ppermute | solution.py:861
  36.4 4.4 %collective-permute-start.12 = (f32[9,16,128]{2,1,0:T(8,128)S(1)}, f32[9,16,128]{2,1,0:T(8,128)S(1)}, u32[]{:S(2)}, u32[]{:S(2)}) collective-permute-start(f32[9,16,128]{2,1,0:T(8,128)S(1)} %shard_map.69.blend_ref), channel_id=1, source_target_pairs={{0,2},{2,0},{1,3},{3,1},{4,6},{6,4},{5,7},{7,5},{8,10},{10,8},{9,1... | collective-permute-start | bytes 221192 | tf_op jit(solution)/shard_map/ppermute | solution.py:868

commit v3 on v2

--- a/solution.py
+++ b/solution.py
@@ -267,27 +267,49 @@
     return jnp.concatenate([ref[first + i] for i in range(count)], axis=1)
 
 
+def column_pieces(start, pieces):
+    first = (start + 64 * LANES) // LANES - 64
+    offset = start - first * LANES
+    held = [(c >= 0) & (c < pieces) for c in (first, first + 1)]
+    return [jnp.clip(c, 0, pieces - 1) for c in (first, first + 1)], held, offset
+
+
 def pack_window(ref, field_ref, levels, top, start):
-    height = field_ref.shape[1] // levels
-    breadth = field_ref.shape[0] * LANES
+    pieces, size, _ = field_ref.shape
+    height = size // levels
     slots = ref.shape[0] - 1
-    lane = iota((levels, breadth), 1)
-    column = jnp.where(lane == breadth - 1, start - 1, start + lane)
-    inside = (column >= 0) & (column < breadth)
-    turn = lax.rem(4 * breadth - start, breadth)
     lane = iota((levels, LANES), 1)
+    (left, right), (left_held, right_held), offset = column_pieces(start, pieces)
+    before = lax.rem(offset + LANES - 1, LANES)
+    (beside, _), (beside_held, _), _ = column_pieces(start - 1, pieces)
+    in_left = lane < LANES - offset
+    held = jnp.where(in_left, left_held.astype(jnp.float32), right_held.astype(jnp.float32))
+    west_held, east_held = beside_held.astype(jnp.float32), right_held.astype(jnp.float32)
+    turn = lax.rem(LANES - offset, LANES)
     extra = jnp.zeros((levels, LANES), jnp.float32)
     for slot in range(slots):
         line = top + slot
-        there = (line >= 0) & (line < height)
-        rows = load_line(field_ref, levels, jnp.clip(line, 0, height - 1))
-        rows = jnp.where(inside & there, pltpu.roll(rows, turn, 1), 0.0)
-        ref[slot] = rows[:, :LANES]
-        east = rows[:, LANES : 2 * LANES]
-        west = rows[:, breadth - LANES :]
-        extra = jnp.where(lane == slot, pltpu.roll(west, slot + 1, 1), extra)
-        extra = jnp.where(lane == EAST_LANE + slot, pltpu.roll(east, EAST_LANE + slot, 1), extra)
+        there = ((line >= 0) & (line < height)).astype(jnp.float32)
+        rows = pl.ds(jnp.clip(line, 0, height - 1), levels, stride=height)
+        near, far, west = field_ref[left, rows, :], field_ref[right, rows, :], field_ref[beside, rows, :]
+        ref[slot] = jnp.where(in_left, pltpu.roll(near, turn, 1), pltpu.roll(far, turn, 1)) * (held * there)
+        west = pltpu.roll(west, lax.rem(LANES + slot - before, LANES), 1) * (west_held * there)
+        east = pltpu.roll(far, lax.rem(LANES + EAST_LANE + slot - offset, LANES), 1) * (east_held * there)
+        extra = jnp.where(lane == slot, west, jnp.where(lane == EAST_LANE + slot, east, extra))
     ref[slots] = extra
+
+
+def place_row(ref, levels, line, start, value):
+    pieces, size, _ = ref.shape
+    height = size // levels
+    lane = iota((levels, LANES), 1)
+    at, held, offset = column_pieces(start, pieces)
+    value = pltpu.roll(value, offset, 1)
+    there = (line >= 0) & (line < height)
+    rows = pl.ds(jnp.clip(line, 0, height - 1), levels, stride=height)
+    for c in range(2):
+        mine = (lane >= offset) if c == 0 else (lane < offset)
+        ref[at[c], rows, :] = jnp.where(mine & (held[c] & there), value, ref[at[c], rows, :])
 
 
 def pack_edges(field_ref, levels):
@@ -409,19 +431,46 @@
     return jnp.where(lev == 0, load_level(ref, height, last), load_level(ref, height, 0))
 
 
+def ghost_row_weights(ghost, breadth):
+    cell, third = iota((breadth, 3 * LANES), 0), iota((breadth, 3 * LANES), 1)
+    kind = third // LANES
+    offset = cell - 3 * (third - kind * LANES)
+    middle = jnp.where(offset == 1, 3, jnp.where((offset == 0) | (offset == 2), 2, 0))
+    weight = jnp.where(kind == 1, middle, jnp.where(offset == kind, 1, 0))
+    return from_right(ghost, table(weight)) * (1.0 / 27.0)
+
+
+def ghost_column_weights(first, last, levels, height):
+    shape = (levels * height, LANES)
+    lane = iota(shape, 1)
+    _, line = split_level(iota(shape, 0), height)
+    block = lane // 8
+    inside = lane - block * 8
+    eastern = inside >= 3
+    kind = jnp.where(eastern, inside - 3, inside)
+    offset = line - 3 * block
+    middle = jnp.where(offset == 1, 3, jnp.where((offset == 0) | (offset == 2), 2, 0))
+    weight = jnp.where(kind == 1, middle, jnp.where(offset == kind, 1, 0))
+    weight = jnp.where((inside < 6) & (block < height // 3), weight, 0).astype(jnp.float32)
+    columns = jnp.where(eastern, last, first) * weight
+    return from_left(level_table(levels, height), columns) * (1.0 / 27.0)
+
+
 def pack_kernel(
     levels,
     west_hbm,
     south_hbm,
     air_hbm,
+    east_hbm,
     north_hbm,
     rows_ref,
     own_ref,
-    edges_ref,
     level_ref,
+    speeds_ref,
     west_ref,
     south_ref,
     air_ref,
+    east_ref,
     north_ref,
     sems,
 ):
@@ -439,12 +488,18 @@
         ]
 
     copies = column_copies(air_hbm, air_ref, 0)
-    copies.append(pltpu.make_async_copy(west_hbm, west_ref, sems.at[2 * pieces]))
-    copies.append(pltpu.make_async_copy(south_hbm, south_ref, sems.at[2 * pieces + 1]))
-    speeds = column_copies(north_hbm, north_ref, pieces)
-    for copy in copies + speeds:
+    copies.append(pltpu.make_async_copy(west_hbm, west_ref, sems.at[3 * pieces]))
+    copies.append(pltpu.make_async_copy(south_hbm, south_ref, sems.at[3 * pieces + 1]))
+    speeds = column_copies(east_hbm, east_ref, pieces) + column_copies(north_hbm, north_ref, 2 * pieces)
+    for copy in copies:
         copy.start()
-    for copy in copies + speeds:
+
+    @pl.when(nest)
+    def _():
+        for copy in speeds:
+            copy.start()
+
+    for copy in copies:
         copy.wait()
     inner = inner_line(height, row)
     level_ref[...] = edge_level(air_ref, height, lev)
@@ -452,13 +507,19 @@
 
     @pl.when(nest)
     def _():
+        for copy in speeds:
+            copy.wait()
         speed = load_line(north_ref, levels, inner)
-        store_slabs(rows_ref, 0, speed)
-        for i in range(pieces, slots + 1):
-            rows_ref[i] = jnp.zeros((levels, LANES), jnp.float32)
-        store_slabs(own_ref, 0, load_line(north_ref, levels, height - 1 - inner))
-        store_slabs(own_ref, pieces, speed)
-        edges_ref[...] = jnp.zeros_like(edges_ref)
+        outer = load_line(north_ref, levels, height - 1 - inner)
+        own_ref[...] = jnp.zeros_like(own_ref)
+        rows_ref[pl.ds(0, slots + 1)] = jnp.zeros_like(own_ref)
+        store_slabs(rows_ref, 4, speed)
+        store_slabs(speeds_ref, 0, outer)
+        store_slabs(speeds_ref, pieces, speed)
+        store_slabs(own_ref, 0, ghost_row_weights(ghost_weight(outer, row == 0), breadth))
+        first = ghost_weight(east_ref[0, :, 0:1], True)
+        last = ghost_weight(east_ref[pieces - 1, :, LANES - 1 : LANES], False)
+        own_ref[3] = ghost_column_weights(first, last, levels, height)
 
     @pl.when(jnp.logical_not(nest))
     def _():
@@ -467,7 +528,8 @@
         part = rows_ref.at[pl.ds(0, slots + 1)]
         pack_window(part, air_ref, levels, top + (1 - row) * third_y, start)
         pack_window(own_ref, air_ref, levels, top + row * third_y, start)
-        edges_ref[...] = pack_edges(air_ref, levels)
+        own_ref[slots] = own_ref[slots] + pack_edges(air_ref, levels)
+        speeds_ref[...] = jnp.zeros_like(speeds_ref)
 
 
 def early_kernel(
@@ -479,13 +541,11 @@
     north_ref,
     rows_ref,
     level_ref,
-    even_ref,
-    odd_ref,
-    speeds_ref,
+    one_ref,
+    three_ref,
     field_ref,
     own_ref,
     other_ref,
-    coef_ref,
     side_ref,
     northern_ref,
     southern_ref,
@@ -507,55 +567,31 @@
     @pl.when(nest)
     def _():
         full_step(*shared, True, northern_ref, southern_ref, None, None)
-        ghost = ghost_weight(join_slabs(speeds_ref, 0, pieces), row == 0)
-        cell, third = iota((breadth, 3 * LANES), 0), iota((breadth, 3 * LANES), 1)
-        kind = third // LANES
-        offset = cell - 3 * (third - kind * LANES)
-        middle = jnp.where(offset == 1, 3, jnp.where((offset == 0) | (offset == 2), 2, 0))
-        weight = jnp.where(kind == 1, middle, jnp.where(offset == kind, 1, 0))
-        store_slabs(coef_ref, 0, from_right(ghost, table(weight)) * (1.0 / 27.0))
-        shape = (size, LANES)
-        lane = iota(shape, 1)
-        _, line = split_level(iota(shape, 0), height)
-        block = lane // 8
-        inside = lane - block * 8
-        eastern = inside >= 3
-        kind = jnp.where(eastern, inside - 3, inside)
-        offset = line - 3 * block
-        middle = jnp.where(offset == 1, 3, jnp.where((offset == 0) | (offset == 2), 2, 0))
-        weight = jnp.where(kind == 1, middle, jnp.where(offset == kind, 1, 0))
-        weight = jnp.where((inside < 6) & (block < third_y), weight, 0).astype(jnp.float32)
-        first = ghost_weight(east_ref[:, 0:1], True)
-        last = ghost_weight(east_ref[:, breadth - 1 : breadth], False)
-        columns = jnp.where(eastern, last, first) * weight
-        coef_ref[3] = from_left(level_table(levels, height), columns) * (1.0 / 27.0)
         own_ref[...] = jnp.zeros_like(own_ref)
         other_ref[...] = jnp.zeros_like(other_ref)
 
     @pl.when(jnp.logical_not(nest))
     def _():
-        columns = neighbour_columns(even_ref[...], odd_ref[...], tile_count - 1, tile)
+        columns = neighbour_columns(one_ref[slots], three_ref[slots], tile_count - 1, tile)
         side_ref[...] = unpack_edges(columns, levels, height)
         full_step(*shared, False, northern_ref, southern_ref, side_ref, None)
         start = west_ref[1] - tile * breadth
         top = south_ref[1] - 1 - row * height
         pack_window(other_ref, field_ref, levels, top + (1 - row) * third_y, start)
         pack_window(own_ref, field_ref, levels, top + row * third_y, start)
-        coef_ref[...] = jnp.zeros_like(coef_ref)
 
 
 def first_kernel(
-    levels, early_ref, east_ref, speeds_ref, one_ref, two_ref, three_ref, own_ref, other_ref, field_ref, edge_ref, window_ref
+    levels, early_ref, east_ref, speeds_ref, one_ref, two_ref, three_ref, field_ref, edge_ref
 ):
     pieces, size, _ = early_ref.shape
     height, breadth = edge_ref.shape
-    slots = own_ref.shape[0] - 1
+    slots = one_ref.shape[0] - 1
     tile, row, lev = place()
     nest = tile == lax.axis_size("tiles") - 1
 
     @pl.when(jnp.logical_not(nest))
     def _():
-        window_ref[...] = own_ref[...] + other_ref[...]
         edge_ref[...] = jnp.zeros_like(edge_ref)
 
     @pl.when(nest)
@@ -580,7 +616,7 @@
 
 
 def average_kernel(
-    levels, field_ref, east_ref, north_ref, rows_ref, level_ref, coef_ref, window_ref, message_ref, part_ref
+    levels, field_ref, east_ref, north_ref, rows_ref, level_ref, own_ref, other_ref, message_ref, part_ref
 ):
     pieces, size, _ = field_ref.shape
     height, breadth = level_ref.shape
@@ -590,10 +626,7 @@
 
     @pl.when(jnp.logical_not(nest))
     def _():
-        slots = window_ref.shape[0]
-        message_ref[pl.ds(0, slots)] = window_ref[...]
-        for i in range(slots, message_ref.shape[0]):
-            message_ref[i] = jnp.zeros((levels, LANES), jnp.float32)
+        message_ref[...] = own_ref[...] + other_ref[...]
 
     @pl.when(nest)
     def _():
@@ -610,13 +643,26 @@
         means = from_left(rows, from_right(part_ref[...], sums)) * (1.0 / 9.0)
         for m in range(third_y):
             message_ref[m] = means[m * levels : (m + 1) * levels]
-        message_ref[pl.ds(third_y, 4)] = coef_ref[...]
         shared = load_line(field_ref, levels, inner_line(height, row))
-        shared = ghost_weight(join_slabs(rows_ref, 0, pieces), row == 0) * shared
-        message_ref[third_y + 4] = from_right(shared, sums) * (1.0 / 9.0)
-
-
-def blend_kernel(levels, weight_ref, field_ref, window_ref, one_ref, two_ref, three_ref, rows_ref):
+        shared = ghost_weight(join_slabs(rows_ref, 4, pieces), row == 0) * shared
+        message_ref[third_y] = from_right(shared, sums) * (1.0 / 9.0)
+        for i in range(third_y + 1, message_ref.shape[0]):
+            message_ref[i] = jnp.zeros((levels, LANES), jnp.float32)
+
+
+def blend_kernel(
+    levels,
+    weight_ref,
+    field_ref,
+    window_ref,
+    one_ref,
+    two_ref,
+    three_ref,
+    coef_one_ref,
+    coef_two_ref,
+    coef_three_ref,
+    rows_ref,
+):
     pieces, size, _ = field_ref.shape
     height = size // levels
     third_y = height // 3
@@ -633,8 +679,15 @@
 
     @pl.when(jnp.logical_not(nest))
     def _():
+        def of_nest(refs, i):
+            one, two, three = refs
+            return jnp.where(tile == 0, three[i], jnp.where(tile == 1, two[i], one[i]))
+
         def mine(i):
-            return jnp.where(tile == 0, three_ref[i], jnp.where(tile == 1, two_ref[i], one_ref[i]))
+            return of_nest((one_ref, two_ref, three_ref), i)
+
+        def coefficient(i):
+            return of_nest((coef_one_ref, coef_two_ref, coef_three_ref), i)
 
         def whole(i):
             odd = tile % 2 == 1
@@ -654,8 +707,8 @@
             last = EAST_LANE + s
             east = jnp.where(at_last, extra[:, last : last + 1], pltpu.roll(x, LANES - 1, 1))
             lines.append((west, x, east))
-        edges = mine(third_y + 3)
-        ghosts = [mine(third_y + q) for q in range(3)]
+        edges = coefficient(3)
+        ghosts = [coefficient(q) for q in range(3)]
 
         def outward(side, q):
             near = lines[1] if side == 0 else lines[slots - 2]
@@ -681,11 +734,13 @@
                     for q in range(3):
                         value = value + jnp.where(row == side, ghosts[q], 0.0) * outward(side, q)
             rows_ref[m] = x + weight * (value - x)
-        rows_ref[third_y] = weight * mine(third_y + 4)
+        rows_ref[third_y] = weight * mine(third_y)
 
 
 def later_kernel(
     levels,
+    west_ref,
+    south_ref,
     field_ref,
     east_ref,
     north_ref,
@@ -693,6 +748,8 @@
     one_ref,
     two_ref,
     three_ref,
+    parent_ref,
+    blend_ref,
     out_ref,
     fine_ref,
     side_ref,
@@ -700,10 +757,12 @@
     southern_ref,
 ):
     height, breadth = level_ref.shape
-    slots = height // 3 + 2
+    third_y = height // 3
+    slots = third_y + 2
     tile, row, lev = place()
-
-    @pl.when(tile == lax.axis_size("tiles") - 1)
+    nest = tile == lax.axis_size("tiles") - 1
+
+    @pl.when(nest)
     def _():
         slabs = [one_ref[s] + two_ref[s] + three_ref[s] for s in range(slots + 1)]
         cells, ring = refine(slabs[:slots], slabs[slots], height, breadth, row)
@@ -727,45 +786,46 @@
             fine_ref,
         )
 
+    @pl.when(jnp.logical_not(nest))
+    def _():
+        out_ref[...] = parent_ref[...]
+        start = west_ref[1] - tile * breadth
+        top = south_ref[1] + row * third_y - row * height
+        for m in range(third_y):
+            place_row(out_ref, levels, top + m, start, blend_ref[m])
+
 
 def last_kernel(
-    levels, west_ref, south_ref, parent_ref, nested_ref, speeds_ref, blend_ref, rows_ref, out_hbm, out_ref, sems
+    levels, west_ref, south_ref, given_ref, speeds_ref, blend_ref, rows_ref, out_hbm, out_ref, sems
 ):
-    pieces, size, _ = parent_ref.shape
+    pieces, size, _ = given_ref.shape
     breadth = pieces * LANES
     height = size // levels
     third_y = height // 3
     tile, row, _ = place()
     nest = tile == lax.axis_size("tiles") - 1
+    out_ref[...] = given_ref[...]
 
     @pl.when(nest)
     def _():
-        out_ref[...] = nested_ref[...]
         inner = inner_line(height, row)
         halo = ghost_weight(join_slabs(speeds_ref, pieces, pieces), row == 1) * join_slabs(rows_ref, 0, pieces)
         store_line(out_ref, levels, inner, load_line(out_ref, levels, inner) + halo)
 
     @pl.when(jnp.logical_not(nest))
     def _():
-        out_ref[...] = parent_ref[...]
         start = west_ref[1] - tile * breadth
-        top = south_ref[1] - row * height
-        lane = iota((levels, breadth), 1)
-        inside = (lane >= start) & (lane < start + LANES)
-        turn = lax.rem(start + 4 * breadth, breadth)
-        empty = jnp.zeros((levels, breadth - LANES), jnp.float32)
-        for block in range(2):
-            for m in range(third_y):
-                line = top + block * third_y + m
-
-                @pl.when((line >= 0) & (line < height))
-                def _():
-                    value = jnp.where(row == block, blend_ref[m], rows_ref[m])
-                    if m == (third_y - 1 if block == 0 else 0):
-                        value = value + jnp.where(row == block, rows_ref[third_y], blend_ref[third_y])
-                    wide = pltpu.roll(jnp.concatenate([value, empty], axis=1), turn, 1)
-                    kept = load_line(out_ref, levels, line)
-                    store_line(out_ref, levels, line, jnp.where(inside, wide, kept))
+        top = south_ref[1] + (1 - row) * third_y - row * height
+        for m in range(third_y):
+            value = rows_ref[m]
+            if m == 0:
+                value = value + jnp.where(row == 0, blend_ref[third_y], 0.0)
+            if m == third_y - 1:
+                value = value + jnp.where(row == 1, blend_ref[third_y], 0.0)
+            place_row(out_ref, levels, top + m, start, value)
+        near = jnp.where(row == 0, third_y - 1, 0)
+        line = south_ref[1] + row * third_y - row * height + near
+        place_row(out_ref, levels, line, start, blend_ref[near] + rows_ref[third_y])
 
     copies = [
         pltpu.make_async_copy(out_ref.at[c], out_hbm.at[:, pl.ds(c * LANES, LANES)], sems.at[c])
@@ -777,16 +837,20 @@
         copy.wait()
 
 
-def call(kernel, outs, inputs, places, scratch=(), flops=0, out_place="v"):
+def call(kernel, outs, inputs, places, scratch=(), flops=0, out_place="v", room=32 * 1024):
     spaces = {"s": pltpu.SMEM, "v": pltpu.VMEM, "h": pltpu.HBM}
     moved = sum(4 * math.prod(shape) for shape in outs) + sum(array.nbytes for array in inputs)
+    inputs = [
+        pltpu.with_memory_space_constraint(array, pltpu.HBM) if p == "h" else array
+        for array, p in zip(inputs, places)
+    ]
     return pl.pallas_call(
         kernel,
-        out_shape=[jax.ShapeDtypeStruct(shape, jnp.float32) for shape in outs],
+        out_shape=[spaces[out_place](shape, jnp.float32) for shape in outs],
         in_specs=[pl.BlockSpec(memory_space=spaces[p]) for p in places],
         out_specs=[pl.BlockSpec(memory_space=spaces[out_place])] * len(outs),
         scratch_shapes=[pltpu.VMEM(s, jnp.float32) if isinstance(s, tuple) else s for s in scratch],
-        compiler_params=pltpu.CompilerParams(vmem_limit_bytes=32 * 1024 * 1024),
+        compiler_params=pltpu.CompilerParams(vmem_limit_bytes=room * 1024),
         cost_estimate=pl.CostEstimate(flops=flops, bytes_accessed=moved, transcendentals=0),
     )(*inputs)
 
@@ -796,16 +860,12 @@
     third_y = height // 3
     pieces = breadth // LANES
     slots = third_y + 2
-    tile_count = lax.axis_size("tiles")
     size = levels * height
     flat = (size, breadth)
     chunked = (pieces, size, LANES)
     air, east, north = (array.reshape(flat) for array in (air_state, wind_east, wind_north))
     weight = jnp.broadcast_to(feedback_weight[:, None], (levels, LANES))
     swap = [(0, 1), (1, 0)]
-    last = tile_count - 1
-    near = [(0, 1), (1, 0)]
-    across = [(1, 2), (2, 1)]
 
     def slabs(count):
         return (count, levels, LANES)
@@ -813,72 +873,73 @@
     def kernel(body):
         return functools.partial(body, levels)
 
-    rows, own, edges, level = call(
+    rows, own, level, speeds = call(
         kernel(pack_kernel),
-        [slabs(slots + 1 + pieces), slabs(slots + 1), (levels, LANES), (height, breadth)],
-        [nest_west, nest_south, air, north],
-        "hhhh",
+        [slabs(slots + 1 + pieces), slabs(slots + 1), (height, breadth), slabs(2 * pieces)],
+        [nest_west, nest_south, air, east, north],
+        "hhhhh",
         [
             pltpu.SMEM((2,), jnp.int32),
             pltpu.SMEM((2,), jnp.int32),
             chunked,
             chunked,
-            pltpu.SemaphoreType.DMA((2 * pieces + 2,)),
+            chunked,
+            pltpu.SemaphoreType.DMA((3 * pieces + 2,)),
         ],
     )
     rows = lax.ppermute(rows, "rows", swap)
-    even = lax.ppermute(edges, "tiles", near)
-    odd = lax.ppermute(edges, "tiles", across)
     level = lax.ppermute(level, "lev", swap)
-    window = own + rows[: slots + 1]
-    speeds = own
-    received = [lax.ppermute(window, "tiles", [(last - step, last)]) for step in (1, 2, 3)]
+    pairs = [[(0, 1), (1, 0), (2, 3), (3, 2)], [(1, 3), (3, 1)], [(0, 3), (3, 0), (1, 2), (2, 1)]]
+
+    def over_tiles(message):
+        return [lax.ppermute(message, "tiles", pair) for pair in pairs]
+
+    starting = over_tiles(own + rows[: slots + 1])
     sides = [(size, LANES), (levels, breadth), (levels, breadth)]
-    early, own, other, coef = call(
+    early, own, other = call(
         kernel(early_kernel),
-        [chunked, slabs(slots + 1), slabs(slots + 1), slabs(4)],
-        [nest_west, nest_south, air, east, north, rows, level, even, odd, speeds],
-        "ssvvvvvvvv",
+        [chunked, slabs(slots + 1), slabs(slots + 1)],
+        [nest_west, nest_south, air, east, north, rows, level, starting[0], starting[2]],
+        "ssvvvvvvv",
         sides,
         flops=30 * size * breadth,
     )
     other = lax.ppermute(other, "rows", swap)
-    first, edge, window = call(
+    first, edge = call(
         kernel(first_kernel),
-        [chunked, (height, breadth), slabs(slots + 1)],
-        [early, east, speeds, *received, own, other],
-        "vvvvvvvv",
+        [chunked, (height, breadth)],
+        [early, east, speeds, *starting],
+        "vvvvvv",
     )
     level = lax.ppermute(edge, "lev", swap)
     (message,) = call(
         kernel(average_kernel),
-        [slabs(third_y + 5)],
-        [first, east, north, rows, level, coef, window],
+        [slabs(slots + 1)],
+        [first, east, north, rows, level, own, other],
         "vvvvvvv",
         [flat],
     )
-    pairs = [[(0, 1), (1, 0), (2, 3), (3, 2)], [(1, 3), (3, 1)], [(0, 3), (3, 0), (1, 2), (2, 1)]]
-    received = [lax.ppermute(message, "tiles", pair) for pair in pairs]
+    received = over_tiles(message)
     (blend,) = call(
         kernel(blend_kernel),
         [slabs(third_y + 1)],
-        [weight, first, window, *received],
-        "vvvvvv",
+        [weight, first, message, *received, *starting],
+        "v" * 9,
     )
     rows = lax.ppermute(blend, "rows", swap)
     (later,) = call(
         kernel(later_kernel),
         [chunked],
-        [first, east, north, level, *received],
-        "vvvvvvv",
+        [nest_west, nest_south, first, east, north, level, *received, early, blend],
+        "ss" + "v" * 9,
         [flat, *sides],
         flops=30 * size * breadth,
     )
     (out,) = call(
         kernel(last_kernel),
         [flat],
-        [nest_west, nest_south, early, later, speeds, blend, rows],
-        "ssvvvvv",
+        [nest_west, nest_south, later, speeds, blend, rows],
+        "ssvvvv",
         [chunked, pltpu.SemaphoreType.DMA((pieces,))],
         out_place="h",
     )

time: 43 us -> 38.9 us (0.905); the launches traced: 42.4 us -> 38.8 us
  starting transfers between devices: 20.5 us -> 17.6 us
  local copies, waits for them, and re-layouts: 2.88 us -> 0.1 us
  waiting for transfers between devices: 12.4 us -> 14.6 us
    ppermute x8 -> x6, starting transfers between devices: 16 us -> 11.5 us  [over_tiles(): return [lax.ppermute(message, 'tiles', pair) for pair in pairs]]
    ppermute x1, waiting for transfers between devices: 0.01 us -> 3.15 us  [per_device_paired(): rows = lax.ppermute(rows, 'rows', swap)]
    ppermute x8 -> x6, waiting for transfers between devices: 3.02 us -> 5.82 us  [over_tiles(): return [lax.ppermute(message, 'tiles', pair) for pair in pairs]]
    unnamed x14 -> x12, local copies, waits for them, and re-layouts: 2.81 us -> 0.03 us
    ppermute x1, waiting for transfers between devices: 4.19 us -> 1.82 us  [per_device_paired(): other = lax.ppermute(other, 'rows', swap)]
    ppermute x1, waiting for transfers between devices: 3.97 us -> 2.09 us  [per_device_paired(): rows = lax.ppermute(blend, 'rows', swap)]
    ppermute x1, starting transfers between devices: 0.45 us -> 1.55 us  [per_device_paired(): rows = lax.ppermute(blend, 'rows', swap)]
    ppermute x1, starting transfers between devices: 0.88 us -> 1.55 us  [per_device_paired(): other = lax.ppermute(other, 'rows', swap)]
  transfers between devices with their start and end apart: 13 -> 11, of which waited for: 5 -> 9; matrix products, arithmetic and copies ran while one was open for 0% -> 0% of each run, Pallas kernels for 6% -> 6%
where the time goes in v3:
time: 38.9 us; the launch traced here: 38.8 us
  starting transfers between devices  17.6 us (45%)
  waiting for transfers between devices  14.6 us (38%)
  Pallas kernels  6.29 us (16%)
    ppermute x6, starting transfers between devices, over_tiles(): return [lax.ppermute(message, 'tiles', pair) for pair in pairs]  11.5 us
    pallas_call x7, Pallas kernels, call(): pl.pallas_call(kernel, out_shape=[spaces[out_place](shape, jnp.float32) f...  6.29 us
    ppermute x6, waiting for transfers between devices, over_tiles(): return [lax.ppermute(message, 'tiles', pair) for pair in pairs]  5.82 us
    ppermute x1, waiting for transfers between devices, per_device_paired(): rows = lax.ppermute(rows, 'rows', swap)  3.15 us
    ppermute x1, starting transfers between devices, per_device_paired(): rows = lax.ppermute(rows, 'rows', swap)  3.01 us
    ppermute x1, waiting for transfers between devices, per_device_paired(): rows = lax.ppermute(blend, 'rows', swap)  2.09 us
    ppermute x1, waiting for transfers between devices, per_device_paired(): other = lax.ppermute(other, 'rows', swap)  1.82 us
    ppermute x1, starting transfers between devices, per_device_paired(): other = lax.ppermute(other, 'rows', swap)  1.55 us
  transfers between devices with their start and end apart: 11, of which 9 were waited for; matrix products, arithmetic and copies ran while one was open for 0% of the time, Pallas kernels for 6%

profile of v3, /device:TPU:0, one launch (start us, length us, event | category | flops | bytes accessed | tf_op | source)
XLA Modules:
  0.0 38.8 jit_solution(14974880643494813076)
XLA Ops:
  0.0 1.7 %shard_map.64 = (f32[14,16,128]{2,1,0:T(8,128)S(1)}, f32[11,16,128]{2,1,0:T(8,128)S(1)}, f32[24,384]{1,0:T(8,128)S(1)}, f32[6,16,128]{2,1,0:T(8,128)S(1)}) custom-call(s32[2]{0:T(128)} %west_ref.5, s32[2]{0:T(128)} %south_ref.5, f32[384,384]{1,0:T(8,128)} %bitcast.13, f32[384,384]{1,0:T(8,128)} %bitcast.4, f32[384,384]{1,0:T(8,128)} %bitcast.9), custom_call_target="tpu_custom_call" | custom-call | bytes 2060304 | tf_op jit(solution)/shard_map/pallas_call | solution.py:847
  1.8 3.0 %collective-permute-start = (f32[14,16,128]{2,1,0:T(8,128)S(1)}, f32[14,16,128]{2,1,0:T(8,128)S(1)}, u32[]{:S(2)}, u32[]{:S(2)}) collective-permute-start(f32[14,16,128]{2,1,0:T(8,128)S(1)} %get-tuple-element.14), channel_id=1, source_target_pairs={{0,2},{2,0},{1,3},{3,1},{4,6},{6,4},{5,7},{7,5},{8,10},{10,8},{9,1... | collective-permute-start | bytes 344072 | tf_op jit(solution)/shard_map/ppermute | solution.py:890
  4.8 3.1 %collective-permute-done.rows_ref = f32[14,16,128]{2,1,0:T(8,128)S(1)} collective-permute-done((f32[14,16,128]{2,1,0:T(8,128)S(1)}, f32[14,16,128]{2,1,0:T(8,128)S(1)}, u32[]{:S(2)}, u32[]{:S(2)}) %collective-permute-start) | collective-permute-done | bytes 114720 | tf_op jit(solution)/shard_map/ppermute | solution.py:890
  7.9 0.0 copy-start.4
  8.0 4.4 %collective-permute-start.3 = (f32[11,16,128]{2,1,0:T(8,128)S(1)}, f32[11,16,128]{2,1,0:T(8,128)S(1)}, u32[]{:S(2)}, u32[]{:S(2)}) collective-permute-start(f32[11,16,128]{2,1,0:T(8,128)S(1)} %slice_add_fusion), channel_id=1, source_target_pairs={{0,12},{12,0},{4,8},{8,4},{1,13},{13,1},{5,9},{9,5},{2,14},{14,2},... | collective-permute-start | bytes 270344 | tf_op jit(solution)/shard_map/ppermute | solution.py:895
  12.4 0.7 %collective-permute-start.4 = (f32[11,16,128]{2,1,0:T(8,128)S(1)}, f32[11,16,128]{2,1,0:T(8,128)S(1)}, u32[]{:S(2)}, u32[]{:S(2)}) collective-permute-start(f32[11,16,128]{2,1,0:T(8,128)S(1)} %slice_add_fusion), channel_id=1, source_target_pairs={{4,12},{12,4},{5,13},{13,5},{6,14},{14,6},{7,15},{15,7},{20,28},{2... | collective-permute-start | bytes 270344 | tf_op jit(solution)/shard_map/ppermute | solution.py:895
  13.1 0.5 %collective-permute-done.1.level_ref = f32[24,384]{1,0:T(8,128)S(1)} collective-permute-done((f32[24,384]{1,0:T(8,128)S(1)}, f32[24,384]{1,0:T(8,128)S(1)}, u32[]{:S(2)}, u32[]{:S(2)}) %collective-permute-start.1) | collective-permute-done | bytes 36896 | tf_op jit(solution)/shard_map/ppermute | solution.py:891
  13.6 1.6 %collective-permute-done.3.three_ref.coef_three_ref = f32[11,16,128]{2,1,0:T(8,128)S(1)} collective-permute-done((f32[11,16,128]{2,1,0:T(8,128)S(1)}, f32[11,16,128]{2,1,0:T(8,128)S(1)}, u32[]{:S(2)}, u32[]{:S(2)}) %collective-permute-start.3) | collective-permute-done | bytes 90144 | tf_op jit(solution)/shard_map/ppermute | solution.py:895
  15.2 1.7 %collective-permute-done.2.one_ref.coef_one_ref = f32[11,16,128]{2,1,0:T(8,128)S(1)} collective-permute-done((f32[11,16,128]{2,1,0:T(8,128)S(1)}, f32[11,16,128]{2,1,0:T(8,128)S(1)}, u32[]{:S(2)}, u32[]{:S(2)}) %collective-permute-start.2) | collective-permute-done | bytes 90144 | tf_op jit(solution)/shard_map/ppermute | solution.py:895
  16.9 1.7 %shard_map.65 = (f32[3,384,128]{2,1,0:T(8,128)S(1)}, f32[11,16,128]{2,1,0:T(8,128)S(1)}, f32[11,16,128]{2,1,0:T(8,128)S(1)}) custom-call(s32[2]{0:T(128)S(1)} %copy-done.3, s32[2]{0:T(128)S(1)} %copy-done.4, f32[384,384]{1,0:T(8,128)S(1)} %bitcast.14, f32[384,384]{1,0:T(8,128)S(1)} %bitcast.5, f32[384,384]{1,0:T(8,128)S(1)} %bitcast.10, ...), custom_call_target="tpu_custom_call" | custom-call | flops 4423680 | bytes 2871312 | tf_op jit(solution)/shard_map/pallas_call | solution.py:847
  18.7 1.6 %collective-permute-start.6 = (f32[11,16,128]{2,1,0:T(8,128)S(1)}, f32[11,16,128]{2,1,0:T(8,128)S(1)}, u32[]{:S(2)}, u32[]{:S(2)}) collective-permute-start(f32[11,16,128]{2,1,0:T(8,128)S(1)} %get-tuple-element.22), channel_id=1, source_target_pairs={{0,2},{2,0},{1,3},{3,1},{4,6},{6,4},{5,7},{7,5},{8,10},{10,8},{9,1... | collective-permute-start | bytes 270344 | tf_op jit(solution)/shard_map/ppermute | solution.py:907
  20.3 1.2 %collective-permute-done.5.level_ref = f32[24,384]{1,0:T(8,128)S(1)} collective-permute-done((f32[24,384]{1,0:T(8,128)S(1)}, f32[24,384]{1,0:T(8,128)S(1)}, u32[]{:S(2)}, u32[]{:S(2)}) %collective-permute-start.5) | collective-permute-done | bytes 36896 | tf_op jit(solution)/shard_map/ppermute | solution.py:914
  21.5 1.8 %collective-permute-done.6.other_ref = f32[11,16,128]{2,1,0:T(8,128)S(1)} collective-permute-done((f32[11,16,128]{2,1,0:T(8,128)S(1)}, f32[11,16,128]{2,1,0:T(8,128)S(1)}, u32[]{:S(2)}, u32[]{:S(2)}) %collective-permute-start.6) | collective-permute-done | bytes 90144 | tf_op jit(solution)/shard_map/ppermute | solution.py:907
  23.3 2.7 %collective-permute-start.9 = (f32[11,16,128]{2,1,0:T(8,128)S(1)}, f32[11,16,128]{2,1,0:T(8,128)S(1)}, u32[]{:S(2)}, u32[]{:S(2)}) collective-permute-start(f32[11,16,128]{2,1,0:T(8,128)S(1)} %shard_map.67.window_ref), channel_id=1, source_target_pairs={{0,12},{12,0},{4,8},{8,4},{1,13},{13,1},{5,9},{9,5},{2,14},{14,2},... | collective-permute-start | bytes 270344 | tf_op jit(solution)/shard_map/ppermute | solution.py:895
  26.0 0.7 %collective-permute-start.8 = (f32[11,16,128]{2,1,0:T(8,128)S(1)}, f32[11,16,128]{2,1,0:T(8,128)S(1)}, u32[]{:S(2)}, u32[]{:S(2)}) collective-permute-start(f32[11,16,128]{2,1,0:T(8,128)S(1)} %shard_map.67.window_ref), channel_id=1, source_target_pairs={{4,12},{12,4},{5,13},{13,5},{6,14},{14,6},{7,15},{15,7},{20,28},{2... | collective-permute-start | bytes 270344 | tf_op jit(solution)/shard_map/ppermute | solution.py:895
  26.6 3.1 %collective-permute-start.7 = (f32[11,16,128]{2,1,0:T(8,128)S(1)}, f32[11,16,128]{2,1,0:T(8,128)S(1)}, u32[]{:S(2)}, u32[]{:S(2)}) collective-permute-start(f32[11,16,128]{2,1,0:T(8,128)S(1)} %shard_map.67.window_ref), channel_id=1, source_target_pairs={{0,4},{4,0},{8,12},{12,8},{1,5},{5,1},{9,13},{13,9},{2,6},{6,2},{1... | collective-permute-start | bytes 270344 | tf_op jit(solution)/shard_map/ppermute | solution.py:895
  29.7 1.0 %collective-permute-done.9.three_ref = f32[11,16,128]{2,1,0:T(8,128)S(1)} collective-permute-done((f32[11,16,128]{2,1,0:T(8,128)S(1)}, f32[11,16,128]{2,1,0:T(8,128)S(1)}, u32[]{:S(2)}, u32[]{:S(2)}) %collective-permute-start.9) | collective-permute-done | bytes 90144 | tf_op jit(solution)/shard_map/ppermute | solution.py:895
  30.7 1.5 %collective-permute-done.7.one_ref = f32[11,16,128]{2,1,0:T(8,128)S(1)} collective-permute-done((f32[11,16,128]{2,1,0:T(8,128)S(1)}, f32[11,16,128]{2,1,0:T(8,128)S(1)}, u32[]{:S(2)}, u32[]{:S(2)}) %collective-permute-start.7) | collective-permute-done | bytes 90144 | tf_op jit(solution)/shard_map/ppermute | solution.py:895
  32.2 0.1 broadcast_in_dim.2.weight_ref
  32.3 0.4 shard_map.68.blend_ref
  32.7 1.6 %collective-permute-start.10 = (f32[9,16,128]{2,1,0:T(8,128)S(1)}, f32[9,16,128]{2,1,0:T(8,128)S(1)}, u32[]{:S(2)}, u32[]{:S(2)}) collective-permute-start(f32[9,16,128]{2,1,0:T(8,128)S(1)} %shard_map.68.blend_ref), channel_id=1, source_target_pairs={{0,2},{2,0},{1,3},{3,1},{4,6},{6,4},{5,7},{7,5},{8,10},{10,8},{9,1... | collective-permute-start | bytes 221192 | tf_op jit(solution)/shard_map/ppermute | solution.py:929
  34.2 0.8 %shard_map.69.given_ref = f32[3,384,128]{2,1,0:T(8,128)S(1)} custom-call(s32[2]{0:T(128)S(1)} %copy-done.3, s32[2]{0:T(128)S(1)} %copy-done.4, f32[3,384,128]{2,1,0:T(8,128)S(1)} %get-tuple-element.19.field_ref, f32[384,384]{1,0:T(8,128)S(1)} %bitcast.8, f32[384,384]{1,0:T(8,128)S(1)} %bitcast.12, f32[24,384]{1,0:T(8,128)S(1)} %collective-permute-done.5.level_ref, ...), custom_call_target="tpu_custom_call" | custom-call | flops 4423680 | bytes 3330064 | tf_op jit(solution)/shard_map/pallas_call | solution.py:847
  35.0 2.1 %collective-permute-done.10.rows_ref = f32[9,16,128]{2,1,0:T(8,128)S(1)} collective-permute-done((f32[9,16,128]{2,1,0:T(8,128)S(1)}, f32[9,16,128]{2,1,0:T(8,128)S(1)}, u32[]{:S(2)}, u32[]{:S(2)}) %collective-permute-start.10) | collective-permute-done | bytes 73760 | tf_op jit(solution)/shard_map/ppermute | solution.py:929
  37.1 1.6 %shard_map.70 = f32[384,384]{1,0:T(8,128)} custom-call(s32[2]{0:T(128)S(1)} %copy-done.3, s32[2]{0:T(128)S(1)} %copy-done.4, f32[3,384,128]{2,1,0:T(8,128)S(1)} %shard_map.69.given_ref, f32[6,16,128]{2,1,0:T(8,128)S(1)} %get-tuple-element.18.speeds_ref, f32[9,16,128]{2,1,0:T(8,128)S(1)} %shard_map.68.blend_ref, ...), custom_call_target="tpu_custom_call" | custom-call | bytes 1376272 | tf_op jit(solution)/shard_map/pallas_call | solution.py:847
  (19 shorter events, 0.1 us)
Async XLA Ops:
  0.0 16.9 %copy-start = (f32[16,24,384]{2,1,0:T(8,128)S(1)}, f32[16,24,384]{2,1,0:T(8,128)}, u32[]{:S(2)}) copy-start(f32[16,24,384]{2,1,0:T(8,128)} %param.7) | copy-start | bytes 1769476
  0.0 16.9 %copy-start.1 = (f32[16,24,384]{2,1,0:T(8,128)S(1)}, f32[16,24,384]{2,1,0:T(8,128)}, u32[]{:S(2)}) copy-start(f32[16,24,384]{2,1,0:T(8,128)} %param.8) | copy-start | bytes 1769476
  0.0 16.9 %copy-start.2 = (f32[16,24,384]{2,1,0:T(8,128)S(1)}, f32[16,24,384]{2,1,0:T(8,128)}, u32[]{:S(2)}) copy-start(f32[16,24,384]{2,1,0:T(8,128)} %param.6) | copy-start | bytes 1769476
  1.8 6.2 %collective-permute-start = (f32[14,16,128]{2,1,0:T(8,128)S(1)}, f32[14,16,128]{2,1,0:T(8,128)S(1)}, u32[]{:S(2)}, u32[]{:S(2)}) collective-permute-start(f32[14,16,128]{2,1,0:T(8,128)S(1)} %get-tuple-element.14), channel_id=1, source_target_pairs={{0,2},{2,0},{1,3},{3,1},{4,6},{6,4},{5,7},{7,5},{8,10},{10,8},{9,1... | collective-permute-start | bytes 344072 | tf_op jit(solution)/shard_map/ppermute | solution.py:890
  7.9 9.0 %copy-start.3 = (s32[2]{0:T(128)S(1)}, s32[2]{0:T(128)}, u32[]{:S(2)}) copy-start(s32[2]{0:T(128)} %west_ref.5) | copy-start | bytes 28
  7.9 9.0 %copy-start.4 = (s32[2]{0:T(128)S(1)}, s32[2]{0:T(128)}, u32[]{:S(2)}) copy-start(s32[2]{0:T(128)} %south_ref.5) | copy-start | bytes 28
  8.0 7.2 %collective-permute-start.3 = (f32[11,16,128]{2,1,0:T(8,128)S(1)}, f32[11,16,128]{2,1,0:T(8,128)S(1)}, u32[]{:S(2)}, u32[]{:S(2)}) collective-permute-start(f32[11,16,128]{2,1,0:T(8,128)S(1)} %slice_add_fusion), channel_id=1, source_target_pairs={{0,12},{12,0},{4,8},{8,4},{1,13},{13,1},{5,9},{9,5},{2,14},{14,2},... | collective-permute-start | bytes 270344 | tf_op jit(solution)/shard_map/ppermute | solution.py:895
  12.4 4.5 %collective-permute-start.2 = (f32[11,16,128]{2,1,0:T(8,128)S(1)}, f32[11,16,128]{2,1,0:T(8,128)S(1)}, u32[]{:S(2)}, u32[]{:S(2)}) collective-permute-start(f32[11,16,128]{2,1,0:T(8,128)S(1)} %slice_add_fusion), channel_id=1, source_target_pairs={{0,4},{4,0},{8,12},{12,8},{1,5},{5,1},{9,13},{13,9},{2,6},{6,2},{1... | collective-permute-start | bytes 270344 | tf_op jit(solution)/shard_map/ppermute | solution.py:895
  12.4 1.2 %collective-permute-start.1 = (f32[24,384]{1,0:T(8,128)S(1)}, f32[24,384]{1,0:T(8,128)S(1)}, u32[]{:S(2)}, u32[]{:S(2)}) collective-permute-start(f32[24,384]{1,0:T(8,128)S(1)} %get-tuple-element.15), channel_id=1, source_target_pairs={{0,1},{1,0},{2,3},{3,2},{4,5},{5,4},{6,7},{7,6},{8,9},{9,8},{10,11... | collective-permute-start | bytes 110600 | tf_op jit(solution)/shard_map/ppermute | solution.py:891
  12.4 7.9 %collective-permute-start.4 = (f32[11,16,128]{2,1,0:T(8,128)S(1)}, f32[11,16,128]{2,1,0:T(8,128)S(1)}, u32[]{:S(2)}, u32[]{:S(2)}) collective-permute-start(f32[11,16,128]{2,1,0:T(8,128)S(1)} %slice_add_fusion), channel_id=1, source_target_pairs={{4,12},{12,4},{5,13},{13,5},{6,14},{14,6},{7,15},{15,7},{20,28},{2... | collective-permute-start | bytes 270344 | tf_op jit(solution)/shard_map/ppermute | solution.py:895
  18.7 4.6 %collective-permute-start.6 = (f32[11,16,128]{2,1,0:T(8,128)S(1)}, f32[11,16,128]{2,1,0:T(8,128)S(1)}, u32[]{:S(2)}, u32[]{:S(2)}) collective-permute-start(f32[11,16,128]{2,1,0:T(8,128)S(1)} %get-tuple-element.22), channel_id=1, source_target_pairs={{0,2},{2,0},{1,3},{3,1},{4,6},{6,4},{5,7},{7,5},{8,10},{10,8},{9,1... | collective-permute-start | bytes 270344 | tf_op jit(solution)/shard_map/ppermute | solution.py:907
  20.2 1.2 %collective-permute-start.5 = (f32[24,384]{1,0:T(8,128)S(1)}, f32[24,384]{1,0:T(8,128)S(1)}, u32[]{:S(2)}, u32[]{:S(2)}) collective-permute-start(f32[24,384]{1,0:T(8,128)S(1)} %get-tuple-element.20), channel_id=1, source_target_pairs={{0,1},{1,0},{2,3},{3,2},{4,5},{5,4},{6,7},{7,6},{8,9},{9,8},{10,11... | collective-permute-start | bytes 110600 | tf_op jit(solution)/shard_map/ppermute | solution.py:914
  23.3 9.0 %copy-start.5 = (f32[16]{0:T(128)S(1)}, f32[16]{0:T(128)}, u32[]{:S(2)}) copy-start(f32[16]{0:T(128)} %param.9) | copy-start | bytes 196
  23.3 7.4 %collective-permute-start.9 = (f32[11,16,128]{2,1,0:T(8,128)S(1)}, f32[11,16,128]{2,1,0:T(8,128)S(1)}, u32[]{:S(2)}, u32[]{:S(2)}) collective-permute-start(f32[11,16,128]{2,1,0:T(8,128)S(1)} %shard_map.67.window_ref), channel_id=1, source_target_pairs={{0,12},{12,0},{4,8},{8,4},{1,13},{13,1},{5,9},{9,5},{2,14},{14,2},... | collective-permute-start | bytes 270344 | tf_op jit(solution)/shard_map/ppermute | solution.py:895
  26.0 4.7 %collective-permute-start.8 = (f32[11,16,128]{2,1,0:T(8,128)S(1)}, f32[11,16,128]{2,1,0:T(8,128)S(1)}, u32[]{:S(2)}, u32[]{:S(2)}) collective-permute-start(f32[11,16,128]{2,1,0:T(8,128)S(1)} %shard_map.67.window_ref), channel_id=1, source_target_pairs={{4,12},{12,4},{5,13},{13,5},{6,14},{14,6},{7,15},{15,7},{20,28},{2... | collective-permute-start | bytes 270344 | tf_op jit(solution)/shard_map/ppermute | solution.py:895
  26.6 5.6 %collective-permute-start.7 = (f32[11,16,128]{2,1,0:T(8,128)S(1)}, f32[11,16,128]{2,1,0:T(8,128)S(1)}, u32[]{:S(2)}, u32[]{:S(2)}) collective-permute-start(f32[11,16,128]{2,1,0:T(8,128)S(1)} %shard_map.67.window_ref), channel_id=1, source_target_pairs={{0,4},{4,0},{8,12},{12,8},{1,5},{5,1},{9,13},{13,9},{2,6},{6,2},{1... | collective-permute-start | bytes 270344 | tf_op jit(solution)/shard_map/ppermute | solution.py:895
  32.7 4.4 %collective-permute-start.10 = (f32[9,16,128]{2,1,0:T(8,128)S(1)}, f32[9,16,128]{2,1,0:T(8,128)S(1)}, u32[]{:S(2)}, u32[]{:S(2)}) collective-permute-start(f32[9,16,128]{2,1,0:T(8,128)S(1)} %shard_map.68.blend_ref), channel_id=1, source_target_pairs={{0,2},{2,0},{1,3},{3,1},{4,6},{6,4},{5,7},{7,5},{8,10},{10,8},{9,1... | collective-permute-start | bytes 221192 | tf_op jit(solution)/shard_map/ppermute | solution.py:929

commit v4 on v3

--- a/solution.py
+++ b/solution.py
@@ -457,79 +457,95 @@
 
 
 def pack_kernel(
-    levels,
-    west_hbm,
-    south_hbm,
-    air_hbm,
-    east_hbm,
-    north_hbm,
-    rows_ref,
-    own_ref,
-    level_ref,
-    speeds_ref,
-    west_ref,
-    south_ref,
-    air_ref,
-    east_ref,
-    north_ref,
-    sems,
+    levels, west_hbm, south_hbm, air_hbm, rows_ref, air_ref, west_ref, south_ref, sems
 ):
     pieces, size, _ = air_ref.shape
-    height, breadth = level_ref.shape
+    breadth = pieces * LANES
+    height = size // levels
+    third_y = height // 3
+    slots = rows_ref.shape[0] - 1 - pieces
+    tile, row, _ = place()
+    nest = tile == lax.axis_size("tiles") - 1
+    copies = [
+        pltpu.make_async_copy(air_hbm.at[:, pl.ds(c * LANES, LANES)], air_ref.at[c], sems.at[c])
+        for c in range(pieces)
+    ]
+    copies.append(pltpu.make_async_copy(west_hbm, west_ref, sems.at[pieces]))
+    copies.append(pltpu.make_async_copy(south_hbm, south_ref, sems.at[pieces + 1]))
+    for copy in copies:
+        copy.start()
+    for copy in copies:
+        copy.wait()
+    store_slabs(rows_ref, slots + 1, load_line(air_ref, levels, inner_line(height, row)))
+    part = rows_ref.at[pl.ds(0, slots + 1)]
+
+    @pl.when(nest)
+    def _():
+        part[...] = jnp.zeros_like(part)
+
+    @pl.when(jnp.logical_not(nest))
+    def _():
+        start = west_ref[0] - tile * breadth
+        top = south_ref[0] - 1 - row * height
+        pack_window(part, air_ref, levels, top + (1 - row) * third_y, start)
+
+
+def own_kernel(levels, west_ref, south_ref, air_ref, east_ref, north_ref, own_ref, level_ref, speeds_ref):
+    pieces, size, _ = air_ref.shape
+    breadth = pieces * LANES
+    height = size // levels
     third_y = height // 3
     slots = own_ref.shape[0] - 1
     tile, row, lev = place()
     nest = tile == lax.axis_size("tiles") - 1
-
-    def column_copies(source, target, first):
-        return [
-            pltpu.make_async_copy(source.at[:, pl.ds(c * LANES, LANES)], target.at[c], sems.at[first + c])
-            for c in range(pieces)
-        ]
-
-    copies = column_copies(air_hbm, air_ref, 0)
-    copies.append(pltpu.make_async_copy(west_hbm, west_ref, sems.at[3 * pieces]))
-    copies.append(pltpu.make_async_copy(south_hbm, south_ref, sems.at[3 * pieces + 1]))
-    speeds = column_copies(east_hbm, east_ref, pieces) + column_copies(north_hbm, north_ref, 2 * pieces)
-    for copy in copies:
-        copy.start()
+    level_ref[...] = edge_level(air_ref, height, lev)
 
     @pl.when(nest)
     def _():
-        for copy in speeds:
-            copy.start()
-
-    for copy in copies:
-        copy.wait()
-    inner = inner_line(height, row)
-    level_ref[...] = edge_level(air_ref, height, lev)
-    store_slabs(rows_ref, slots + 1, load_line(air_ref, levels, inner))
-
-    @pl.when(nest)
-    def _():
-        for copy in speeds:
-            copy.wait()
-        speed = load_line(north_ref, levels, inner)
-        outer = load_line(north_ref, levels, height - 1 - inner)
+        inner = inner_line(height, row)
+        shape = (2 * levels, size)
+        taken = iota(shape, 0)
+        level, line = split_level(iota(shape, 1), height)
+        wanted = jnp.where(taken < levels, height - 1 - inner, inner)
+        picked = table((lax.rem(taken, levels) == level) & (line == wanted))
+        speeds = from_left(picked, north_ref[...])
+        outer = speeds[:levels]
+        store_slabs(speeds_ref, 0, outer)
+        store_slabs(speeds_ref, pieces, speeds[levels:])
         own_ref[...] = jnp.zeros_like(own_ref)
-        rows_ref[pl.ds(0, slots + 1)] = jnp.zeros_like(own_ref)
-        store_slabs(rows_ref, 4, speed)
-        store_slabs(speeds_ref, 0, outer)
-        store_slabs(speeds_ref, pieces, speed)
         store_slabs(own_ref, 0, ghost_row_weights(ghost_weight(outer, row == 0), breadth))
-        first = ghost_weight(east_ref[0, :, 0:1], True)
-        last = ghost_weight(east_ref[pieces - 1, :, LANES - 1 : LANES], False)
+        first = ghost_weight(east_ref[:, 0:1], True)
+        last = ghost_weight(east_ref[:, breadth - 1 : breadth], False)
         own_ref[3] = ghost_column_weights(first, last, levels, height)
 
     @pl.when(jnp.logical_not(nest))
     def _():
         start = west_ref[0] - tile * breadth
         top = south_ref[0] - 1 - row * height
-        part = rows_ref.at[pl.ds(0, slots + 1)]
-        pack_window(part, air_ref, levels, top + (1 - row) * third_y, start)
         pack_window(own_ref, air_ref, levels, top + row * third_y, start)
         own_ref[slots] = own_ref[slots] + pack_edges(air_ref, levels)
         speeds_ref[...] = jnp.zeros_like(speeds_ref)
+
+
+def set_halo(rows_ref, first, northern_ref, southern_ref, row):
+    halo = join_slabs(rows_ref, first, rows_ref.shape[0] - first)
+    zero = jnp.zeros_like(halo)
+    northern_ref[...] = jnp.where(row == 0, zero, halo)
+    southern_ref[...] = jnp.where(row == 0, halo, zero)
+
+
+def parent_step(
+    levels, west_ref, south_ref, shared, rows_ref, columns, field_ref, other_ref, side_ref, northern_ref, southern_ref
+):
+    height = side_ref.shape[0] // levels
+    slots = other_ref.shape[0] - 1
+    tile, row, lev = place()
+    set_halo(rows_ref, slots + 1, northern_ref, southern_ref, row)
+    side_ref[...] = unpack_edges(columns, levels, height)
+    full_step(field_ref, *shared, levels, lev, False, northern_ref, southern_ref, side_ref, None)
+    start = west_ref[1] - tile * field_ref.shape[0] * LANES
+    top = south_ref[1] - 1 - row * height
+    pack_window(other_ref, field_ref, levels, top + (1 - row) * (height // 3), start)
 
 
 def early_kernel(
@@ -542,47 +558,77 @@
     rows_ref,
     level_ref,
     one_ref,
-    three_ref,
+    speeds_ref,
     field_ref,
-    own_ref,
     other_ref,
     side_ref,
     northern_ref,
     southern_ref,
 ):
-    size, breadth = air_ref.shape
-    height = size // levels
-    third_y = height // 3
-    pieces = breadth // LANES
-    slots = own_ref.shape[0] - 1
+    pieces = field_ref.shape[0]
+    slots = other_ref.shape[0] - 1
     tile_count = lax.axis_size("tiles")
     tile, row, lev = place()
-    nest = tile == tile_count - 1
-    halo = join_slabs(rows_ref, slots + 1, pieces)
-    zero = jnp.zeros_like(halo)
-    northern_ref[...] = jnp.where(row == 0, zero, halo)
-    southern_ref[...] = jnp.where(row == 0, halo, zero)
-    shared = (field_ref, air_ref, east_ref, north_ref, level_ref, levels, lev)
-
-    @pl.when(nest)
-    def _():
-        full_step(*shared, True, northern_ref, southern_ref, None, None)
-        own_ref[...] = jnp.zeros_like(own_ref)
+    shared = (air_ref, east_ref, north_ref, level_ref)
+
+    @pl.when(tile == tile_count - 1)
+    def _():
+        set_halo(rows_ref, slots + 1, northern_ref, southern_ref, row)
+        full_step(field_ref, *shared, levels, lev, True, northern_ref, southern_ref, None, None)
         other_ref[...] = jnp.zeros_like(other_ref)
-
-    @pl.when(jnp.logical_not(nest))
+        other_ref[pl.ds(0, pieces)] = speeds_ref[pl.ds(pieces, pieces)]
+
+    @pl.when(tile == 0)
+    def _():
+        columns = neighbour_columns(one_ref[slots], one_ref[slots], tile_count - 1, tile)
+        refs = (field_ref, other_ref, side_ref, northern_ref, southern_ref)
+        parent_step(levels, west_ref, south_ref, shared, rows_ref, columns, *refs)
+
+
+def middle_kernel(
+    levels,
+    west_ref,
+    south_ref,
+    air_ref,
+    east_ref,
+    north_ref,
+    rows_ref,
+    level_ref,
+    three_ref,
+    one_ref,
+    given_field_ref,
+    given_other_ref,
+    field_ref,
+    other_ref,
+    side_ref,
+    northern_ref,
+    southern_ref,
+):
+    slots = other_ref.shape[0] - 1
+    tile_count = lax.axis_size("tiles")
+    tile, _, _ = place()
+    shared = (air_ref, east_ref, north_ref, level_ref)
+
+    @pl.when((tile > 0) & (tile < tile_count - 1))
     def _():
         columns = neighbour_columns(one_ref[slots], three_ref[slots], tile_count - 1, tile)
-        side_ref[...] = unpack_edges(columns, levels, height)
-        full_step(*shared, False, northern_ref, southern_ref, side_ref, None)
-        start = west_ref[1] - tile * breadth
-        top = south_ref[1] - 1 - row * height
-        pack_window(other_ref, field_ref, levels, top + (1 - row) * third_y, start)
-        pack_window(own_ref, field_ref, levels, top + row * third_y, start)
+        refs = (field_ref, other_ref, side_ref, northern_ref, southern_ref)
+        parent_step(levels, west_ref, south_ref, shared, rows_ref, columns, *refs)
 
 
 def first_kernel(
-    levels, early_ref, east_ref, speeds_ref, one_ref, two_ref, three_ref, field_ref, edge_ref
+    levels,
+    west_ref,
+    south_ref,
+    early_ref,
+    east_ref,
+    speeds_ref,
+    three_ref,
+    two_ref,
+    one_ref,
+    field_ref,
+    edge_ref,
+    own_ref,
 ):
     pieces, size, _ = early_ref.shape
     height, breadth = edge_ref.shape
@@ -593,6 +639,9 @@
     @pl.when(jnp.logical_not(nest))
     def _():
         edge_ref[...] = jnp.zeros_like(edge_ref)
+        start = west_ref[1] - tile * breadth
+        top = south_ref[1] - 1 - row * height
+        pack_window(own_ref, early_ref, levels, top + row * (height // 3), start)
 
     @pl.when(nest)
     def _():
@@ -615,25 +664,17 @@
         edge_ref[...] = edge_level(field_ref, height, lev)
 
 
-def average_kernel(
-    levels, field_ref, east_ref, north_ref, rows_ref, level_ref, own_ref, other_ref, message_ref, part_ref
-):
+def average_kernel(levels, field_ref, east_ref, north_ref, other_ref, message_ref, part_ref, nothing_ref):
     pieces, size, _ = field_ref.shape
-    height, breadth = level_ref.shape
+    height, breadth = nothing_ref.shape
     third_y = height // 3
     tile, row, lev = place()
-    nest = tile == lax.axis_size("tiles") - 1
-
-    @pl.when(jnp.logical_not(nest))
-    def _():
-        message_ref[...] = own_ref[...] + other_ref[...]
-
-    @pl.when(nest)
-    def _():
-        full_step(part_ref, field_ref, east_ref, north_ref, level_ref, levels, lev, True, None, None, None, None)
-        cell, third = iota((breadth, LANES), 0), iota((breadth, LANES), 1)
-        offset = cell - 3 * third
-        sums = table((offset >= 0) & (offset <= 2))
+
+    @pl.when(tile == lax.axis_size("tiles") - 1)
+    def _():
+        nothing_ref[...] = jnp.zeros_like(nothing_ref)
+        full_step(part_ref, field_ref, east_ref, north_ref, nothing_ref, levels, lev, True, None, None, None, None)
+        sums = sums_table(breadth)
         shape = (third_y * levels, size)
         taken = iota(shape, 0)
         block = taken // levels
@@ -644,10 +685,37 @@
         for m in range(third_y):
             message_ref[m] = means[m * levels : (m + 1) * levels]
         shared = load_line(field_ref, levels, inner_line(height, row))
-        shared = ghost_weight(join_slabs(rows_ref, 4, pieces), row == 0) * shared
+        shared = ghost_weight(join_slabs(other_ref, 0, pieces), row == 0) * shared
         message_ref[third_y] = from_right(shared, sums) * (1.0 / 9.0)
         for i in range(third_y + 1, message_ref.shape[0]):
             message_ref[i] = jnp.zeros((levels, LANES), jnp.float32)
+
+
+def sums_table(breadth):
+    offset = iota((breadth, LANES), 0) - 3 * iota((breadth, LANES), 1)
+    return table((offset >= 0) & (offset <= 2))
+
+
+def message_kernel(levels, level_ref, part_ref, own_ref, other_ref, message_ref):
+    height, breadth = level_ref.shape
+    third_y = height // 3
+    tile, row, lev = place()
+    nest = tile == lax.axis_size("tiles") - 1
+
+    @pl.when(jnp.logical_not(nest))
+    def _():
+        message_ref[...] = own_ref[...] + other_ref[...]
+
+    @pl.when(nest)
+    def _():
+        offset = iota((third_y, height), 1) - 3 * iota((third_y, height), 0)
+        rows = table((offset >= 0) & (offset <= 2))
+        across = from_left(rows, from_right(level_ref[...], sums_table(breadth))) * (VERTICAL_MIX / 9.0)
+        at_edge = iota((levels, LANES), 0) == jnp.where(lev == 0, levels - 1, 0)
+        for m in range(third_y):
+            message_ref[m] = part_ref[m] + jnp.where(at_edge, across[m : m + 1], 0.0)
+        for i in range(third_y, message_ref.shape[0]):
+            message_ref[i] = part_ref[i]
 
 
 def blend_kernel(
@@ -658,9 +726,9 @@
     one_ref,
     two_ref,
     three_ref,
+    coef_three_ref,
+    coef_two_ref,
     coef_one_ref,
-    coef_two_ref,
-    coef_three_ref,
     rows_ref,
 ):
     pieces, size, _ = field_ref.shape
@@ -837,20 +905,22 @@
         copy.wait()
 
 
-def call(kernel, outs, inputs, places, scratch=(), flops=0, out_place="v", room=32 * 1024):
+def call(kernel, outs, inputs, places, scratch=(), flops=0, out_place="v", aliases=()):
     spaces = {"s": pltpu.SMEM, "v": pltpu.VMEM, "h": pltpu.HBM}
-    moved = sum(4 * math.prod(shape) for shape in outs) + sum(array.nbytes for array in inputs)
+    outs = [spaces[out_place](out, jnp.float32) if isinstance(out, tuple) else out for out in outs]
+    moved = sum(4 * math.prod(out.shape) for out in outs) + sum(array.nbytes for array in inputs)
     inputs = [
-        pltpu.with_memory_space_constraint(array, pltpu.HBM) if p == "h" else array
+        array if p == "v" else pltpu.with_memory_space_constraint(array, spaces[p])
         for array, p in zip(inputs, places)
     ]
     return pl.pallas_call(
         kernel,
-        out_shape=[spaces[out_place](shape, jnp.float32) for shape in outs],
+        out_shape=outs,
         in_specs=[pl.BlockSpec(memory_space=spaces[p]) for p in places],
-        out_specs=[pl.BlockSpec(memory_space=spaces[out_place])] * len(outs),
+        out_specs=[pl.BlockSpec(memory_space=out.memory_space) for out in outs],
         scratch_shapes=[pltpu.VMEM(s, jnp.float32) if isinstance(s, tuple) else s for s in scratch],
-        compiler_params=pltpu.CompilerParams(vmem_limit_bytes=room * 1024),
+        input_output_aliases=dict(aliases),
+        compiler_params=pltpu.CompilerParams(vmem_limit_bytes=32 * 1024 * 1024),
         cost_estimate=pl.CostEstimate(flops=flops, bytes_accessed=moved, transcendentals=0),
     )(*inputs)
 
@@ -873,19 +943,19 @@
     def kernel(body):
         return functools.partial(body, levels)
 
-    rows, own, level, speeds = call(
+    rows, air_pieces, west, south = call(
         kernel(pack_kernel),
-        [slabs(slots + 1 + pieces), slabs(slots + 1), (height, breadth), slabs(2 * pieces)],
-        [nest_west, nest_south, air, east, north],
-        "hhhhh",
-        [
-            pltpu.SMEM((2,), jnp.int32),
-            pltpu.SMEM((2,), jnp.int32),
-            chunked,
-            chunked,
-            chunked,
-            pltpu.SemaphoreType.DMA((3 * pieces + 2,)),
-        ],
+        [slabs(slots + 1 + pieces), chunked, pltpu.SMEM((2,), jnp.int32), pltpu.SMEM((2,), jnp.int32)],
+        [nest_west, nest_south, air],
+        "hhh",
+        [pltpu.SemaphoreType.DMA((pieces + 2,))],
+    )
+    own, level, speeds = call(
+        kernel(own_kernel),
+        [slabs(slots + 1), (height, breadth), slabs(2 * pieces)],
+        [west, south, air_pieces, east, north],
+        "ssvvv",
+        flops=30 * size * breadth,
     )
     rows = lax.ppermute(rows, "rows", swap)
     level = lax.ppermute(level, "lev", swap)
@@ -896,41 +966,58 @@
 
     starting = over_tiles(own + rows[: slots + 1])
     sides = [(size, LANES), (levels, breadth), (levels, breadth)]
-    early, own, other = call(
+    early, other = call(
         kernel(early_kernel),
-        [chunked, slabs(slots + 1), slabs(slots + 1)],
-        [nest_west, nest_south, air, east, north, rows, level, starting[0], starting[2]],
+        [chunked, slabs(slots + 1)],
+        [west, south, air, east, north, rows, level, starting[0], speeds],
         "ssvvvvvvv",
         sides,
         flops=30 * size * breadth,
     )
+    early, other = call(
+        kernel(middle_kernel),
+        [chunked, slabs(slots + 1)],
+        [west, south, air, east, north, rows, level, starting[2], starting[0], early, other],
+        "ssvvvvvvvvv",
+        sides,
+        flops=30 * size * breadth,
+        aliases=[(9, 0), (10, 1)],
+    )
     other = lax.ppermute(other, "rows", swap)
-    first, edge = call(
+    first, edge, own = call(
         kernel(first_kernel),
-        [chunked, (height, breadth)],
-        [early, east, speeds, *starting],
-        "vvvvvv",
+        [chunked, (height, breadth), slabs(slots + 1)],
+        [west, south, early, east, speeds, *starting[::-1]],
+        "ssvvvvvv",
+        flops=10 * size * breadth,
     )
     level = lax.ppermute(edge, "lev", swap)
-    (message,) = call(
+    (part,) = call(
         kernel(average_kernel),
         [slabs(slots + 1)],
-        [first, east, north, rows, level, own, other],
-        "vvvvvvv",
-        [flat],
+        [first, east, north, other],
+        "vvvv",
+        [flat, (height, breadth)],
+        flops=30 * size * breadth,
+    )
+    (message,) = call(
+        kernel(message_kernel),
+        [slabs(slots + 1)],
+        [level, part, own, other],
+        "vvvv",
     )
     received = over_tiles(message)
     (blend,) = call(
         kernel(blend_kernel),
         [slabs(third_y + 1)],
-        [weight, first, message, *received, *starting],
+        [weight, first, message, *received, *starting[::-1]],
         "v" * 9,
     )
     rows = lax.ppermute(blend, "rows", swap)
     (later,) = call(
         kernel(later_kernel),
         [chunked],
-        [nest_west, nest_south, first, east, north, level, *received, early, blend],
+        [west, south, first, east, north, level, *received, early, blend],
         "ss" + "v" * 9,
         [flat, *sides],
         flops=30 * size * breadth,
@@ -938,7 +1025,7 @@
     (out,) = call(
         kernel(last_kernel),
         [flat],
-        [nest_west, nest_south, later, speeds, blend, rows],
+        [west, south, later, speeds, blend, rows],
         "ssvvvv",
         [chunked, pltpu.SemaphoreType.DMA((pieces,))],
         out_place="h",

time: 38.9 us -> 35.8 us (0.920)
  waiting for transfers between devices: 14.6 us -> 12 us
  Pallas kernels: 6.29 us -> 4.69 us
  local copies, waits for them, and re-layouts: 0.1 us -> 1.15 us
    pallas_call x7 -> x10, Pallas kernels: 6.29 us -> 4.69 us  [call(): pl.pallas_call(kernel, out_shape=outs, in_specs=[pl.BlockSpec(memory_spac...]
    ppermute x6, waiting for transfers between devices: 5.82 us -> 4.27 us  [over_tiles(): return [lax.ppermute(message, 'tiles', pair) for pair in pairs]]
    ppermute x1, waiting for transfers between devices: 3.15 us -> 1.78 us  [per_device_paired(): rows = lax.ppermute(rows, 'rows', swap)]
    ppermute x1, waiting for transfers between devices: 1.2 us -> 0.01 us  [per_device_paired(): level = lax.ppermute(edge, 'lev', swap)]
    unnamed x12 -> x10, local copies, waits for them, and re-layouts: 0.03 us -> 1.08 us
    ppermute x1, waiting for transfers between devices: 1.82 us -> 2.77 us  [per_device_paired(): other = lax.ppermute(other, 'rows', swap)]
    ppermute x1, waiting for transfers between devices: 2.09 us -> 2.65 us  [per_device_paired(): rows = lax.ppermute(blend, 'rows', swap)]
  transfers between devices with their start and end apart: 11 -> 11, of which waited for: 9 -> 6; matrix products, arithmetic and copies ran while one was open for 0% -> 0% of each run, Pallas kernels for 6% -> 5%
where the time goes in v4:
time: 35.8 us; the launch traced here: 35.7 us
  starting transfers between devices  17.7 us (49%)
  waiting for transfers between devices  12 us (34%)
  Pallas kernels  4.69 us (13%)
  local copies, waits for them, and re-layouts  1.15 us (3%)
    ppermute x6, starting transfers between devices, over_tiles(): return [lax.ppermute(message, 'tiles', pair) for pair in pairs]  11.6 us
    pallas_call x10, Pallas kernels, call(): pl.pallas_call(kernel, out_shape=outs, in_specs=[pl.BlockSpec(memory_spac...  4.69 us
    ppermute x6, waiting for transfers between devices, over_tiles(): return [lax.ppermute(message, 'tiles', pair) for pair in pairs]  4.27 us
    ppermute x1, starting transfers between devices, per_device_paired(): rows = lax.ppermute(rows, 'rows', swap)  3 us
    ppermute x1, waiting for transfers between devices, per_device_paired(): other = lax.ppermute(other, 'rows', swap)  2.77 us
    ppermute x1, waiting for transfers between devices, per_device_paired(): rows = lax.ppermute(blend, 'rows', swap)  2.65 us
    ppermute x1, waiting for transfers between devices, per_device_paired(): rows = lax.ppermute(rows, 'rows', swap)  1.78 us
    ppermute x1, starting transfers between devices, per_device_paired(): rows = lax.ppermute(blend, 'rows', swap)  1.56 us
  transfers between devices with their start and end apart: 11, of which 6 were waited for; matrix products, arithmetic and copies ran while one was open for 0% of the time, Pallas kernels for 5%

profile of v4, /device:TPU:0, one launch (start us, length us, event | category | flops | bytes accessed | tf_op | source)
XLA Modules:
  0.0 35.7 jit_solution(4219444766236988116)
XLA Ops:
  0.0 1.4 %shard_map.64 = (f32[14,16,128]{2,1,0:T(8,128)S(1)}, f32[3,384,128]{2,1,0:T(8,128)S(1)}, s32[2]{0:T(128)S(4)}, s32[2]{0:T(128)S(4)}) custom-call(s32[2]{0:T(128)} %west_hbm.1, s32[2]{0:T(128)} %south_hbm.1, f32[384,384]{1,0:T(8,128)} %bitcast.15), custom_call_target="tpu_custom_call" | custom-call | bytes 1294368 | tf_op jit(solution)/shard_map/pallas_call | solution.py:916
  1.5 3.0 %collective-permute-start = (f32[14,16,128]{2,1,0:T(8,128)S(1)}, f32[14,16,128]{2,1,0:T(8,128)S(1)}, u32[]{:S(2)}, u32[]{:S(2)}) collective-permute-start(f32[14,16,128]{2,1,0:T(8,128)S(1)} %get-tuple-element.21), channel_id=1, source_target_pairs={{0,2},{2,0},{1,3},{3,1},{4,6},{6,4},{5,7},{7,5},{8,10},{10,8},{9,1... | collective-permute-start | bytes 344072 | tf_op jit(solution)/shard_map/ppermute | solution.py:960
  4.5 1.1 %copy-done.1 = f32[16,24,384]{2,1,0:T(8,128)S(1)} copy-done((f32[16,24,384]{2,1,0:T(8,128)S(1)}, f32[16,24,384]{2,1,0:T(8,128)}, u32[]{:S(2)}) %copy-start.1) | copy-done | bytes 589848
  5.5 0.3 shard_map.65
  5.8 1.8 %collective-permute-done.rows_ref = f32[14,16,128]{2,1,0:T(8,128)S(1)} collective-permute-done((f32[14,16,128]{2,1,0:T(8,128)S(1)}, f32[14,16,128]{2,1,0:T(8,128)S(1)}, u32[]{:S(2)}, u32[]{:S(2)}) %collective-permute-start) | collective-permute-done | bytes 114720 | tf_op jit(solution)/shard_map/ppermute | solution.py:960
  7.6 1.9 %collective-permute-start.3 = (f32[11,16,128]{2,1,0:T(8,128)S(1)}, f32[11,16,128]{2,1,0:T(8,128)S(1)}, u32[]{:S(2)}, u32[]{:S(2)}) collective-permute-start(f32[11,16,128]{2,1,0:T(8,128)S(1)} %slice_add_fusion), channel_id=1, source_target_pairs={{0,4},{4,0},{8,12},{12,8},{1,5},{5,1},{9,13},{13,9},{2,6},{6,2},{1... | collective-permute-start | bytes 270344 | tf_op jit(solution)/shard_map/ppermute | solution.py:965
  9.5 2.5 %collective-permute-start.2 = (f32[11,16,128]{2,1,0:T(8,128)S(1)}, f32[11,16,128]{2,1,0:T(8,128)S(1)}, u32[]{:S(2)}, u32[]{:S(2)}) collective-permute-start(f32[11,16,128]{2,1,0:T(8,128)S(1)} %slice_add_fusion), channel_id=1, source_target_pairs={{0,12},{12,0},{4,8},{8,4},{1,13},{13,1},{5,9},{9,5},{2,14},{14,2},... | collective-permute-start | bytes 270344 | tf_op jit(solution)/shard_map/ppermute | solution.py:965
  12.0 0.7 %collective-permute-start.4 = (f32[11,16,128]{2,1,0:T(8,128)S(1)}, f32[11,16,128]{2,1,0:T(8,128)S(1)}, u32[]{:S(2)}, u32[]{:S(2)}) collective-permute-start(f32[11,16,128]{2,1,0:T(8,128)S(1)} %slice_add_fusion), channel_id=1, source_target_pairs={{4,12},{12,4},{5,13},{13,5},{6,14},{14,6},{7,15},{15,7},{20,28},{2... | collective-permute-start | bytes 270344 | tf_op jit(solution)/shard_map/ppermute | solution.py:965
  12.7 0.5 %collective-permute-done.1.level_ref = f32[24,384]{1,0:T(8,128)S(1)} collective-permute-done((f32[24,384]{1,0:T(8,128)S(1)}, f32[24,384]{1,0:T(8,128)S(1)}, u32[]{:S(2)}, u32[]{:S(2)}) %collective-permute-start.1) | collective-permute-done | bytes 36896 | tf_op jit(solution)/shard_map/ppermute | solution.py:961
  13.2 1.1 %shard_map.66 = (f32[3,384,128]{2,1,0:T(8,128)S(1)}, f32[11,16,128]{2,1,0:T(8,128)S(1)}) custom-call(s32[2]{0:T(128)S(4)} %get-tuple-element.19.west_ref, s32[2]{0:T(128)S(4)} %get-tuple-element.20.south_ref, f32[384,384]{1,0:T(8,128)S(1)} %bitcast.16, f32[384,384]{1,0:T(8,128)S(1)} %bitcast.5, f32[384,384]{1,0:T(8,128)S(1)} %bitcast.11, ...), custom_call_target="tpu_custom_call" | custom-call | flops 4423680 | bytes 2740240 | tf_op jit(solution)/shard_map/pallas_call | solution.py:916
  14.3 1.6 %collective-permute-done.2.three_ref.coef_three_ref = f32[11,16,128]{2,1,0:T(8,128)S(1)} collective-permute-done((f32[11,16,128]{2,1,0:T(8,128)S(1)}, f32[11,16,128]{2,1,0:T(8,128)S(1)}, u32[]{:S(2)}, u32[]{:S(2)}) %collective-permute-start.2) | collective-permute-done | bytes 90144 | tf_op jit(solution)/shard_map/ppermute | solution.py:965
  15.8 1.5 %collective-permute-start.6 = (f32[11,16,128]{2,1,0:T(8,128)S(1)}, f32[11,16,128]{2,1,0:T(8,128)S(1)}, u32[]{:S(2)}, u32[]{:S(2)}) collective-permute-start(f32[11,16,128]{2,1,0:T(8,128)S(1)} %get-tuple-element.31), channel_id=1, source_target_pairs={{0,2},{2,0},{1,3},{3,1},{4,6},{6,4},{5,7},{7,5},{8,10},{10,8},{9,1... | collective-permute-start | bytes 270344 | tf_op jit(solution)/shard_map/ppermute | solution.py:986
  17.3 0.2 shard_map.68
  17.5 0.1 collective-permute-start.5
  17.6 2.8 %collective-permute-done.6.other_ref = f32[11,16,128]{2,1,0:T(8,128)S(1)} collective-permute-done((f32[11,16,128]{2,1,0:T(8,128)S(1)}, f32[11,16,128]{2,1,0:T(8,128)S(1)}, u32[]{:S(2)}, u32[]{:S(2)}) %collective-permute-start.6) | collective-permute-done | bytes 90144 | tf_op jit(solution)/shard_map/ppermute | solution.py:986
  20.4 4.0 %collective-permute-start.9 = (f32[11,16,128]{2,1,0:T(8,128)S(1)}, f32[11,16,128]{2,1,0:T(8,128)S(1)}, u32[]{:S(2)}, u32[]{:S(2)}) collective-permute-start(f32[11,16,128]{2,1,0:T(8,128)S(1)} %shard_map.70.window_ref), channel_id=1, source_target_pairs={{0,12},{12,0},{4,8},{8,4},{1,13},{13,1},{5,9},{9,5},{2,14},{14,2},... | collective-permute-start | bytes 270344 | tf_op jit(solution)/shard_map/ppermute | solution.py:965
  24.4 0.7 %collective-permute-start.8 = (f32[11,16,128]{2,1,0:T(8,128)S(1)}, f32[11,16,128]{2,1,0:T(8,128)S(1)}, u32[]{:S(2)}, u32[]{:S(2)}) collective-permute-start(f32[11,16,128]{2,1,0:T(8,128)S(1)} %shard_map.70.window_ref), channel_id=1, source_target_pairs={{4,12},{12,4},{5,13},{13,5},{6,14},{14,6},{7,15},{15,7},{20,28},{2... | collective-permute-start | bytes 270344 | tf_op jit(solution)/shard_map/ppermute | solution.py:965
  25.1 1.9 %collective-permute-start.7 = (f32[11,16,128]{2,1,0:T(8,128)S(1)}, f32[11,16,128]{2,1,0:T(8,128)S(1)}, u32[]{:S(2)}, u32[]{:S(2)}) collective-permute-start(f32[11,16,128]{2,1,0:T(8,128)S(1)} %shard_map.70.window_ref), channel_id=1, source_target_pairs={{0,4},{4,0},{8,12},{12,8},{1,5},{5,1},{9,13},{13,9},{2,6},{6,2},{1... | collective-permute-start | bytes 270344 | tf_op jit(solution)/shard_map/ppermute | solution.py:965
  27.0 2.7 %collective-permute-done.7.one_ref = f32[11,16,128]{2,1,0:T(8,128)S(1)} collective-permute-done((f32[11,16,128]{2,1,0:T(8,128)S(1)}, f32[11,16,128]{2,1,0:T(8,128)S(1)}, u32[]{:S(2)}, u32[]{:S(2)}) %collective-permute-start.7) | collective-permute-done | bytes 90144 | tf_op jit(solution)/shard_map/ppermute | solution.py:965
  29.8 0.4 %shard_map.71.blend_ref = f32[9,16,128]{2,1,0:T(8,128)S(1)} custom-call(f32[16,128]{1,0:T(8,128)S(1)} %broadcast_in_dim.2.weight_ref, f32[3,384,128]{2,1,0:T(8,128)S(1)} %get-tuple-element.29.field_ref, f32[11,16,128]{2,1,0:T(8,128)S(1)} %shard_map.70.window_ref, f32[11,16,128]{2,1,0:T(8,128)S(1)} %collective-permute-done.7.one_ref, ...), custom_call_target="tpu_custom_call" | custom-call | bytes 1302528 | tf_op jit(solution)/shard_map/pallas_call | solution.py:916
  30.1 1.6 %collective-permute-start.10 = (f32[9,16,128]{2,1,0:T(8,128)S(1)}, f32[9,16,128]{2,1,0:T(8,128)S(1)}, u32[]{:S(2)}, u32[]{:S(2)}) collective-permute-start(f32[9,16,128]{2,1,0:T(8,128)S(1)} %shard_map.71.blend_ref), channel_id=1, source_target_pairs={{0,2},{2,0},{1,3},{3,1},{4,6},{6,4},{5,7},{7,5},{8,10},{10,8},{9,1... | collective-permute-start | bytes 221192 | tf_op jit(solution)/shard_map/ppermute | solution.py:1016
  31.7 0.2 shard_map.72.given_ref
  31.9 2.6 %collective-permute-done.10.rows_ref = f32[9,16,128]{2,1,0:T(8,128)S(1)} collective-permute-done((f32[9,16,128]{2,1,0:T(8,128)S(1)}, f32[9,16,128]{2,1,0:T(8,128)S(1)}, u32[]{:S(2)}, u32[]{:S(2)}) %collective-permute-start.10) | collective-permute-done | bytes 73760 | tf_op jit(solution)/shard_map/ppermute | solution.py:1016
  34.6 1.1 %shard_map.73 = f32[384,384]{1,0:T(8,128)} custom-call(s32[2]{0:T(128)S(4)} %get-tuple-element.19.west_ref, s32[2]{0:T(128)S(4)} %get-tuple-element.20.south_ref, f32[3,384,128]{2,1,0:T(8,128)S(1)} %shard_map.72.given_ref, f32[6,16,128]{2,1,0:T(8,128)S(1)} %get-tuple-element.25.speeds_ref, f32[9,16,128]{2,1,0:T(8,128)S(1)} %shard_map.71.blend_ref, ...), custom_call_target="tpu_custom_call" | custom-call | bytes 1376272 | tf_op jit(solution)/shard_map/pallas_call | solution.py:916
  (20 shorter events, 0.2 us)
Async XLA Ops:
  0.0 4.5 %copy-start = (f32[16,24,384]{2,1,0:T(8,128)S(1)}, f32[16,24,384]{2,1,0:T(8,128)}, u32[]{:S(2)}) copy-start(f32[16,24,384]{2,1,0:T(8,128)} %param.7) | copy-start | bytes 1769476
  1.5 6.1 %collective-permute-start = (f32[14,16,128]{2,1,0:T(8,128)S(1)}, f32[14,16,128]{2,1,0:T(8,128)S(1)}, u32[]{:S(2)}, u32[]{:S(2)}) collective-permute-start(f32[14,16,128]{2,1,0:T(8,128)S(1)} %get-tuple-element.21), channel_id=1, source_target_pairs={{0,2},{2,0},{1,3},{3,1},{4,6},{6,4},{5,7},{7,5},{8,10},{10,8},{9,1... | collective-permute-start | bytes 344072 | tf_op jit(solution)/shard_map/ppermute | solution.py:960
  4.5 1.1 %copy-start.1 = (f32[16,24,384]{2,1,0:T(8,128)S(1)}, f32[16,24,384]{2,1,0:T(8,128)}, u32[]{:S(2)}) copy-start(f32[16,24,384]{2,1,0:T(8,128)} %param.8) | copy-start | bytes 1769476
  5.5 7.7 %copy-start.3 = (f32[16,24,384]{2,1,0:T(8,128)S(1)}, f32[16,24,384]{2,1,0:T(8,128)}, u32[]{:S(2)}) copy-start(f32[16,24,384]{2,1,0:T(8,128)} %param.6) | copy-start | bytes 1769476
  7.6 5.6 %collective-permute-start.3 = (f32[11,16,128]{2,1,0:T(8,128)S(1)}, f32[11,16,128]{2,1,0:T(8,128)S(1)}, u32[]{:S(2)}, u32[]{:S(2)}) collective-permute-start(f32[11,16,128]{2,1,0:T(8,128)S(1)} %slice_add_fusion), channel_id=1, source_target_pairs={{0,4},{4,0},{8,12},{12,8},{1,5},{5,1},{9,13},{13,9},{2,6},{6,2},{1... | collective-permute-start | bytes 270344 | tf_op jit(solution)/shard_map/ppermute | solution.py:965
  9.5 6.3 %collective-permute-start.2 = (f32[11,16,128]{2,1,0:T(8,128)S(1)}, f32[11,16,128]{2,1,0:T(8,128)S(1)}, u32[]{:S(2)}, u32[]{:S(2)}) collective-permute-start(f32[11,16,128]{2,1,0:T(8,128)S(1)} %slice_add_fusion), channel_id=1, source_target_pairs={{0,12},{12,0},{4,8},{8,4},{1,13},{13,1},{5,9},{9,5},{2,14},{14,2},... | collective-permute-start | bytes 270344 | tf_op jit(solution)/shard_map/ppermute | solution.py:965
  12.0 1.2 %collective-permute-start.1 = (f32[24,384]{1,0:T(8,128)S(1)}, f32[24,384]{1,0:T(8,128)S(1)}, u32[]{:S(2)}, u32[]{:S(2)}) collective-permute-start(f32[24,384]{1,0:T(8,128)S(1)} %get-tuple-element.23), channel_id=1, source_target_pairs={{0,1},{1,0},{2,3},{3,2},{4,5},{5,4},{6,7},{7,6},{8,9},{9,8},{10,11... | collective-permute-start | bytes 110600 | tf_op jit(solution)/shard_map/ppermute | solution.py:961
  12.0 5.3 %collective-permute-start.4 = (f32[11,16,128]{2,1,0:T(8,128)S(1)}, f32[11,16,128]{2,1,0:T(8,128)S(1)}, u32[]{:S(2)}, u32[]{:S(2)}) collective-permute-start(f32[11,16,128]{2,1,0:T(8,128)S(1)} %slice_add_fusion), channel_id=1, source_target_pairs={{4,12},{12,4},{5,13},{13,5},{6,14},{14,6},{7,15},{15,7},{20,28},{2... | collective-permute-start | bytes 270344 | tf_op jit(solution)/shard_map/ppermute | solution.py:965
  15.8 4.5 %collective-permute-start.6 = (f32[11,16,128]{2,1,0:T(8,128)S(1)}, f32[11,16,128]{2,1,0:T(8,128)S(1)}, u32[]{:S(2)}, u32[]{:S(2)}) collective-permute-start(f32[11,16,128]{2,1,0:T(8,128)S(1)} %get-tuple-element.31), channel_id=1, source_target_pairs={{0,2},{2,0},{1,3},{3,1},{4,6},{6,4},{5,7},{7,5},{8,10},{10,8},{9,1... | collective-permute-start | bytes 270344 | tf_op jit(solution)/shard_map/ppermute | solution.py:986
  17.3 3.0 %copy-start.2 = (f32[16,24,384]{2,1,0:T(8,128)S(1)}, f32[16,24,384]{2,1,0:T(8,128)}, u32[]{:S(2)}) copy-start(f32[16,24,384]{2,1,0:T(8,128)} %param.8) | copy-start | bytes 1769476
  17.5 2.9 %collective-permute-start.5 = (f32[24,384]{1,0:T(8,128)S(1)}, f32[24,384]{1,0:T(8,128)S(1)}, u32[]{:S(2)}, u32[]{:S(2)}) collective-permute-start(f32[24,384]{1,0:T(8,128)S(1)} %get-tuple-element.30), channel_id=1, source_target_pairs={{0,1},{1,0},{2,3},{3,2},{4,5},{5,4},{6,7},{7,6},{8,9},{9,8},{10,11... | collective-permute-start | bytes 110600 | tf_op jit(solution)/shard_map/ppermute | solution.py:994
  20.4 9.3 %copy-start.4 = (f32[16]{0:T(128)S(1)}, f32[16]{0:T(128)}, u32[]{:S(2)}) copy-start(f32[16]{0:T(128)} %param.9) | copy-start | bytes 196
  20.4 6.6 %collective-permute-start.9 = (f32[11,16,128]{2,1,0:T(8,128)S(1)}, f32[11,16,128]{2,1,0:T(8,128)S(1)}, u32[]{:S(2)}, u32[]{:S(2)}) collective-permute-start(f32[11,16,128]{2,1,0:T(8,128)S(1)} %shard_map.70.window_ref), channel_id=1, source_target_pairs={{0,12},{12,0},{4,8},{8,4},{1,13},{13,1},{5,9},{9,5},{2,14},{14,2},... | collective-permute-start | bytes 270344 | tf_op jit(solution)/shard_map/ppermute | solution.py:965
  24.4 2.6 %collective-permute-start.8 = (f32[11,16,128]{2,1,0:T(8,128)S(1)}, f32[11,16,128]{2,1,0:T(8,128)S(1)}, u32[]{:S(2)}, u32[]{:S(2)}) collective-permute-start(f32[11,16,128]{2,1,0:T(8,128)S(1)} %shard_map.70.window_ref), channel_id=1, source_target_pairs={{4,12},{12,4},{5,13},{13,5},{6,14},{14,6},{7,15},{15,7},{20,28},{2... | collective-permute-start | bytes 270344 | tf_op jit(solution)/shard_map/ppermute | solution.py:965
  25.1 4.6 %collective-permute-start.7 = (f32[11,16,128]{2,1,0:T(8,128)S(1)}, f32[11,16,128]{2,1,0:T(8,128)S(1)}, u32[]{:S(2)}, u32[]{:S(2)}) collective-permute-start(f32[11,16,128]{2,1,0:T(8,128)S(1)} %shard_map.70.window_ref), channel_id=1, source_target_pairs={{0,4},{4,0},{8,12},{12,8},{1,5},{5,1},{9,13},{13,9},{2,6},{6,2},{1... | collective-permute-start | bytes 270344 | tf_op jit(solution)/shard_map/ppermute | solution.py:965
  30.1 4.4 %collective-permute-start.10 = (f32[9,16,128]{2,1,0:T(8,128)S(1)}, f32[9,16,128]{2,1,0:T(8,128)S(1)}, u32[]{:S(2)}, u32[]{:S(2)}) collective-permute-start(f32[9,16,128]{2,1,0:T(8,128)S(1)} %shard_map.71.blend_ref), channel_id=1, source_target_pairs={{0,2},{2,0},{1,3},{3,1},{4,6},{6,4},{5,7},{7,5},{8,10},{10,8},{9,1... | collective-permute-start | bytes 221192 | tf_op jit(solution)/shard_map/ppermute | solution.py:1016

commit v5 on v4

--- a/solution.py
+++ b/solution.py
@@ -176,6 +176,7 @@
 FIRST_LANE = 32
 LAST_LANE = 96
 EAST_LANE = 64
+WEIGHTS = 4
 
 
 def iota(shape, dim):
@@ -457,7 +458,7 @@
 
 
 def pack_kernel(
-    levels, west_hbm, south_hbm, air_hbm, rows_ref, air_ref, west_ref, south_ref, sems
+    levels, west_hbm, south_hbm, air_hbm, north_hbm, rows_ref, air_ref, west_ref, south_ref, north_ref, sems
 ):
     pieces, size, _ = air_ref.shape
     breadth = pieces * LANES
@@ -466,22 +467,37 @@
     slots = rows_ref.shape[0] - 1 - pieces
     tile, row, _ = place()
     nest = tile == lax.axis_size("tiles") - 1
-    copies = [
-        pltpu.make_async_copy(air_hbm.at[:, pl.ds(c * LANES, LANES)], air_ref.at[c], sems.at[c])
-        for c in range(pieces)
-    ]
-    copies.append(pltpu.make_async_copy(west_hbm, west_ref, sems.at[pieces]))
-    copies.append(pltpu.make_async_copy(south_hbm, south_ref, sems.at[pieces + 1]))
+    inner = inner_line(height, row)
+
+    def column_copies(source, target, first):
+        return [
+            pltpu.make_async_copy(source.at[:, pl.ds(c * LANES, LANES)], target.at[c], sems.at[first + c])
+            for c in range(pieces)
+        ]
+
+    copies = column_copies(air_hbm, air_ref, 0)
+    copies.append(pltpu.make_async_copy(west_hbm, west_ref, sems.at[2 * pieces]))
+    copies.append(pltpu.make_async_copy(south_hbm, south_ref, sems.at[2 * pieces + 1]))
+    speeds = column_copies(north_hbm, north_ref, pieces)
     for copy in copies:
         copy.start()
+
+    @pl.when(nest)
+    def _():
+        for copy in speeds:
+            copy.start()
+
     for copy in copies:
         copy.wait()
-    store_slabs(rows_ref, slots + 1, load_line(air_ref, levels, inner_line(height, row)))
+    store_slabs(rows_ref, slots + 1, load_line(air_ref, levels, inner))
     part = rows_ref.at[pl.ds(0, slots + 1)]
 
     @pl.when(nest)
     def _():
+        for copy in speeds:
+            copy.wait()
         part[...] = jnp.zeros_like(part)
+        store_slabs(rows_ref, WEIGHTS, load_line(north_ref, levels, inner))
 
     @pl.when(jnp.logical_not(nest))
     def _():
@@ -490,7 +506,9 @@
         pack_window(part, air_ref, levels, top + (1 - row) * third_y, start)
 
 
-def own_kernel(levels, west_ref, south_ref, air_ref, east_ref, north_ref, own_ref, level_ref, speeds_ref):
+def own_kernel(
+    levels, west_ref, south_ref, air_ref, east_ref, north_ref, own_ref, level_ref, speeds_ref, edges_ref
+):
     pieces, size, _ = air_ref.shape
     breadth = pieces * LANES
     height = size // levels
@@ -513,17 +531,19 @@
         store_slabs(speeds_ref, 0, outer)
         store_slabs(speeds_ref, pieces, speeds[levels:])
         own_ref[...] = jnp.zeros_like(own_ref)
+        edges_ref[...] = jnp.zeros_like(edges_ref)
         store_slabs(own_ref, 0, ghost_row_weights(ghost_weight(outer, row == 0), breadth))
         first = ghost_weight(east_ref[:, 0:1], True)
         last = ghost_weight(east_ref[:, breadth - 1 : breadth], False)
-        own_ref[3] = ghost_column_weights(first, last, levels, height)
+        own_ref[WEIGHTS - 1] = ghost_column_weights(first, last, levels, height)
 
     @pl.when(jnp.logical_not(nest))
     def _():
         start = west_ref[0] - tile * breadth
         top = south_ref[0] - 1 - row * height
         pack_window(own_ref, air_ref, levels, top + row * third_y, start)
-        own_ref[slots] = own_ref[slots] + pack_edges(air_ref, levels)
+        edges_ref[...] = pack_edges(air_ref, levels)
+        own_ref[slots] = own_ref[slots] + edges_ref[...]
         speeds_ref[...] = jnp.zeros_like(speeds_ref)
 
 
@@ -558,14 +578,12 @@
     rows_ref,
     level_ref,
     one_ref,
-    speeds_ref,
     field_ref,
     other_ref,
     side_ref,
     northern_ref,
     southern_ref,
 ):
-    pieces = field_ref.shape[0]
     slots = other_ref.shape[0] - 1
     tile_count = lax.axis_size("tiles")
     tile, row, lev = place()
@@ -576,7 +594,6 @@
         set_halo(rows_ref, slots + 1, northern_ref, southern_ref, row)
         full_step(field_ref, *shared, levels, lev, True, northern_ref, southern_ref, None, None)
         other_ref[...] = jnp.zeros_like(other_ref)
-        other_ref[pl.ds(0, pieces)] = speeds_ref[pl.ds(pieces, pieces)]
 
     @pl.when(tile == 0)
     def _():
@@ -611,7 +628,7 @@
 
     @pl.when((tile > 0) & (tile < tile_count - 1))
     def _():
-        columns = neighbour_columns(one_ref[slots], three_ref[slots], tile_count - 1, tile)
+        columns = neighbour_columns(one_ref[slots], three_ref[...], tile_count - 1, tile)
         refs = (field_ref, other_ref, side_ref, northern_ref, southern_ref)
         parent_step(levels, west_ref, south_ref, shared, rows_ref, columns, *refs)
 
@@ -664,7 +681,7 @@
         edge_ref[...] = edge_level(field_ref, height, lev)
 
 
-def average_kernel(levels, field_ref, east_ref, north_ref, other_ref, message_ref, part_ref, nothing_ref):
+def average_kernel(levels, field_ref, east_ref, north_ref, rows_ref, message_ref, part_ref, nothing_ref):
     pieces, size, _ = field_ref.shape
     height, breadth = nothing_ref.shape
     third_y = height // 3
@@ -685,7 +702,7 @@
         for m in range(third_y):
             message_ref[m] = means[m * levels : (m + 1) * levels]
         shared = load_line(field_ref, levels, inner_line(height, row))
-        shared = ghost_weight(join_slabs(other_ref, 0, pieces), row == 0) * shared
+        shared = ghost_weight(join_slabs(rows_ref, WEIGHTS, pieces), row == 0) * shared
         message_ref[third_y] = from_right(shared, sums) * (1.0 / 9.0)
         for i in range(third_y + 1, message_ref.shape[0]):
             message_ref[i] = jnp.zeros((levels, LANES), jnp.float32)
@@ -775,7 +792,7 @@
             last = EAST_LANE + s
             east = jnp.where(at_last, extra[:, last : last + 1], pltpu.roll(x, LANES - 1, 1))
             lines.append((west, x, east))
-        edges = coefficient(3)
+        edges = coefficient(WEIGHTS - 1)
         ghosts = [coefficient(q) for q in range(3)]
 
         def outward(side, q):
@@ -930,6 +947,7 @@
     third_y = height // 3
     pieces = breadth // LANES
     slots = third_y + 2
+    tile_count = lax.axis_size("tiles")
     size = levels * height
     flat = (size, breadth)
     chunked = (pieces, size, LANES)
@@ -946,38 +964,45 @@
     rows, air_pieces, west, south = call(
         kernel(pack_kernel),
         [slabs(slots + 1 + pieces), chunked, pltpu.SMEM((2,), jnp.int32), pltpu.SMEM((2,), jnp.int32)],
-        [nest_west, nest_south, air],
-        "hhh",
-        [pltpu.SemaphoreType.DMA((pieces + 2,))],
-    )
-    own, level, speeds = call(
+        [nest_west, nest_south, air, north],
+        "hhhh",
+        [chunked, pltpu.SemaphoreType.DMA((2 * pieces + 2,))],
+    )
+    own, level, speeds, edges = call(
         kernel(own_kernel),
-        [slabs(slots + 1), (height, breadth), slabs(2 * pieces)],
+        [slabs(slots + 1), (height, breadth), slabs(2 * pieces), (levels, LANES)],
         [west, south, air_pieces, east, north],
         "ssvvv",
         flops=30 * size * breadth,
     )
     rows = lax.ppermute(rows, "rows", swap)
     level = lax.ppermute(level, "lev", swap)
-    pairs = [[(0, 1), (1, 0), (2, 3), (3, 2)], [(1, 3), (3, 1)], [(0, 3), (3, 0), (1, 2), (2, 1)]]
-
-    def over_tiles(message):
-        return [lax.ppermute(message, "tiles", pair) for pair in pairs]
-
-    starting = over_tiles(own + rows[: slots + 1])
+    where = [(t, r, l) for t in range(tile_count) for r in range(2) for l in range(2)]
+    at = {position: i for i, position in enumerate(where)}
+
+    def over_tiles(message, step, *without):
+        pairs = []
+        for t, r, l in where:
+            idle = t in without or (t ^ step) in without
+            pairs.append((at[t, r, l], at[(t, r, 1 - l) if idle else (t ^ step, r, l)]))
+        return lax.ppermute(message, ("tiles", "rows", "lev"), pairs)
+
+    window = own + rows[: slots + 1]
+    starting = [over_tiles(window, 1), over_tiles(window, 2, 0), over_tiles(window, 3, 1)]
+    halo = over_tiles(edges, 3, 0)
     sides = [(size, LANES), (levels, breadth), (levels, breadth)]
     early, other = call(
         kernel(early_kernel),
         [chunked, slabs(slots + 1)],
-        [west, south, air, east, north, rows, level, starting[0], speeds],
-        "ssvvvvvvv",
+        [west, south, air, east, north, rows, level, starting[0]],
+        "ssvvvvvv",
         sides,
         flops=30 * size * breadth,
     )
     early, other = call(
         kernel(middle_kernel),
         [chunked, slabs(slots + 1)],
-        [west, south, air, east, north, rows, level, starting[2], starting[0], early, other],
+        [west, south, air, east, north, rows, level, halo, starting[0], early, other],
         "ssvvvvvvvvv",
         sides,
         flops=30 * size * breadth,
@@ -995,7 +1020,7 @@
     (part,) = call(
         kernel(average_kernel),
         [slabs(slots + 1)],
-        [first, east, north, other],
+        [first, east, north, rows],
         "vvvv",
         [flat, (height, breadth)],
         flops=30 * size * breadth,
@@ -1006,7 +1031,7 @@
         [level, part, own, other],
         "vvvv",
     )
-    received = over_tiles(message)
+    received = [over_tiles(message, 1), over_tiles(message, 2, 0), over_tiles(message, 3)]
     (blend,) = call(
         kernel(blend_kernel),
         [slabs(third_y + 1)],

time: 35.8 us -> 34.5 us (0.964)
  local copies, waits for them, and re-layouts: 1.15 us -> 0.08 us
  starting transfers between devices: 17.7 us -> 16.8 us
  waiting for transfers between devices: 12 us -> 12.6 us
    ppermute x1, waiting for transfers between devices: 2.77 us -> 0.01 us  [per_device_paired(): other = lax.ppermute(other, 'rows', swap)]
    ppermute x6 -> x7, waiting for transfers between devices: 4.27 us -> 5.97 us  [over_tiles(): return lax.ppermute(message, ('tiles', 'rows', 'lev'), pairs)]
    ppermute x6 -> x7, starting transfers between devices: 11.6 us -> 10.3 us  [over_tiles(): return lax.ppermute(message, ('tiles', 'rows', 'lev'), pairs)]
    ppermute x1, waiting for transfers between devices: 0.01 us -> 1.18 us  [per_device_paired(): level = lax.ppermute(edge, 'lev', swap)]
    unnamed x10 -> x8, local copies, waits for them, and re-layouts: 1.08 us -> 0.01 us
    ppermute x1, waiting for transfers between devices: 1.78 us -> 2.83 us  [per_device_paired(): rows = lax.ppermute(rows, 'rows', swap)]
    ppermute x1, waiting for transfers between devices: 0.55 us -> 0.01 us  [per_device_paired(): level = lax.ppermute(level, 'lev', swap)]
  transfers between devices with their start and end apart: 11 -> 12, of which waited for: 6 -> 6; matrix products, arithmetic and copies ran while one was open for 0% -> 0% of each run, Pallas kernels for 5% -> 5%
where the time goes in v5:
time: 34.5 us; the launch traced here: 34.3 us
  starting transfers between devices  16.8 us (49%)
  waiting for transfers between devices  12.6 us (37%)
  Pallas kernels  4.77 us (14%)
    ppermute x7, starting transfers between devices, over_tiles(): return lax.ppermute(message, ('tiles', 'rows', 'lev'), pairs)  10.3 us
    ppermute x7, waiting for transfers between devices, over_tiles(): return lax.ppermute(message, ('tiles', 'rows', 'lev'), pairs)  5.97 us
    pallas_call x10, Pallas kernels, call(): pl.pallas_call(kernel, out_shape=outs, in_specs=[pl.BlockSpec(memory_spac...  4.77 us
    ppermute x1, starting transfers between devices, per_device_paired(): rows = lax.ppermute(rows, 'rows', swap)  3 us
    ppermute x1, waiting for transfers between devices, per_device_paired(): rows = lax.ppermute(rows, 'rows', swap)  2.83 us
    ppermute x1, waiting for transfers between devices, per_device_paired(): rows = lax.ppermute(blend, 'rows', swap)  2.61 us
    ppermute x1, starting transfers between devices, per_device_paired(): other = lax.ppermute(other, 'rows', swap)  1.75 us
    ppermute x1, starting transfers between devices, per_device_paired(): rows = lax.ppermute(blend, 'rows', swap)  1.61 us
  transfers between devices with their start and end apart: 12, of which 6 were waited for; matrix products, arithmetic and copies ran while one was open for 0% of the time, Pallas kernels for 5%

profile of v5, /device:TPU:0, one launch (start us, length us, event | category | flops | bytes accessed | tf_op | source)
XLA Modules:
  0.0 34.3 jit_solution(12429088148792846504)
XLA Ops:
  0.0 1.5 %shard_map.64 = (f32[14,16,128]{2,1,0:T(8,128)S(1)}, f32[3,384,128]{2,1,0:T(8,128)S(1)}, s32[2]{0:T(128)S(4)}, s32[2]{0:T(128)S(4)}) custom-call(s32[2]{0:T(128)} %west_hbm.1, s32[2]{0:T(128)} %south_hbm.1, f32[384,384]{1,0:T(8,128)} %bitcast.16, f32[384,384]{1,0:T(8,128)} %bitcast.10), custom_call_target="tpu_custom_call" | custom-call | bytes 1884192 | tf_op jit(solution)/shard_map/pallas_call | solution.py:933
  1.5 3.0 %collective-permute-start = (f32[14,16,128]{2,1,0:T(8,128)S(1)}, f32[14,16,128]{2,1,0:T(8,128)S(1)}, u32[]{:S(2)}, u32[]{:S(2)}) collective-permute-start(f32[14,16,128]{2,1,0:T(8,128)S(1)} %get-tuple-element.22), channel_id=1, source_target_pairs={{0,2},{2,0},{1,3},{3,1},{4,6},{6,4},{5,7},{7,5},{8,10},{10,8},{9,1... | collective-permute-start | bytes 344072 | tf_op jit(solution)/shard_map/ppermute | solution.py:978
  4.5 0.3 shard_map.65
  4.8 2.8 %collective-permute-done.rows_ref = f32[14,16,128]{2,1,0:T(8,128)S(1)} collective-permute-done((f32[14,16,128]{2,1,0:T(8,128)S(1)}, f32[14,16,128]{2,1,0:T(8,128)S(1)}, u32[]{:S(2)}, u32[]{:S(2)}) %collective-permute-start) | collective-permute-done | bytes 114720 | tf_op jit(solution)/shard_map/ppermute | solution.py:978
  7.7 1.9 %collective-permute-start.3 = (f32[11,16,128]{2,1,0:T(8,128)S(1)}, f32[11,16,128]{2,1,0:T(8,128)S(1)}, u32[]{:S(2)}, u32[]{:S(2)}) collective-permute-start(f32[11,16,128]{2,1,0:T(8,128)S(1)} %slice_add_fusion), channel_id=1, source_target_pairs={{0,4},{1,5},{2,6},{3,7},{4,0},{5,1},{6,2},{7,3},{8,12},{9,13},{10,... | collective-permute-start | bytes 270344 | tf_op jit(solution)/shard_map/ppermute | solution.py:988
  9.6 0.5 %collective-permute-start.5 = (f32[11,16,128]{2,1,0:T(8,128)S(1)}, f32[11,16,128]{2,1,0:T(8,128)S(1)}, u32[]{:S(2)}, u32[]{:S(2)}) collective-permute-start(f32[11,16,128]{2,1,0:T(8,128)S(1)} %slice_add_fusion), channel_id=1, source_target_pairs={{0,1},{1,0},{2,3},{3,2},{4,12},{5,13},{6,14},{7,15},{8,9},{9,8},{1... | collective-permute-start | bytes 270344 | tf_op jit(solution)/shard_map/ppermute | solution.py:988
  10.1 2.1 %collective-permute-start.4 = (f32[11,16,128]{2,1,0:T(8,128)S(1)}, f32[11,16,128]{2,1,0:T(8,128)S(1)}, u32[]{:S(2)}, u32[]{:S(2)}) collective-permute-start(f32[11,16,128]{2,1,0:T(8,128)S(1)} %slice_add_fusion), channel_id=1, source_target_pairs={{0,12},{1,13},{2,14},{3,15},{4,5},{5,4},{6,7},{7,6},{8,9},{9,8},{1... | collective-permute-start | bytes 270344 | tf_op jit(solution)/shard_map/ppermute | solution.py:988
  12.1 0.2 collective-permute-start.2
  12.3 1.1 %shard_map.66 = (f32[3,384,128]{2,1,0:T(8,128)S(1)}, f32[11,16,128]{2,1,0:T(8,128)S(1)}) custom-call(s32[2]{0:T(128)S(4)} %get-tuple-element.20.west_ref, s32[2]{0:T(128)S(4)} %get-tuple-element.21.south_ref, f32[384,384]{1,0:T(8,128)S(1)} %bitcast.17, f32[384,384]{1,0:T(8,128)S(1)} %bitcast.5, f32[384,384]{1,0:T(8,128)S(1)} %bitcast.12, ...), custom_call_target="tpu_custom_call" | custom-call | flops 4423680 | bytes 2691088 | tf_op jit(solution)/shard_map/pallas_call | solution.py:933
  13.4 1.8 %collective-permute-start.7 = (f32[11,16,128]{2,1,0:T(8,128)S(1)}, f32[11,16,128]{2,1,0:T(8,128)S(1)}, u32[]{:S(2)}, u32[]{:S(2)}) collective-permute-start(f32[11,16,128]{2,1,0:T(8,128)S(1)} %get-tuple-element.34), channel_id=1, source_target_pairs={{0,2},{2,0},{1,3},{3,1},{4,6},{6,4},{5,7},{7,5},{8,10},{10,8},{9,1... | collective-permute-start | bytes 270344 | tf_op jit(solution)/shard_map/ppermute | solution.py:1011
  15.2 3.1 %collective-permute-done.4.three_ref.coef_three_ref = f32[11,16,128]{2,1,0:T(8,128)S(1)} collective-permute-done((f32[11,16,128]{2,1,0:T(8,128)S(1)}, f32[11,16,128]{2,1,0:T(8,128)S(1)}, u32[]{:S(2)}, u32[]{:S(2)}) %collective-permute-start.4) | collective-permute-done | bytes 90144 | tf_op jit(solution)/shard_map/ppermute | solution.py:988
  18.3 0.2 shard_map.68
  18.5 0.1 collective-permute-start.6
  18.6 1.2 %collective-permute-done.6.level_ref = f32[24,384]{1,0:T(8,128)S(1)} collective-permute-done((f32[24,384]{1,0:T(8,128)S(1)}, f32[24,384]{1,0:T(8,128)S(1)}, u32[]{:S(2)}, u32[]{:S(2)}) %collective-permute-start.6) | collective-permute-done | bytes 36896 | tf_op jit(solution)/shard_map/ppermute | solution.py:1019
  19.8 2.7 %collective-permute-start.10 = (f32[11,16,128]{2,1,0:T(8,128)S(1)}, f32[11,16,128]{2,1,0:T(8,128)S(1)}, u32[]{:S(2)}, u32[]{:S(2)}) collective-permute-start(f32[11,16,128]{2,1,0:T(8,128)S(1)} %shard_map.70.window_ref), channel_id=1, source_target_pairs={{0,12},{1,13},{2,14},{3,15},{4,8},{5,9},{6,10},{7,11},{8,4},{9,5},... | collective-permute-start | bytes 270344 | tf_op jit(solution)/shard_map/ppermute | solution.py:988
  22.5 0.2 collective-permute-start.9
  22.7 2.8 %collective-permute-start.8 = (f32[11,16,128]{2,1,0:T(8,128)S(1)}, f32[11,16,128]{2,1,0:T(8,128)S(1)}, u32[]{:S(2)}, u32[]{:S(2)}) collective-permute-start(f32[11,16,128]{2,1,0:T(8,128)S(1)} %shard_map.70.window_ref), channel_id=1, source_target_pairs={{0,4},{1,5},{2,6},{3,7},{4,0},{5,1},{6,2},{7,3},{8,12},{9,13},{10,... | collective-permute-start | bytes 270344 | tf_op jit(solution)/shard_map/ppermute | solution.py:988
  25.5 1.0 %collective-permute-done.10.three_ref = f32[11,16,128]{2,1,0:T(8,128)S(1)} collective-permute-done((f32[11,16,128]{2,1,0:T(8,128)S(1)}, f32[11,16,128]{2,1,0:T(8,128)S(1)}, u32[]{:S(2)}, u32[]{:S(2)}) %collective-permute-start.10) | collective-permute-done | bytes 90144 | tf_op jit(solution)/shard_map/ppermute | solution.py:988
  26.5 1.8 %collective-permute-done.8.one_ref = f32[11,16,128]{2,1,0:T(8,128)S(1)} collective-permute-done((f32[11,16,128]{2,1,0:T(8,128)S(1)}, f32[11,16,128]{2,1,0:T(8,128)S(1)}, u32[]{:S(2)}, u32[]{:S(2)}) %collective-permute-start.8) | collective-permute-done | bytes 90144 | tf_op jit(solution)/shard_map/ppermute | solution.py:988
  28.5 0.4 %shard_map.71.blend_ref = f32[9,16,128]{2,1,0:T(8,128)S(1)} custom-call(f32[16,128]{1,0:T(8,128)S(1)} %broadcast_in_dim.2.weight_ref, f32[3,384,128]{2,1,0:T(8,128)S(1)} %get-tuple-element.31.field_ref, f32[11,16,128]{2,1,0:T(8,128)S(1)} %shard_map.70.window_ref, f32[11,16,128]{2,1,0:T(8,128)S(1)} %collective-permute-done.8.one_ref, ...), custom_call_target="tpu_custom_call" | custom-call | bytes 1302528 | tf_op jit(solution)/shard_map/pallas_call | solution.py:933
  28.8 1.6 %collective-permute-start.11 = (f32[9,16,128]{2,1,0:T(8,128)S(1)}, f32[9,16,128]{2,1,0:T(8,128)S(1)}, u32[]{:S(2)}, u32[]{:S(2)}) collective-permute-start(f32[9,16,128]{2,1,0:T(8,128)S(1)} %shard_map.71.blend_ref), channel_id=1, source_target_pairs={{0,2},{2,0},{1,3},{3,1},{4,6},{6,4},{5,7},{7,5},{8,10},{10,8},{9,1... | collective-permute-start | bytes 221192 | tf_op jit(solution)/shard_map/ppermute | solution.py:1041
  30.5 0.2 shard_map.72.given_ref
  30.7 2.6 %collective-permute-done.11.rows_ref = f32[9,16,128]{2,1,0:T(8,128)S(1)} collective-permute-done((f32[9,16,128]{2,1,0:T(8,128)S(1)}, f32[9,16,128]{2,1,0:T(8,128)S(1)}, u32[]{:S(2)}, u32[]{:S(2)}) %collective-permute-start.11) | collective-permute-done | bytes 73760 | tf_op jit(solution)/shard_map/ppermute | solution.py:1041
  33.3 1.1 %shard_map.73 = f32[384,384]{1,0:T(8,128)} custom-call(s32[2]{0:T(128)S(4)} %get-tuple-element.20.west_ref, s32[2]{0:T(128)S(4)} %get-tuple-element.21.south_ref, f32[3,384,128]{2,1,0:T(8,128)S(1)} %shard_map.72.given_ref, f32[6,16,128]{2,1,0:T(8,128)S(1)} %get-tuple-element.30.speeds_ref, f32[9,16,128]{2,1,0:T(8,128)S(1)} %shard_map.71.blend_ref, ...), custom_call_target="tpu_custom_call" | custom-call | bytes 1376272 | tf_op jit(solution)/shard_map/pallas_call | solution.py:933
  (20 shorter events, 0.2 us)
Async XLA Ops:
  0.0 4.5 %copy-start = (f32[16,24,384]{2,1,0:T(8,128)S(1)}, f32[16,24,384]{2,1,0:T(8,128)}, u32[]{:S(2)}) copy-start(f32[16,24,384]{2,1,0:T(8,128)} %param.7) | copy-start | bytes 1769476
  0.0 4.5 %copy-start.1 = (f32[16,24,384]{2,1,0:T(8,128)S(1)}, f32[16,24,384]{2,1,0:T(8,128)}, u32[]{:S(2)}) copy-start(f32[16,24,384]{2,1,0:T(8,128)} %param.8) | copy-start | bytes 1769476
  1.5 6.1 %collective-permute-start = (f32[14,16,128]{2,1,0:T(8,128)S(1)}, f32[14,16,128]{2,1,0:T(8,128)S(1)}, u32[]{:S(2)}, u32[]{:S(2)}) collective-permute-start(f32[14,16,128]{2,1,0:T(8,128)S(1)} %get-tuple-element.22), channel_id=1, source_target_pairs={{0,2},{2,0},{1,3},{3,1},{4,6},{6,4},{5,7},{7,5},{8,10},{10,8},{9,1... | collective-permute-start | bytes 344072 | tf_op jit(solution)/shard_map/ppermute | solution.py:978
  4.5 7.8 %copy-start.2 = (f32[16,24,384]{2,1,0:T(8,128)S(1)}, f32[16,24,384]{2,1,0:T(8,128)}, u32[]{:S(2)}) copy-start(f32[16,24,384]{2,1,0:T(8,128)} %param.6) | copy-start | bytes 1769476
  7.7 4.6 %collective-permute-start.3 = (f32[11,16,128]{2,1,0:T(8,128)S(1)}, f32[11,16,128]{2,1,0:T(8,128)S(1)}, u32[]{:S(2)}, u32[]{:S(2)}) collective-permute-start(f32[11,16,128]{2,1,0:T(8,128)S(1)} %slice_add_fusion), channel_id=1, source_target_pairs={{0,4},{1,5},{2,6},{3,7},{4,0},{5,1},{6,2},{7,3},{8,12},{9,13},{10,... | collective-permute-start | bytes 270344 | tf_op jit(solution)/shard_map/ppermute | solution.py:988
  9.6 2.7 %collective-permute-start.1 = (f32[24,384]{1,0:T(8,128)S(1)}, f32[24,384]{1,0:T(8,128)S(1)}, u32[]{:S(2)}, u32[]{:S(2)}) collective-permute-start(f32[24,384]{1,0:T(8,128)S(1)} %get-tuple-element.24), channel_id=1, source_target_pairs={{0,1},{1,0},{2,3},{3,2},{4,5},{5,4},{6,7},{7,6},{8,9},{9,8},{10,11... | collective-permute-start | bytes 110600 | tf_op jit(solution)/shard_map/ppermute | solution.py:979
  9.6 5.6 %collective-permute-start.5 = (f32[11,16,128]{2,1,0:T(8,128)S(1)}, f32[11,16,128]{2,1,0:T(8,128)S(1)}, u32[]{:S(2)}, u32[]{:S(2)}) collective-permute-start(f32[11,16,128]{2,1,0:T(8,128)S(1)} %slice_add_fusion), channel_id=1, source_target_pairs={{0,1},{1,0},{2,3},{3,2},{4,12},{5,13},{6,14},{7,15},{8,9},{9,8},{1... | collective-permute-start | bytes 270344 | tf_op jit(solution)/shard_map/ppermute | solution.py:988
  10.1 8.2 %collective-permute-start.4 = (f32[11,16,128]{2,1,0:T(8,128)S(1)}, f32[11,16,128]{2,1,0:T(8,128)S(1)}, u32[]{:S(2)}, u32[]{:S(2)}) collective-permute-start(f32[11,16,128]{2,1,0:T(8,128)S(1)} %slice_add_fusion), channel_id=1, source_target_pairs={{0,12},{1,13},{2,14},{3,15},{4,5},{5,4},{6,7},{7,6},{8,9},{9,8},{1... | collective-permute-start | bytes 270344 | tf_op jit(solution)/shard_map/ppermute | solution.py:988
  12.1 1.3 %collective-permute-start.2 = (f32[16,128]{1,0:T(8,128)S(1)}, f32[16,128]{1,0:T(8,128)S(1)}, u32[]{:S(2)}, u32[]{:S(2)}) collective-permute-start(f32[16,128]{1,0:T(8,128)S(1)} %get-tuple-element.25), channel_id=1, source_target_pairs={{0,1},{1,0},{2,3},{3,2},{4,8},{5,9},{6,10},{7,11},{8,4},{9,5},{10,... | collective-permute-start | bytes 24584 | tf_op jit(solution)/shard_map/ppermute | solution.py:988
  13.4 6.3 %collective-permute-start.7 = (f32[11,16,128]{2,1,0:T(8,128)S(1)}, f32[11,16,128]{2,1,0:T(8,128)S(1)}, u32[]{:S(2)}, u32[]{:S(2)}) collective-permute-start(f32[11,16,128]{2,1,0:T(8,128)S(1)} %get-tuple-element.34), channel_id=1, source_target_pairs={{0,2},{2,0},{1,3},{3,1},{4,6},{6,4},{5,7},{7,5},{8,10},{10,8},{9,1... | collective-permute-start | bytes 270344 | tf_op jit(solution)/shard_map/ppermute | solution.py:1011
  18.5 1.3 %collective-permute-start.6 = (f32[24,384]{1,0:T(8,128)S(1)}, f32[24,384]{1,0:T(8,128)S(1)}, u32[]{:S(2)}, u32[]{:S(2)}) collective-permute-start(f32[24,384]{1,0:T(8,128)S(1)} %get-tuple-element.32), channel_id=1, source_target_pairs={{0,1},{1,0},{2,3},{3,2},{4,5},{5,4},{6,7},{7,6},{8,9},{9,8},{10,11... | collective-permute-start | bytes 110600 | tf_op jit(solution)/shard_map/ppermute | solution.py:1019
  19.8 8.6 %copy-start.3 = (f32[16]{0:T(128)S(1)}, f32[16]{0:T(128)}, u32[]{:S(2)}) copy-start(f32[16]{0:T(128)} %param.9) | copy-start | bytes 196
  19.8 6.7 %collective-permute-start.10 = (f32[11,16,128]{2,1,0:T(8,128)S(1)}, f32[11,16,128]{2,1,0:T(8,128)S(1)}, u32[]{:S(2)}, u32[]{:S(2)}) collective-permute-start(f32[11,16,128]{2,1,0:T(8,128)S(1)} %shard_map.70.window_ref), channel_id=1, source_target_pairs={{0,12},{1,13},{2,14},{3,15},{4,8},{5,9},{6,10},{7,11},{8,4},{9,5},... | collective-permute-start | bytes 270344 | tf_op jit(solution)/shard_map/ppermute | solution.py:988
  22.5 4.0 %collective-permute-start.9 = (f32[11,16,128]{2,1,0:T(8,128)S(1)}, f32[11,16,128]{2,1,0:T(8,128)S(1)}, u32[]{:S(2)}, u32[]{:S(2)}) collective-permute-start(f32[11,16,128]{2,1,0:T(8,128)S(1)} %shard_map.70.window_ref), channel_id=1, source_target_pairs={{0,1},{1,0},{2,3},{3,2},{4,12},{5,13},{6,14},{7,15},{8,9},{9,8},{1... | collective-permute-start | bytes 270344 | tf_op jit(solution)/shard_map/ppermute | solution.py:988
  22.7 5.7 %collective-permute-start.8 = (f32[11,16,128]{2,1,0:T(8,128)S(1)}, f32[11,16,128]{2,1,0:T(8,128)S(1)}, u32[]{:S(2)}, u32[]{:S(2)}) collective-permute-start(f32[11,16,128]{2,1,0:T(8,128)S(1)} %shard_map.70.window_ref), channel_id=1, source_target_pairs={{0,4},{1,5},{2,6},{3,7},{4,0},{5,1},{6,2},{7,3},{8,12},{9,13},{10,... | collective-permute-start | bytes 270344 | tf_op jit(solution)/shard_map/ppermute | solution.py:988
  28.8 4.4 %collective-permute-start.11 = (f32[9,16,128]{2,1,0:T(8,128)S(1)}, f32[9,16,128]{2,1,0:T(8,128)S(1)}, u32[]{:S(2)}, u32[]{:S(2)}) collective-permute-start(f32[9,16,128]{2,1,0:T(8,128)S(1)} %shard_map.71.blend_ref), channel_id=1, source_target_pairs={{0,2},{2,0},{1,3},{3,1},{4,6},{6,4},{5,7},{7,5},{8,10},{10,8},{9,1... | collective-permute-start | bytes 221192 | tf_op jit(solution)/shard_map/ppermute | solution.py:1041

commit v6 on v5

--- a/solution.py
+++ b/solution.py
@@ -713,7 +713,7 @@
     return table((offset >= 0) & (offset <= 2))
 
 
-def message_kernel(levels, level_ref, part_ref, own_ref, other_ref, message_ref):
+def message_kernel(levels, level_ref, part_ref, coef_ref, own_ref, other_ref, message_ref, side_ref):
     height, breadth = level_ref.shape
     third_y = height // 3
     tile, row, lev = place()
@@ -734,18 +734,21 @@
         for i in range(third_y, message_ref.shape[0]):
             message_ref[i] = part_ref[i]
 
+    side_ref[pl.ds(0, message_ref.shape[0])] = message_ref[...]
+    side_ref[pl.ds(message_ref.shape[0], WEIGHTS)] = coef_ref[pl.ds(0, WEIGHTS)]
+
 
 def blend_kernel(
     levels,
+    western,
     weight_ref,
     field_ref,
     window_ref,
-    one_ref,
-    two_ref,
-    three_ref,
-    coef_three_ref,
-    coef_two_ref,
-    coef_one_ref,
+    beside_ref,
+    middle_ref,
+    other_ref,
+    coef_middle_ref,
+    coef_near_ref,
     rows_ref,
 ):
     pieces, size, _ = field_ref.shape
@@ -764,22 +767,17 @@
 
     @pl.when(jnp.logical_not(nest))
     def _():
-        def of_nest(refs, i):
-            one, two, three = refs
-            return jnp.where(tile == 0, three[i], jnp.where(tile == 1, two[i], one[i]))
+        paired = (tile == 1) | (tile == (0 if western else 2))
 
         def mine(i):
-            return of_nest((one_ref, two_ref, three_ref), i)
+            return jnp.where(tile == 1, middle_ref[i], other_ref[i])
 
         def coefficient(i):
-            return of_nest((coef_one_ref, coef_two_ref, coef_three_ref), i)
+            other = beside_ref[slots + 1 + i] if western else coef_near_ref[i]
+            return jnp.where(tile == 1, coef_middle_ref[i], other)
 
         def whole(i):
-            odd = tile % 2 == 1
-            west = jnp.where(odd, one_ref[i], three_ref[i])
-            east = jnp.where(odd, three_ref[i], one_ref[i])
-            part = jnp.where(tile == 0, window_ref[i], window_ref[i] + west)
-            return jnp.where(tile == tile_count - 2, part, part + east)
+            return jnp.where(paired, window_ref[i] + beside_ref[i], window_ref[i])
 
         weight = weight_ref[:, 0:1]
         extra = whole(slots)
@@ -830,9 +828,8 @@
     east_ref,
     north_ref,
     level_ref,
-    one_ref,
-    two_ref,
-    three_ref,
+    middle_ref,
+    other_ref,
     parent_ref,
     blend_ref,
     out_ref,
@@ -849,7 +846,7 @@
 
     @pl.when(nest)
     def _():
-        slabs = [one_ref[s] + two_ref[s] + three_ref[s] for s in range(slots + 1)]
+        slabs = [middle_ref[s] + other_ref[s] for s in range(slots + 1)]
         cells, ring = refine(slabs[:slots], slabs[slots], height, breadth, row)
         fine_ref[...] = cells[:, :breadth]
         side_ref[...] = cells[:, breadth:]
@@ -987,9 +984,16 @@
             pairs.append((at[t, r, l], at[(t, r, 1 - l) if idle else (t ^ step, r, l)]))
         return lax.ppermute(message, ("tiles", "rows", "lev"), pairs)
 
+    halo = over_tiles(edges, 3, 0)
+    eastern = nest_west[1] > breadth
+    rows, halo, eastern, weight = lax.optimization_barrier((rows, halo, eastern, weight))
     window = own + rows[: slots + 1]
-    starting = [over_tiles(window, 1), over_tiles(window, 2, 0), over_tiles(window, 3, 1)]
-    halo = over_tiles(edges, 3, 0)
+    around = [(t, (t - 1) % tile_count) for t in range(tile_count)]
+    starting = [
+        over_tiles(window, 1),
+        over_tiles(window, 2, 0),
+        lax.ppermute(window, "tiles", around),
+    ]
     sides = [(size, LANES), (levels, breadth), (levels, breadth)]
     early, other = call(
         kernel(early_kernel),
@@ -1025,35 +1029,51 @@
         [flat, (height, breadth)],
         flops=30 * size * breadth,
     )
-    (message,) = call(
+    message, side_message = call(
         kernel(message_kernel),
-        [slabs(slots + 1)],
-        [level, part, own, other],
-        "vvvv",
-    )
-    received = [over_tiles(message, 1), over_tiles(message, 2, 0), over_tiles(message, 3)]
-    (blend,) = call(
-        kernel(blend_kernel),
-        [slabs(third_y + 1)],
-        [weight, first, message, *received, *starting[::-1]],
-        "v" * 9,
-    )
-    rows = lax.ppermute(blend, "rows", swap)
-    (later,) = call(
-        kernel(later_kernel),
-        [chunked],
-        [west, south, first, east, north, level, *received, early, blend],
-        "ss" + "v" * 9,
-        [flat, *sides],
-        flops=30 * size * breadth,
-    )
-    (out,) = call(
-        kernel(last_kernel),
-        [flat],
-        [west, south, later, speeds, blend, rows],
-        "ssvvvv",
-        [chunked, pltpu.SemaphoreType.DMA((pieces,))],
-        out_place="h",
+        [slabs(slots + 1), slabs(slots + 1 + WEIGHTS)],
+        [level, part, starting[1], own, other],
+        "vvvvv",
+    )
+    def finish(western, arrays):
+        west, south, weight, first, east, north, level, message, side_message, early, speeds, coefs = arrays
+        if western:
+            other, beside = over_tiles(message, 3, 1), over_tiles(side_message, 1, 3)
+        else:
+            other, beside = over_tiles(message, 1, 0), over_tiles(side_message, 3, 0)
+        middle = over_tiles(message, 2, 0)
+        (blend,) = call(
+            functools.partial(blend_kernel, levels, western),
+            [slabs(third_y + 1)],
+            [weight, first, message, beside, middle, other, *coefs],
+            "v" * 8,
+        )
+        rows = lax.ppermute(blend, "rows", swap)
+        (later,) = call(
+            kernel(later_kernel),
+            [chunked],
+            [west, south, first, east, north, level, middle, other, early, blend],
+            "ss" + "v" * 8,
+            [flat, *sides],
+            flops=30 * size * breadth,
+        )
+        (out,) = call(
+            kernel(last_kernel),
+            [flat],
+            [west, south, later, speeds, blend, rows],
+            "ssvvvv",
+            [chunked, pltpu.SemaphoreType.DMA((pieces,))],
+            out_place="h",
+        )
+        return out
+
+    arrays = (west, south, weight, first, east, north, level, message, side_message, early, speeds)
+    arrays += ((starting[1], starting[0]),)
+    out = lax.cond(
+        eastern,
+        functools.partial(finish, False),
+        functools.partial(finish, True),
+        arrays,
     )
     return out.reshape(air_state.shape)
 

time: 34.5 us -> 32.5 us (0.942)
  the two profiles are of different devices: /device:TPU:0 before, /device:TPU:12 now
where the time goes in v6:
time: 32.5 us; the launch traced here: 32.3 us
  waiting for transfers between devices  13.4 us (41%)
  starting transfers between devices  12.7 us (39%)
  Pallas kernels  4.78 us (15%)
  between operations  0.76 us (2%)
  local copies, waits for them, and re-layouts  0.67 us (2%)
    ppermute x6, starting transfers between devices, over_tiles(): return lax.ppermute(message, ('tiles', 'rows', 'lev'), pairs)  9.11 us
    ppermute x6, waiting for transfers between devices, over_tiles(): return lax.ppermute(message, ('tiles', 'rows', 'lev'), pairs)  8.45 us
    pallas_call x10, Pallas kernels, call(): pl.pallas_call(kernel, out_shape=outs, in_specs=[pl.BlockSpec(memory_spac...  4.78 us
    ppermute x1, waiting for transfers between devices, finish(): rows = lax.ppermute(blend, 'rows', swap)  3.24 us
    ppermute x1, starting transfers between devices, per_device_paired(): rows = lax.ppermute(rows, 'rows', swap)  1.56 us
    ppermute x1, waiting for transfers between devices, per_device_paired(): level = lax.ppermute(edge, 'lev', swap)  1.18 us
    ppermute x1, starting transfers between devices, finish(): rows = lax.ppermute(blend, 'rows', swap)  0.96 us
    ppermute x1, starting transfers between devices, per_device_paired(): other = lax.ppermute(other, 'rows', swap)  0.91 us
  transfers between devices with their start and end apart: 12, of which 7 were waited for; matrix products, arithmetic and copies ran while one was open for 2% of the time, Pallas kernels for 6%

profile of v6, /device:TPU:12, one launch (start us, length us, event | category | flops | bytes accessed | tf_op | source)
XLA Modules:
  0.0 32.3 jit_solution(11504560889363644917)
XLA Ops:
  0.0 1.5 %shard_map.66 = (f32[14,16,128]{2,1,0:T(8,128)S(1)}, f32[3,384,128]{2,1,0:T(8,128)S(1)}, s32[2]{0:T(128)S(4)}, s32[2]{0:T(128)S(4)}) custom-call(s32[2]{0:T(128)} %west_hbm.1, s32[2]{0:T(128)} %south_hbm.1, f32[384,384]{1,0:T(8,128)} %bitcast.6, f32[384,384]{1,0:T(8,128)} %bitcast.16), custom_call_target="tpu_custom_call" | custom-call | bytes 1884192 | tf_op jit(solution)/shard_map/pallas_call | solution.py:930
  1.5 1.6 %collective-permute-start.8 = (f32[14,16,128]{2,1,0:T(8,128)S(1)}, f32[14,16,128]{2,1,0:T(8,128)S(1)}, u32[]{:S(2)}, u32[]{:S(2)}) collective-permute-start(f32[14,16,128]{2,1,0:T(8,128)S(1)} %get-tuple-element.108), channel_id=1, source_target_pairs={{0,2},{2,0},{1,3},{3,1},{4,6},{6,4},{5,7},{7,5},{8,10},{10,8},{9,1... | collective-permute-start | bytes 344072 | tf_op jit(solution)/shard_map/ppermute | solution.py:975
  3.1 0.3 shard_map.67
  3.4 1.6 %collective-permute-start.9 = (f32[16,128]{1,0:T(8,128)S(1)}, f32[16,128]{1,0:T(8,128)S(1)}, u32[]{:S(2)}, u32[]{:S(2)}) collective-permute-start(f32[16,128]{1,0:T(8,128)S(1)} %get-tuple-element.112), channel_id=1, source_target_pairs={{0,1},{1,0},{2,3},{3,2},{4,8},{5,9},{6,10},{7,11},{8,4},{9,5},{10,... | collective-permute-start | bytes 24584 | tf_op jit(solution)/shard_map/ppermute | solution.py:985
  5.0 0.6 %slice.6 = s32[1]{0:T(128)} slice(s32[2]{0:T(128)S(1)} %copy-done.3), slice={[1:2]} | slice | bytes 8 | tf_op jit(solution)/shard_map/slice | solution.py:988
  6.3 0.8 %collective-permute-done.9.three_ref = f32[16,128]{1,0:T(8,128)S(1)} collective-permute-done((f32[16,128]{1,0:T(8,128)S(1)}, f32[16,128]{1,0:T(8,128)S(1)}, u32[]{:S(2)}, u32[]{:S(2)}) %collective-permute-start.9) | collective-permute-done | bytes 8224 | tf_op jit(solution)/shard_map/ppermute | solution.py:985
  7.4 2.9 %collective-permute-start.13 = (f32[11,16,128]{2,1,0:T(8,128)S(1)}, f32[11,16,128]{2,1,0:T(8,128)S(1)}, u32[]{:S(2)}, u32[]{:S(2)}) collective-permute-start(f32[11,16,128]{2,1,0:T(8,128)S(1)} %slice_add_fusion), channel_id=1, source_target_pairs={{0,1},{1,0},{2,3},{3,2},{4,12},{5,13},{6,14},{7,15},{8,9},{9,8},{1... | collective-permute-start | bytes 270344 | tf_op jit(solution)/shard_map/ppermute | solution.py:985
  10.3 1.5 %collective-permute-done.11.one_ref = f32[11,16,128]{2,1,0:T(8,128)S(1)} collective-permute-done((f32[11,16,128]{2,1,0:T(8,128)S(1)}, f32[11,16,128]{2,1,0:T(8,128)S(1)}, u32[]{:S(2)}, u32[]{:S(2)}) %collective-permute-start.11) | collective-permute-done | bytes 90144 | tf_op jit(solution)/shard_map/ppermute | solution.py:985
  11.8 1.1 %shard_map.69 = (f32[3,384,128]{2,1,0:T(8,128)S(1)}, f32[11,16,128]{2,1,0:T(8,128)S(1)}) custom-call(s32[2]{0:T(128)S(4)} %get-tuple-element.109.west_ref, s32[2]{0:T(128)S(4)} %get-tuple-element.110.south_ref, f32[384,384]{1,0:T(8,128)S(1)} %bitcast.8, f32[384,384]{1,0:T(8,128)S(1)} %bitcast.11, ...), custom_call_target="tpu_custom_call", output_to_operand_aliasing={{0}: (9, {}), {1}: (10, {})} | custom-call | flops 4423680 | bytes 3379216 | tf_op jit(solution)/shard_map/pallas_call | solution.py:930
  12.9 0.9 %collective-permute-start.15 = (f32[11,16,128]{2,1,0:T(8,128)S(1)}, f32[11,16,128]{2,1,0:T(8,128)S(1)}, u32[]{:S(2)}, u32[]{:S(2)}) collective-permute-start(f32[11,16,128]{2,1,0:T(8,128)S(1)} %get-tuple-element.125), channel_id=1, source_target_pairs={{0,2},{2,0},{1,3},{3,1},{4,6},{6,4},{5,7},{7,5},{8,10},{10,8},{9,1... | collective-permute-start | bytes 270344 | tf_op jit(solution)/shard_map/ppermute | solution.py:1015
  13.8 1.8 %collective-permute-done.13.two_ref.coef_ref = f32[11,16,128]{2,1,0:T(8,128)S(1)} collective-permute-done((f32[11,16,128]{2,1,0:T(8,128)S(1)}, f32[11,16,128]{2,1,0:T(8,128)S(1)}, u32[]{:S(2)}, u32[]{:S(2)}) %collective-permute-start.13) | collective-permute-done | bytes 90144 | tf_op jit(solution)/shard_map/ppermute | solution.py:985
  15.6 0.5 %collective-permute-done.12.three_ref = f32[11,16,128]{2,1,0:T(8,128)S(1)} collective-permute-done((f32[11,16,128]{2,1,0:T(8,128)S(1)}, f32[11,16,128]{2,1,0:T(8,128)S(1)}, u32[]{:S(2)}, u32[]{:S(2)}) %collective-permute-start.12) | collective-permute-done | bytes 90144 | tf_op jit(solution)/shard_map/ppermute | solution.py:995
  16.2 0.2 shard_map.70
  16.5 1.2 %collective-permute-done.14.level_ref = f32[24,384]{1,0:T(8,128)S(1)} collective-permute-done((f32[24,384]{1,0:T(8,128)S(1)}, f32[24,384]{1,0:T(8,128)S(1)}, u32[]{:S(2)}, u32[]{:S(2)}) %collective-permute-start.14) | collective-permute-done | bytes 36896 | tf_op jit(solution)/shard_map/ppermute | solution.py:1023
  17.7 14.7 %conditional.1 = (f32[16,24,384]{2,1,0:T(8,128)}) conditional(s32[]{:T(128)} %convert_element_type.3, (f32[11,16,128]{2,1,0:T(8,128)S(1)}, f32[15,16,128]{2,1,0:T(8,128)S(1)}, f32[16,128]{1,0:T(8,128)S(1)}, f32[3,384,128]{2,1,0:T(8,128)S(1)}, f32[11,16,128]{2,1,0:T(8,128)S(1)}, /*index=5*/f32[11,16,128]{2,1,0:T(8,128)S(1)}, s32[2]{0:T(128)S(4)}, ...), branch_computations={%region_0.0_spmd, %region_1.0_spmd} | conditional | flops 4423680 | bytes 7368904 | solution.py:1072
  17.7 0.2 collective-permute-start.2
  17.9 0.1 collective-permute-start.1
  18.0 4.1 %collective-permute-start = (f32[11,16,128]{2,1,0:T(8,128)S(1)}, f32[11,16,128]{2,1,0:T(8,128)S(1)}, u32[]{:S(2)}, u32[]{:S(2)}) collective-permute-start(f32[11,16,128]{2,1,0:T(8,128)S(1)} %get-tuple-element.67.window_ref), channel_id=1, source_target_pairs={{0,1},{1,0},{2,3},{3,2},{4,12},{5,13},{6,14},{7,15},{8,9},{9,8},{1... | collective-permute-start | bytes 270344 | tf_op jit(solution)/shard_map/cond/branch_0_fun/ppermute | solution.py:985
  22.1 4.3 %collective-permute-done.middle_ref = f32[11,16,128]{2,1,0:T(8,128)S(1)} collective-permute-done((f32[11,16,128]{2,1,0:T(8,128)S(1)}, f32[11,16,128]{2,1,0:T(8,128)S(1)}, u32[]{:S(2)}, u32[]{:S(2)}) %collective-permute-start) | collective-permute-done | bytes 90144 | tf_op jit(solution)/shard_map/cond/branch_0_fun/ppermute | solution.py:985
  26.4 0.4 %branch_0_fun.3.blend_ref = f32[9,16,128]{2,1,0:T(8,128)S(1)} custom-call(f32[16,128]{1,0:T(8,128)S(1)} %get-tuple-element.69.weight_ref, f32[3,384,128]{2,1,0:T(8,128)S(1)} %get-tuple-element.63.field_ref, f32[11,16,128]{2,1,0:T(8,128)S(1)} %get-tuple-element.67.window_ref, f32[15,16,128]{2,1,0:T(8,128)S(1)} %collective-permute-done.2.beside_ref, ...), custom_call_target="tpu_custom_call" | custom-call | bytes 1245184 | tf_op jit(solution)/shard_map/cond/branch_0_fun/pallas_call | solution.py:930
  26.8 1.0 %collective-permute-start.3 = (f32[9,16,128]{2,1,0:T(8,128)S(1)}, f32[9,16,128]{2,1,0:T(8,128)S(1)}, u32[]{:S(2)}, u32[]{:S(2)}) collective-permute-start(f32[9,16,128]{2,1,0:T(8,128)S(1)} %branch_0_fun.3.blend_ref), channel_id=1, source_target_pairs={{0,2},{2,0},{1,3},{3,1},{4,6},{6,4},{5,7},{7,5},{8,10},{10,8},{9,1... | collective-permute-start | bytes 221192 | tf_op jit(solution)/shard_map/cond/branch_0_fun/ppermute | solution.py:1051
  27.8 0.2 branch_0_fun.4.given_ref
  28.0 3.2 %collective-permute-done.3.rows_ref = f32[9,16,128]{2,1,0:T(8,128)S(1)} collective-permute-done((f32[9,16,128]{2,1,0:T(8,128)S(1)}, f32[9,16,128]{2,1,0:T(8,128)S(1)}, u32[]{:S(2)}, u32[]{:S(2)}) %collective-permute-start.3) | collective-permute-done | bytes 73760 | tf_op jit(solution)/shard_map/cond/branch_0_fun/ppermute | solution.py:1051
  31.2 1.1 %branch_0_fun.5 = f32[384,384]{1,0:T(8,128)} custom-call(s32[2]{0:T(128)S(4)} %get-tuple-element.61.west_ref, s32[2]{0:T(128)S(4)} %get-tuple-element.62.south_ref, f32[3,384,128]{2,1,0:T(8,128)S(1)} %branch_0_fun.4.given_ref, f32[6,16,128]{2,1,0:T(8,128)S(1)} %get-tuple-element.73.speeds_ref, f32[9,16,128]{2,1,0:T(8,128)S(1)} %branch_0_fun.3.blend_ref, ...), custom_call_target="tpu_custom_call" | custom-call | bytes 1376272 | tf_op jit(solution)/shard_map/cond/branch_0_fun/pallas_call | solution.py:930
  (24 shorter events, 0.4 us)
Async XLA Ops:
  0.0 3.1 %copy-start.1 = (f32[16,24,384]{2,1,0:T(8,128)S(1)}, f32[16,24,384]{2,1,0:T(8,128)}, u32[]{:S(2)}) copy-start(f32[16,24,384]{2,1,0:T(8,128)} %param.9) | copy-start | bytes 1769476
  0.0 3.1 %copy-start.2 = (f32[16,24,384]{2,1,0:T(8,128)S(1)}, f32[16,24,384]{2,1,0:T(8,128)}, u32[]{:S(2)}) copy-start(f32[16,24,384]{2,1,0:T(8,128)} %param.10) | copy-start | bytes 1769476
  1.5 5.6 %collective-permute-start.8 = (f32[14,16,128]{2,1,0:T(8,128)S(1)}, f32[14,16,128]{2,1,0:T(8,128)S(1)}, u32[]{:S(2)}, u32[]{:S(2)}) collective-permute-start(f32[14,16,128]{2,1,0:T(8,128)S(1)} %get-tuple-element.108), channel_id=1, source_target_pairs={{0,2},{2,0},{1,3},{3,1},{4,6},{6,4},{5,7},{7,5},{8,10},{10,8},{9,1... | collective-permute-start | bytes 344072 | tf_op jit(solution)/shard_map/ppermute | solution.py:975
  3.1 8.7 %copy-start = (f32[16,24,384]{2,1,0:T(8,128)S(1)}, f32[16,24,384]{2,1,0:T(8,128)}, u32[]{:S(2)}) copy-start(f32[16,24,384]{2,1,0:T(8,128)} %param.8) | copy-start | bytes 1769476
  3.4 1.7 %copy-start.3 = (s32[2]{0:T(128)S(1)}, s32[2]{0:T(128)}, u32[]{:S(2)}) copy-start(s32[2]{0:T(128)} %west_hbm.1) | copy-start | bytes 28
  3.4 3.7 %collective-permute-start.9 = (f32[16,128]{1,0:T(8,128)S(1)}, f32[16,128]{1,0:T(8,128)S(1)}, u32[]{:S(2)}, u32[]{:S(2)}) collective-permute-start(f32[16,128]{1,0:T(8,128)S(1)} %get-tuple-element.112), channel_id=1, source_target_pairs={{0,1},{1,0},{2,3},{3,2},{4,8},{5,9},{6,10},{7,11},{8,4},{9,5},{10,... | collective-permute-start | bytes 24584 | tf_op jit(solution)/shard_map/ppermute | solution.py:985
  6.3 0.8 %copy-start.4 = (f32[16]{0:T(128)S(1)}, f32[16]{0:T(128)}, u32[]{:S(2)}) copy-start(f32[16]{0:T(128)} %param.11) | copy-start | bytes 196
  7.2 4.6 %collective-permute-start.11 = (f32[11,16,128]{2,1,0:T(8,128)S(1)}, f32[11,16,128]{2,1,0:T(8,128)S(1)}, u32[]{:S(2)}, u32[]{:S(2)}) collective-permute-start(f32[11,16,128]{2,1,0:T(8,128)S(1)} %slice_add_fusion), channel_id=1, source_target_pairs={{0,4},{1,5},{2,6},{3,7},{4,0},{5,1},{6,2},{7,3},{8,12},{9,13},{10,... | collective-permute-start | bytes 270344 | tf_op jit(solution)/shard_map/ppermute | solution.py:985
  7.3 3.0 %collective-permute-start.10 = (f32[24,384]{1,0:T(8,128)S(1)}, f32[24,384]{1,0:T(8,128)S(1)}, u32[]{:S(2)}, u32[]{:S(2)}) collective-permute-start(f32[24,384]{1,0:T(8,128)S(1)} %get-tuple-element.115), channel_id=1, source_target_pairs={{0,1},{1,0},{2,3},{3,2},{4,5},{5,4},{6,7},{7,6},{8,9},{9,8},{10,11... | collective-permute-start | bytes 110600 | tf_op jit(solution)/shard_map/ppermute | solution.py:976
  7.4 8.3 %collective-permute-start.13 = (f32[11,16,128]{2,1,0:T(8,128)S(1)}, f32[11,16,128]{2,1,0:T(8,128)S(1)}, u32[]{:S(2)}, u32[]{:S(2)}) collective-permute-start(f32[11,16,128]{2,1,0:T(8,128)S(1)} %slice_add_fusion), channel_id=1, source_target_pairs={{0,1},{1,0},{2,3},{3,2},{4,12},{5,13},{6,14},{7,15},{8,9},{9,8},{1... | collective-permute-start | bytes 270344 | tf_op jit(solution)/shard_map/ppermute | solution.py:985
  10.3 5.9 %collective-permute-start.12 = (f32[11,16,128]{2,1,0:T(8,128)S(1)}, f32[11,16,128]{2,1,0:T(8,128)S(1)}, u32[]{:S(2)}, u32[]{:S(2)}) collective-permute-start(f32[11,16,128]{2,1,0:T(8,128)S(1)} %slice_add_fusion), channel_id=1, source_target_pairs={{0,12},{4,0},{8,4},{12,8},{1,13},{5,1},{9,5},{13,9},{2,14},{6,2},{... | collective-permute-start | bytes 270344 | tf_op jit(solution)/shard_map/ppermute | solution.py:995
  12.9 4.7 %collective-permute-start.15 = (f32[11,16,128]{2,1,0:T(8,128)S(1)}, f32[11,16,128]{2,1,0:T(8,128)S(1)}, u32[]{:S(2)}, u32[]{:S(2)}) collective-permute-start(f32[11,16,128]{2,1,0:T(8,128)S(1)} %get-tuple-element.125), channel_id=1, source_target_pairs={{0,2},{2,0},{1,3},{3,1},{4,6},{6,4},{5,7},{7,5},{8,10},{10,8},{9,1... | collective-permute-start | bytes 270344 | tf_op jit(solution)/shard_map/ppermute | solution.py:1015
  16.4 1.3 %collective-permute-start.14 = (f32[24,384]{1,0:T(8,128)S(1)}, f32[24,384]{1,0:T(8,128)S(1)}, u32[]{:S(2)}, u32[]{:S(2)}) collective-permute-start(f32[24,384]{1,0:T(8,128)S(1)} %get-tuple-element.122), channel_id=1, source_target_pairs={{0,1},{1,0},{2,3},{3,2},{4,5},{5,4},{6,7},{7,6},{8,9},{9,8},{10,11... | collective-permute-start | bytes 110600 | tf_op jit(solution)/shard_map/ppermute | solution.py:1023
  17.7 8.8 %collective-permute-start.2 = (f32[15,16,128]{2,1,0:T(8,128)S(1)}, f32[15,16,128]{2,1,0:T(8,128)S(1)}, u32[]{:S(2)}, u32[]{:S(2)}) collective-permute-start(f32[15,16,128]{2,1,0:T(8,128)S(1)} %get-tuple-element.70), channel_id=1, source_target_pairs={{0,4},{1,5},{2,6},{3,7},{4,0},{5,1},{6,2},{7,3},{8,9},{9,8},{10,11... | collective-permute-start | bytes 368648 | tf_op jit(solution)/shard_map/cond/branch_0_fun/ppermute | solution.py:985
  17.9 4.3 %collective-permute-start.1 = (f32[11,16,128]{2,1,0:T(8,128)S(1)}, f32[11,16,128]{2,1,0:T(8,128)S(1)}, u32[]{:S(2)}, u32[]{:S(2)}) collective-permute-start(f32[11,16,128]{2,1,0:T(8,128)S(1)} %get-tuple-element.67.window_ref), channel_id=1, source_target_pairs={{0,12},{1,13},{2,14},{3,15},{4,5},{5,4},{6,7},{7,6},{8,9},{9,8},{1... | collective-permute-start | bytes 270344 | tf_op jit(solution)/shard_map/cond/branch_0_fun/ppermute | solution.py:985
  18.0 8.5 %collective-permute-start = (f32[11,16,128]{2,1,0:T(8,128)S(1)}, f32[11,16,128]{2,1,0:T(8,128)S(1)}, u32[]{:S(2)}, u32[]{:S(2)}) collective-permute-start(f32[11,16,128]{2,1,0:T(8,128)S(1)} %get-tuple-element.67.window_ref), channel_id=1, source_target_pairs={{0,1},{1,0},{2,3},{3,2},{4,12},{5,13},{6,14},{7,15},{8,9},{9,8},{1... | collective-permute-start | bytes 270344 | tf_op jit(solution)/shard_map/cond/branch_0_fun/ppermute | solution.py:985
  26.8 4.4 %collective-permute-start.3 = (f32[9,16,128]{2,1,0:T(8,128)S(1)}, f32[9,16,128]{2,1,0:T(8,128)S(1)}, u32[]{:S(2)}, u32[]{:S(2)}) collective-permute-start(f32[9,16,128]{2,1,0:T(8,128)S(1)} %branch_0_fun.3.blend_ref), channel_id=1, source_target_pairs={{0,2},{2,0},{1,3},{3,1},{4,6},{6,4},{5,7},{7,5},{8,10},{10,8},{9,1... | collective-permute-start | bytes 221192 | tf_op jit(solution)/shard_map/cond/branch_0_fun/ppermute | solution.py:1051
